TPU v7x, 32 devices: a whole 2x2x4 slice. The times are simulated.
32 devices in a mesh: dp: 8 (over y, x, core), tensor: 4 (over z).
Axes of the slice: x: 2, y: 2, z: 4, core: 2. Of those that a mesh axis runs over, the one named last changes fastest.
Arguments:
- tokens: bfloat16 [8192, 2048], P('dp', 'tensor'), may hold values from -36 to 36
- norm_one_gain: bfloat16 [2048], P('tensor'), may hold values from 0.25 to 1.75
- norm_one_shift: bfloat16 [2048], P('tensor'), may hold values from -4 to 4
- project_weight: bfloat16 [2048, 3, 2048], P(None, None, 'tensor'), may hold values from -0.125 to 0.125
- project_bias: bfloat16 [3, 2048], P(None, 'tensor'), may hold values from -6 to 6
- output_weight: bfloat16 [2048, 2048], P('tensor'), may hold values from -0.5 to 0.5
- norm_two_gain: bfloat16 [2048], P('tensor'), may hold values from 0.25 to 1.75
- norm_two_shift: bfloat16 [2048], P('tensor'), may hold values from -4 to 4
- gate_up_weight: bfloat16 [2048, 2, 5632], P(None, None, 'tensor'), may hold values from -0.125 to 0.125
- down_weight: bfloat16 [5632, 2048], P('tensor'), may hold values from -0.078125 to 0.078125
- cotangent: bfloat16 [8192, 2048], P('dp', 'tensor'), may hold values from -6 to 6
Outputs:
- result: bfloat16 [8192, 2048], P('dp', 'tensor')
- tokens_grad: float32 [8192, 2048], P('dp', 'tensor')
- norm_one_gain_grad: float32 [2048], P('tensor')
- norm_one_shift_grad: float32 [2048], P('tensor')
- project_weight_grad: float32 [2048, 3, 2048], P(None, None, 'tensor')
- project_bias_grad: float32 [3, 2048], P(None, 'tensor')
- output_weight_grad: float32 [2048, 2048], P('tensor')
- norm_two_gain_grad: float32 [2048], P('tensor')
- norm_two_shift_grad: float32 [2048], P('tensor')
- gate_up_weight_grad: float32 [2048, 2, 5632], P(None, None, 'tensor')
- down_weight_grad: float32 [5632, 2048], P('tensor')
All inputs are finite; a program needn't handle non-finite values.
Results may differ from a plain program's by a relative error of at most 0.013.
Values may be sent and summed in bfloat16 or wider, within the bound.
No kernel may reach another device: no remote copies, remote signals or barrier semaphores. Data moves between devices by JAX's collectives and lax.ppermute only.
A program may use at most 320 MiB of HBM per device.

v0:
```python
import jax
import jax.numpy as jnp
from jax import lax
from jax.sharding import PartitionSpec as P

D = 2048
HEAD_DIM = 64
ROT = 16
SEQ = 1024


EPSILON = 1e-05
ROPE_BASE = 10000.0


def norm_forward(values, gain_full, shift_full):
    row_mean = jnp.mean(values, axis=-1, keepdims=True)
    centered = values - row_mean
    inverse = lax.rsqrt(jnp.mean(centered * centered, axis=-1, keepdims=True) + EPSILON)
    unit_rows = centered * inverse
    return (unit_rows * gain_full + shift_full, unit_rows, inverse)


def norm_back_terms(delta_normed, unit_rows, gain_share):
    scaled = delta_normed * gain_share
    stat_terms = (jnp.sum(scaled, axis=-1), jnp.sum(scaled * unit_rows, axis=-1))
    return (
        scaled,
        stat_terms,
        jnp.sum(delta_normed * unit_rows, axis=0),
        jnp.sum(delta_normed, axis=0),
    )


def norm_back_finish(scaled, unit_rows, inverse, stat_totals):
    first_mean = stat_totals[0][:, None] / D
    second_mean = stat_totals[1][:, None] / D
    return inverse * (scaled - first_mean - unit_rows * second_mean)


def rotary_tables(length):
    half_rot = ROT // 2
    positions = jnp.arange(length, dtype=jnp.float32)[:, None]
    exponent = jnp.arange(half_rot, dtype=jnp.float32)[None, :] * (2.0 / ROT)
    angles = positions * ROPE_BASE ** (-exponent)
    return (jnp.cos(angles)[:, None, :], jnp.sin(angles)[:, None, :])


def rotate(heads_in, cosine_table, sine_table):
    half_rot = ROT // 2
    first_half = heads_in[..., :half_rot]
    second = heads_in[..., half_rot:ROT]
    return jnp.concatenate(
        [
            first_half * cosine_table - second * sine_table,
            second * cosine_table + first_half * sine_table,
            heads_in[..., ROT:],
        ],
        axis=-1,
    )


def rotate_back(gradient, cosine_table, sine_table):
    half_rot = ROT // 2
    first_half = gradient[..., :half_rot]
    second = gradient[..., half_rot:ROT]
    return jnp.concatenate(
        [
            first_half * cosine_table + second * sine_table,
            second * cosine_table - first_half * sine_table,
            gradient[..., ROT:],
        ],
        axis=-1,
    )


def block_scores(query_heads, key_heads, number, block_rows):
    key_stop = (number + 1) * block_rows
    query_block = query_heads[:, number * block_rows : key_stop]
    scores = jnp.einsum(
        "sqhc,skhc->shqk", query_block, key_heads[:, :key_stop], preferred_element_type=jnp.float32
    ) * HEAD_DIM ** (-0.5)
    row_index = number * block_rows + jnp.arange(block_rows, dtype=jnp.int32)[:, None]
    column_index = jnp.arange(key_stop, dtype=jnp.int32)[None, :]
    return (jnp.where(column_index <= row_index, scores, -1000000000.0), query_block, key_stop)


def attend(query_heads, key_heads, value_heads, block_rows):
    contexts = []
    log_sums = []
    for number in range(query_heads.shape[1] // block_rows):
        scores, query_block, key_stop = block_scores(query_heads, key_heads, number, block_rows)
        maximum = jnp.max(scores, axis=-1, keepdims=True)
        raised = jnp.exp(scores - maximum)
        row_total = jnp.sum(raised, axis=-1, keepdims=True)
        probabilities = (raised / row_total).astype(jnp.bfloat16)
        contexts.append(
            jnp.einsum(
                "shqk,skhc->sqhc",
                probabilities,
                value_heads[:, :key_stop],
                preferred_element_type=jnp.float32,
            )
        )
        log_sums.append(maximum + jnp.log(row_total))
    return (jnp.concatenate(contexts, axis=1), log_sums)


def attend_back(query_heads, key_heads, value_heads, delta_context, log_sums, block_rows):
    score_scale = HEAD_DIM ** (-0.5)
    query_parts = []
    delta_keys = jnp.zeros(key_heads.shape, jnp.float32)
    delta_values = jnp.zeros(value_heads.shape, jnp.float32)
    for number in range(query_heads.shape[1] // block_rows):
        scores, query_block, key_stop = block_scores(query_heads, key_heads, number, block_rows)
        probabilities = jnp.exp(scores - log_sums[number])
        context_block = delta_context[:, number * block_rows : key_stop]
        delta_probs = jnp.einsum(
            "sqhc,skhc->shqk",
            context_block,
            value_heads[:, :key_stop],
            preferred_element_type=jnp.float32,
        )
        row_dot = jnp.sum(probabilities * delta_probs, axis=-1, keepdims=True)
        delta_scores = (probabilities * (delta_probs - row_dot)).astype(jnp.bfloat16)
        query_parts.append(
            jnp.einsum(
                "shqk,skhc->sqhc",
                delta_scores,
                key_heads[:, :key_stop],
                preferred_element_type=jnp.float32,
            )
            * score_scale
        )
        delta_keys = delta_keys.at[:, :key_stop].add(
            jnp.einsum(
                "shqk,sqhc->skhc", delta_scores, query_block, preferred_element_type=jnp.float32
            )
            * score_scale
        )
        delta_values = delta_values.at[:, :key_stop].add(
            jnp.einsum(
                "shqk,sqhc->skhc",
                probabilities.astype(jnp.bfloat16),
                context_block,
                preferred_element_type=jnp.float32,
            )
        )
    return (jnp.concatenate(query_parts, axis=1), delta_keys, delta_values)


def per_device(
    tokens,
    norm_one_gain,
    norm_one_shift,
    project_weight,
    project_bias,
    output_weight,
    norm_two_gain,
    norm_two_shift,
    gate_up_weight,
    down_weight,
    cotangent,
):
    width_share = tokens.shape[1]
    token_count = tokens.shape[0]
    heads_here = width_share // HEAD_DIM
    sequences = token_count // SEQ
    block_rows = min(512, SEQ)
    offset = lax.axis_index("tensor") * width_share
    whole_input, gain_one, shift_one, gain_two, shift_two = (
        lax.all_gather(tokens, "tensor", axis=1, tiled=True),
        lax.all_gather(norm_one_gain, "tensor", axis=0, tiled=True),
        lax.all_gather(norm_one_shift, "tensor", axis=0, tiled=True),
        lax.all_gather(norm_two_gain, "tensor", axis=0, tiled=True),
        lax.all_gather(norm_two_shift, "tensor", axis=0, tiled=True),
    )
    inputs = whole_input.astype(jnp.float32)
    normed_one, unit_one, inverse_one = norm_forward(
        inputs, gain_one.astype(jnp.float32), shift_one.astype(jnp.float32)
    )
    normed_one = normed_one.astype(jnp.bfloat16)
    project = jnp.einsum(
        "td,dkc->tkc", normed_one, project_weight, preferred_element_type=jnp.float32
    )
    project = (project + project_bias.astype(jnp.float32)).reshape(
        sequences, SEQ, 3, heads_here, HEAD_DIM
    )
    cosine_table, sine_table = rotary_tables(SEQ)
    query_heads = rotate(project[:, :, 0], cosine_table, sine_table).astype(jnp.bfloat16)
    key_heads = rotate(project[:, :, 1], cosine_table, sine_table).astype(jnp.bfloat16)
    value_heads = project[:, :, 2].astype(jnp.bfloat16)
    context, log_sums = attend(query_heads, key_heads, value_heads, block_rows)
    context = context.astype(jnp.bfloat16).reshape(token_count, width_share)
    partial_branch = jnp.dot(context, output_weight, preferred_element_type=jnp.float32)
    branch = lax.psum(partial_branch, "tensor")
    middle = inputs + branch
    middle_share = lax.dynamic_slice_in_dim(middle, offset, width_share, 1)
    normed_two, unit_two, inverse_two = norm_forward(
        middle, gain_two.astype(jnp.float32), shift_two.astype(jnp.float32)
    )
    normed_two = normed_two.astype(jnp.bfloat16)
    gate_up = jnp.einsum(
        "td,dkf->tkf", normed_two, gate_up_weight, preferred_element_type=jnp.float32
    )
    gate_pre = gate_up[:, 0]
    upward = gate_up[:, 1]
    gate_sigmoid = jax.nn.sigmoid(gate_pre)
    hidden = (gate_pre * gate_sigmoid * upward).astype(jnp.bfloat16)
    mlp_share = lax.psum_scatter(
        jnp.dot(hidden, down_weight, preferred_element_type=jnp.float32),
        "tensor",
        scatter_dimension=1,
        tiled=True,
    )
    result = (middle_share + mlp_share).astype(jnp.bfloat16)
    upstream = lax.all_gather(cotangent, "tensor", axis=1, tiled=True)
    down_weight_grad = jnp.einsum("tf,td->fd", hidden, upstream, preferred_element_type=jnp.float32)
    delta_hidden = jnp.einsum(
        "td,fd->tf", upstream, down_weight, preferred_element_type=jnp.float32
    )
    delta_gate = (
        delta_hidden * upward * (gate_sigmoid + gate_pre * gate_sigmoid * (1.0 - gate_sigmoid))
    )
    delta_up = delta_hidden * gate_pre * gate_sigmoid
    delta_gate_up = jnp.stack([delta_gate, delta_up], axis=1).astype(jnp.bfloat16)
    gate_up_weight_grad = jnp.einsum(
        "td,tkf->dkf", normed_two, delta_gate_up, preferred_element_type=jnp.float32
    )
    delta_normed_two = jnp.einsum(
        "tkf,dkf->td", delta_gate_up, gate_up_weight, preferred_element_type=jnp.float32
    )
    delta_two_share = lax.psum_scatter(delta_normed_two, "tensor", scatter_dimension=1, tiled=True)
    unit_two_share = lax.dynamic_slice_in_dim(unit_two, offset, width_share, 1)
    scaled_two, terms_two, norm_two_gain_grad, norm_two_shift_grad = norm_back_terms(
        delta_two_share, unit_two_share, norm_two_gain.astype(jnp.float32)
    )
    totals_two = lax.psum((terms_two[0], terms_two[1]), "tensor")
    delta_middle_share = cotangent.astype(jnp.float32) + norm_back_finish(
        scaled_two, unit_two_share, inverse_two, totals_two
    )
    delta_branch = lax.all_gather(
        delta_middle_share.astype(jnp.bfloat16), "tensor", axis=1, tiled=True
    )
    output_weight_grad = jnp.einsum(
        "tc,td->cd", context, delta_branch, preferred_element_type=jnp.float32
    )
    delta_context = jnp.einsum(
        "td,cd->tc", delta_branch, output_weight, preferred_element_type=jnp.float32
    )
    delta_context = delta_context.astype(jnp.bfloat16).reshape(sequences, SEQ, heads_here, HEAD_DIM)
    delta_query, delta_keys, delta_values = attend_back(
        query_heads, key_heads, value_heads, delta_context, log_sums, block_rows
    )
    delta_project = jnp.stack(
        [
            rotate_back(delta_query, cosine_table, sine_table),
            rotate_back(delta_keys, cosine_table, sine_table),
            delta_values,
        ],
        axis=2,
    )
    delta_project = delta_project.reshape(token_count, 3, width_share).astype(jnp.bfloat16)
    project_bias_grad = jnp.sum(delta_project, axis=0, dtype=jnp.float32)
    project_weight_grad = jnp.einsum(
        "td,tkc->dkc", normed_one, delta_project, preferred_element_type=jnp.float32
    )
    delta_normed_one = jnp.einsum(
        "tkc,dkc->td", delta_project, project_weight, preferred_element_type=jnp.float32
    )
    delta_one_share = lax.psum_scatter(delta_normed_one, "tensor", scatter_dimension=1, tiled=True)
    unit_one_share = lax.dynamic_slice_in_dim(unit_one, offset, width_share, 1)
    scaled_one, terms_one, norm_one_gain_grad, norm_one_shift_grad = norm_back_terms(
        delta_one_share, unit_one_share, norm_one_gain.astype(jnp.float32)
    )
    totals_one = lax.psum((terms_one[0], terms_one[1]), "tensor")
    tokens_grad = delta_middle_share + norm_back_finish(
        scaled_one, unit_one_share, inverse_one, totals_one
    )
    (
        norm_one_gain_grad,
        norm_one_shift_grad,
        project_weight_grad,
        project_bias_grad,
        output_weight_grad,
        norm_two_gain_grad,
        norm_two_shift_grad,
        gate_up_weight_grad,
        down_weight_grad,
    ) = lax.psum(
        (
            norm_one_gain_grad,
            norm_one_shift_grad,
            project_weight_grad,
            project_bias_grad,
            output_weight_grad,
            norm_two_gain_grad,
            norm_two_shift_grad,
            gate_up_weight_grad,
            down_weight_grad,
        ),
        "dp",
    )
    return (
        result,
        tokens_grad,
        norm_one_gain_grad,
        norm_one_shift_grad,
        project_weight_grad,
        project_bias_grad,
        output_weight_grad,
        norm_two_gain_grad,
        norm_two_shift_grad,
        gate_up_weight_grad,
        down_weight_grad,
    )


def solution(mesh):
    return jax.shard_map(
        per_device,
        mesh=mesh,
        in_specs=(
            P("dp", "tensor"),
            P("tensor"),
            P("tensor"),
            P(None, None, "tensor"),
            P(None, "tensor"),
            P("tensor", None),
            P("tensor"),
            P("tensor"),
            P(None, None, "tensor"),
            P("tensor", None),
            P("dp", "tensor"),
        ),
        out_specs=(
            P("dp", "tensor"),
            P("dp", "tensor"),
            P("tensor"),
            P("tensor"),
            P(None, None, "tensor"),
            P(None, "tensor"),
            P("tensor", None),
            P("tensor"),
            P("tensor"),
            P(None, None, "tensor"),
            P("tensor", None),
        ),
        check_vma=False,
    )
```

profile of v0, /device:TPU:0, one launch (start us, length us, event | category | flops | bytes accessed | tf_op | source)
XLA Modules:
  0.0 1747.8 jit_solution(2672416198703303327)
XLA Ops:
  9.3 13.5 all-gather.1
  23.6 12.2 all-gather
  37.3 56.0 %all-gather.8.cloned.1.call-done = bf16[1024,2048]{1,0:T(8,128)(2,1)} async-done(((bf16[1024,512]{1,0:T(8,128)(2,1)}), bf16[1024,2048]{1,0:T(8,128)(2,1)}) %all-gather.8.cloned.1.call-update) | async-done | bytes 4194320 | tf_op jit(solution)/shard_map/all_gather | solution.py:172
  139.9 12.0 all-gather.3
  151.9 14.4 all-gather.2
  166.3 262.4 %all-reduce.9.cloned.1.call-done = f32[1024,2048]{1,0:T(8,128)} async-done(((f32[1024,2048]{1,0:T(8,128)}), f32[1024,2048]{1,0:T(8,128)}) %all-reduce.9.cloned.1.call-update) | async-done | bytes 8388624 | tf_op jit(solution)/shard_map/psum | solution.py:196
  443.2 17.8 %fusion.4 = f32[1024,2,1408]{2,0,1:T(8,128)} fusion(bf16[2048,2,1408]{2,1,0:T(2,128)(2,1)} %param.31, f32[1024,2048]{1,0:T(8,128)S(1)} %subtract_multiply_fusion, f32[2048]{0:T(1024)S(1)} %bitcast.181, f32[2048]{0:T(1024)S(1)} %bitcast.183), kind=kOutput, calls=%fused_computation.13 | convolution fusion | flops 11817451520 | bytes 31473664 | tf_op jit(solution)/shard_map/td,dkf->tkf/dot_general | solution.py:203
  461.0 49.0 %all-gather.10.cloned.1.call-done = bf16[1024,2048]{1,0:T(8,128)(2,1)} async-done(((bf16[1024,512]{1,0:T(8,128)(2,1)}), bf16[1024,2048]{1,0:T(8,128)(2,1)}) %all-gather.10.cloned.1.call-update) | async-done | bytes 4194320 | tf_op jit(solution)/shard_map/all_gather | solution.py:217
  510.1 15.5 fusion.26
  528.0 17.4 fusion.16
  545.5 143.1 %reduce-scatter.6.cloned.1.call-done = f32[1024,512]{1,0:T(8,128)} async-done(((f32[1024,2048]{1,0:T(8,128)}), f32[1024,512]{1,0:T(8,128)}) %reduce-scatter.6.cloned.1.call-update) | async-done | bytes 2097168 | tf_op jit(solution)/shard_map/reduce_scatter | solution.py:233
  707.7 11.8 fusion.71
  719.5 67.4 %all-gather.12.cloned.1.call-done = bf16[1024,2048]{1,0:T(8,128)(2,1)} async-done(((bf16[1024,512]{1,0:T(8,128)(2,1)}), bf16[1024,2048]{1,0:T(8,128)(2,1)}) %all-gather.12.cloned.1.call-update) | async-done | bytes 4194320 | tf_op jit(solution)/shard_map/all_gather | solution.py:242
  818.4 11.9 multiply_reduce_fusion
  830.2 11.9 multiply_convert_fusion
  866.1 11.4 fusion.72
  877.5 21.0 %fusion.25 = f32[2048,2,1408]{2,0,1:T(8,128)} fusion(bf16[1024,1,1408]{2,0,1:T(8,128)(2,1)} %copy-done.53, bf16[1024,1,1408]{2,0,1:T(8,128)(2,1)} %copy-done.52, f32[1024,2048]{1,0:T(8,128)} %copy-done.7, f32[2048]{0:T(1024)S(1)} %bitcast.182, f32[2048]{0:T(1024)S(1)} %bitcast.184), kind=kOutput, calls=%fused_computation.49 | convolution fusion | flops 11828985856 | bytes 37240832 | tf_op jit(solution)/shard_map/td,tkf->dkf/dot_general | solution.py:227
  902.9 11.8 fusion.51
  915.4 16.7 reduce-scatter.4.cloned.1.call-done
  936.3 143.4 %reduce-scatter.8.cloned.1.call-done = f32[1024,512]{1,0:T(8,128)} async-done(((f32[1024,2048]{1,0:T(8,128)}), f32[1024,512]{1,0:T(8,128)}) %reduce-scatter.8.cloned.1.call-update) | async-done | bytes 2097168 | tf_op jit(solution)/shard_map/reduce_scatter | solution.py:271
  1082.7 25.3 %all-reduce.2 = (f32[512]{0:T(512)}, f32[512]{0:T(512)}, f32[3,512]{1,0:T(4,128)}, f32[512]{0:T(512)}, f32[512]{0:T(512)}) all-reduce(f32[512]{0:T(512)S(1)} %get-tuple-element.99, f32[512]{0:T(512)S(1)} %get-tuple-element.104, f32[3,512]{1,0:T(4,128)S(1)} %convert_reduce_fusion.1, ...), channel_id=1, replica_groups=mesh['dp'=8,'tensor'=4] {'dp'}, use_global_device_ids=true, to_apply=%region_23.24 | all-reduce | flops 3584 | bytes 28672 | tf_op jit(solution)/shard_map/psum | solution.py:290
  1108.0 11.8 all-reduce.4
  1124.2 553.9 %all-reduce.11.cloned.1.call-done = (f32[2048,3,512]{2,0,1:T(8,128)}, f32[512,2048]{1,0:T(8,128)}, f32[2048,2,1408]{2,0,1:T(8,128)}, f32[1408,2048]{1,0:T(8,128)}) async-done(((f32[2048,3,512]{2,0,1:T(8,128)}, f32[512,2048]{1,0:T(8,128)}, f32[2048,2,1408]{2,0,1:T(8,128)}, f32[1408,2048]{1,0:T(8,128)}), (f32[2048,3,512]{2,0,1:T(8,128)}, f32[512,2048]{1,0:T(8,128)}, f32[2048,2,1408]{2,0,1:T(8,128)}, ...) | async-done | bytes 51380240 | tf_op jit(solution)/shard_map/psum | solution.py:290
  1678.1 38.6 %copy.47 = f32[2048,2,1408]{2,1,0:T(2,128)} copy(f32[2048,2,1408]{2,0,1:T(8,128)} %get-tuple-element.112) | data formatting | bytes 46137344
  (198 shorter events, 182.4 us)
Async XLA Ops:
  7.2 126.1 %copy-start = (bf16[512,2048]{1,0:T(8,128)(2,1)S(1)}, bf16[512,2048]{1,0:T(8,128)(2,1)}, u32[]{:S(2)}) copy-start(bf16[512,2048]{1,0:T(8,128)(2,1)} %param.28) | copy-start | bytes 6291460
  7.2 86.0 %all-gather.8.cloned.1.call-start = ((), (), s32[]{:S(2)}) async-start(), calls=%async_computation.3 | async-start | bytes 5242880 | tf_op jit(solution)/shard_map/all_gather | solution.py:172
  7.9 420.7 %all-reduce.9.cloned.1.call-start = ((), (), s32[]{:S(2)}) async-start(), calls=%async_computation.4 | async-start | bytes 16777216 | tf_op jit(solution)/shard_map/psum | solution.py:196
  22.9 85.5 %copy-start.40 = (f32[4,1,512]{2,1,0:T(1,128)}, f32[4,1,512]{2,1,0:T(1,128)S(1)}, u32[]{:S(2)}) copy-start(f32[4,1,512]{2,1,0:T(1,128)S(1)} %convert_element_type.143) | copy-start | bytes 24580
  35.8 72.6 %copy-start.42 = (f32[4,1,512]{2,1,0:T(1,128)}, f32[4,1,512]{2,1,0:T(1,128)S(1)}, u32[]{:S(2)}) copy-start(f32[4,1,512]{2,1,0:T(1,128)S(1)} %convert_element_type.142) | copy-start | bytes 24580
  36.1 76.3 %copy-start.30 = (f32[1024,8]{0,1:T(8,128)}, f32[1024,8]{0,1:T(8,128)S(1)}, u32[]{:S(2)}) copy-start(f32[1024,8]{0,1:T(8,128)S(1)} %get-tuple-element.140) | copy-start | bytes 98308
  36.1 76.3 %copy-start.32 = (f32[1024,8]{0,1:T(8,128)}, f32[1024,8]{0,1:T(8,128)S(1)}, u32[]{:S(2)}) copy-start(f32[1024,8]{0,1:T(8,128)S(1)} %get-tuple-element.141) | copy-start | bytes 98308
  96.7 332.0 %copy-start.36 = (f32[1024]{0:T(1024)}, f32[1024]{0:T(1024)S(1)}, u32[]{:S(2)}) copy-start(f32[1024]{0:T(1024)S(1)} %broadcast_multiply_fusion.5) | copy-start | bytes 12292
  97.9 330.8 %copy-start.34 = (f32[1024]{0:T(1024)}, f32[1024]{0:T(1024)S(1)}, u32[]{:S(2)}) copy-start(f32[1024]{0:T(1024)S(1)} %add_rsqrt_fusion.1) | copy-start | bytes 12292
  139.1 371.0 %all-gather.10.cloned.1.call-start = ((), (), s32[]{:S(2)}) async-start(), calls=%async_computation.6 | async-start | bytes 5242880 | tf_op jit(solution)/shard_map/all_gather | solution.py:217
  139.8 548.7 %reduce-scatter.6.cloned.1.call-start = ((), (), s32[]{:S(2)}) async-start(), calls=%async_computation.7 | async-start | bytes 10485760 | tf_op jit(solution)/shard_map/reduce_scatter | solution.py:233
  545.4 241.5 %all-gather.12.cloned.1.call-start = ((), (), s32[]{:S(2)}) async-start(), calls=%async_computation.8 | async-start | bytes 5242880 | tf_op jit(solution)/shard_map/all_gather | solution.py:242
  707.6 224.5 %reduce-scatter.4.cloned.1.call-start = ((), (), s32[]{:S(2)}) async-start(), calls=%async_computation.5 | async-start | bytes 10485760 | tf_op jit(solution)/shard_map/reduce_scatter | solution.py:210
  719.4 360.3 %reduce-scatter.8.cloned.1.call-start = ((), (), s32[]{:S(2)}) async-start(), calls=%async_computation.9 | async-start | bytes 10485760 | tf_op jit(solution)/shard_map/reduce_scatter | solution.py:271
  850.5 52.3 %copy-start.15 = (bf16[1024,1,512]{2,0,1:T(8,128)(2,1)}, bf16[1024,1,512]{2,0,1:T(8,128)(2,1)S(1)}, u32[]{:S(2)}) copy-start(bf16[1024,1,512]{2,0,1:T(8,128)(2,1)S(1)} %copy.43) | copy-start | bytes 3145732
  854.8 48.1 %copy-start.17 = (bf16[1024,1,512]{2,0,1:T(8,128)(2,1)}, bf16[1024,1,512]{2,0,1:T(8,128)(2,1)S(1)}, u32[]{:S(2)}) copy-start(bf16[1024,1,512]{2,0,1:T(8,128)(2,1)S(1)} %copy.42) | copy-start | bytes 3145732
  866.0 812.0 %all-reduce.11.cloned.1.call-start = ((), (), s32[]{:S(2)}) async-start(), calls=%async_computation.10 | async-start | bytes 102760448 | tf_op jit(solution)/shard_map/psum | solution.py:290
  877.5 21.0 %copy-start.47 = (bf16[1024,2048]{1,0:T(8,128)(2,1)S(1)}, bf16[1024,2048]{1,0:T(8,128)(2,1)}, u32[]{:S(2)}) copy-start(bf16[1024,2048]{1,0:T(8,128)(2,1)} %all-gather.12.cloned.1.call-done) | copy-start | bytes 12582916
  877.5 21.0 %copy-start.49 = (bf16[8,64,512]{2,1,0:T(8,128)(2,1)S(1)}, bf16[8,64,512]{2,1,0:T(8,128)(2,1)}, u32[]{:S(2)}) copy-start(bf16[8,64,512]{2,1,0:T(8,128)(2,1)} %copy-done.48) | copy-start | bytes 1572868
  877.5 21.0 %copy-start.51 = (bf16[8,64,512]{2,1,0:T(8,128)(2,1)S(1)}, bf16[8,64,512]{2,1,0:T(8,128)(2,1)}, u32[]{:S(2)}) copy-start(bf16[8,64,512]{2,1,0:T(8,128)(2,1)} %copy-done.50) | copy-start | bytes 1572868
  915.4 20.4 %copy-start.14 = (bf16[1024,1,512]{2,0,1:T(8,128)(2,1)S(1)}, bf16[1024,1,512]{2,0,1:T(8,128)(2,1)}, u32[]{:S(2)}) copy-start(bf16[1024,1,512]{2,0,1:T(8,128)(2,1)} %copy.44) | copy-start | bytes 3145732
  915.4 167.2 %copy-start.38 = (f32[512]{0:T(512)S(1)}, f32[512]{0:T(512)}, u32[]{:S(2)}) copy-start(f32[512]{0:T(512)} %get-tuple-element.97) | copy-start | bytes 6148
  915.4 204.4 %copy-start.10 = (f32[1024,512]{1,0:T(8,128)S(1)}, f32[1024,512]{1,0:T(8,128)}, u32[]{:S(2)}) copy-start(f32[1024,512]{1,0:T(8,128)} %get-tuple-element.119) | copy-start | bytes 6291460
  932.1 150.5 %copy-start.39 = (f32[512]{0:T(512)S(1)}, f32[512]{0:T(512)}, u32[]{:S(2)}) copy-start(f32[512]{0:T(512)} %get-tuple-element.103) | copy-start | bytes 6148
  (38 other events, 193.9 us)
Sparse Core Ops, SparseCore 0:
  9.6 83.5 all-gather.7
  139.2 289.4 all-reduce.8
  430.2 79.7 all-gather.9
  545.5 142.9 reduce-scatter.5
  707.7 79.1 all-gather.11
  789.1 142.9 reduce-scatter.3
  934.5 145.1 reduce-scatter.7
  1085.1 592.8 all-reduce.10
where the time goes:
time: 1760 us; the launch traced here: 1750 us
  waiting for transfers between devices  1290 us (73%)
  matrix products  192 us (11%)
  blocking collectives  100 us (6%)
  local copies, waits for them, and re-layouts  85.4 us (5%)
  other arithmetic  60.6 us (3%)
    psum x1, waiting for transfers between devices, per_device(): lax.psum((norm_one_gain_grad, norm_one_shift_grad, project_weight_grad, p...  554 us
    psum x1, waiting for transfers between devices, per_device(): branch = lax.psum(partial_branch, 'tensor')  262 us
    reduce_scatter x1, waiting for transfers between devices, per_device(): lax.psum_scatter(delta_normed_one, 'tensor', scatter_dimension=1, tiled=T...  143 us
    reduce_scatter x1, waiting for transfers between devices, per_device(): lax.psum_scatter(delta_normed_two, 'tensor', scatter_dimension=1, tiled=T...  143 us
    unnamed x116, local copies, waits for them, and re-layouts  79 us
    all_gather x1, waiting for transfers between devices, per_device(): lax.all_gather(delta_middle_share.astype(jnp.bfloat16), 'tensor', axis=1,...  67.4 us
    all_gather x1, waiting for transfers between devices, per_device(): lax.all_gather(tokens, 'tensor', axis=1, tiled=True)  56 us
    all_gather x1, waiting for transfers between devices, per_device(): upstream = lax.all_gather(cotangent, 'tensor', axis=1, tiled=True)  49 us
  transfers between devices with their start and end apart: 8, of which 8 were waited for; matrix products, arithmetic and copies ran while one was open for 10% of the time, Pallas kernels for 0%

commit v1 on v0

v1 whole, which is shorter than its diff:
```python
import functools

import jax
import jax.numpy as jnp
from jax import lax
from jax.experimental import pallas as pl
from jax.experimental.pallas import tpu as pltpu
from jax.sharding import PartitionSpec as P

D = 2048
HEAD_DIM = 64
ROT = 16
SEQ = 1024
PAIR = 2 * HEAD_DIM
CHUNKS = 1
SUB = 256
LIGHT = 64
EXTRA = 16

EPSILON = 1e-05
ROPE_BASE = 10000.0
BF = jnp.bfloat16
F32 = jnp.float32
NT = (((1,), (1,)), ((), ()))
TN = (((0,), (0,)), ((), ()))
ANY = pl.BlockSpec(memory_space=pl.ANY)


def dot(a, b, dims=(((1,), (0,)), ((), ()))):
    return lax.dot_general(a, b, dims, preferred_element_type=F32)


def params(mib):
    return pltpu.CompilerParams(vmem_limit_bytes=mib << 20)


def cost(flops, nbytes):
    return pl.CostEstimate(flops=int(flops) // LIGHT, bytes_accessed=int(nbytes) // LIGHT, transcendentals=0)


def after(value, *others):
    return lax.optimization_barrier((value, *others))[0]


def kernel_call(body, grid, ins, in_specs, outs, out_specs, previous=(), scratch=(), mib=56, flops=0, name=None, weight=1):
    given = len(ins)
    previous = dict(previous)
    aliases = {given + i: out for i, out in enumerate(previous)}

    def run(*refs):
        body(*refs[:given], *refs[given + len(previous) :])

    nbytes = sum(a.size * a.dtype.itemsize for a in ins) + sum(o.size * o.dtype.itemsize for o in outs)
    return pl.pallas_call(
        run,
        grid=grid,
        in_specs=list(in_specs) + [ANY] * len(previous),
        out_specs=list(out_specs),
        out_shape=list(outs),
        input_output_aliases=aliases,
        scratch_shapes=list(scratch),
        compiler_params=params(mib),
        cost_estimate=cost(weight * flops, nbytes),
        name=name,
    )(*ins, *previous.values())


def still(block, index):
    return pl.BlockSpec(block, index, pipeline_mode=pl.Buffered(1))


def sds(shape, dtype):
    return jax.ShapeDtypeStruct(shape, dtype)


def prefetched(body, scalars, grid, ins, in_specs, outs, out_specs, mib=56, flops=0, name=None):
    nbytes = sum(a.size * a.dtype.itemsize for a in ins) + sum(o.size * o.dtype.itemsize for o in outs)
    return pl.pallas_call(
        body,
        grid_spec=pltpu.PrefetchScalarGridSpec(
            num_scalar_prefetch=1, grid=grid, in_specs=in_specs, out_specs=out_specs
        ),
        out_shape=outs,
        compiler_params=params(mib),
        cost_estimate=cost(flops, nbytes),
        name=name,
    )(jnp.stack(scalars).astype(jnp.int32), *ins)


def norm_rows(x_ref, gain, shift, normed_ref, stats_ref, rows=64):
    def step(i, carry):
        at = pl.ds(pl.multiple_of(i * rows, rows), rows)
        x = x_ref[at, :].astype(F32)
        mean = jnp.mean(x, axis=-1, keepdims=True)
        centered = x - mean
        inverse = lax.rsqrt(jnp.mean(centered * centered, axis=-1, keepdims=True) + EPSILON)
        normed_ref[at, :] = (centered * inverse * gain + shift).astype(BF)
        lane = lax.broadcasted_iota(jnp.int32, (rows, 128), 1)
        stats_ref[at, :] = jnp.where(lane == 0, mean, inverse)
        return carry

    lax.fori_loop(0, x_ref.shape[0] // rows, step, 0)


def rope_tables():
    lane = jnp.arange(PAIR, dtype=jnp.int32)[None, :] % HEAD_DIM
    half = ROT // 2
    index = (lane % half).astype(F32)
    angles = jnp.arange(SEQ, dtype=F32)[:, None] * ROPE_BASE ** (-(index * (2.0 / ROT)))
    turned = lane < ROT
    cosine = jnp.where(turned, jnp.cos(angles), 1.0)
    low = jnp.where(turned & (lane >= half), jnp.sin(angles), 0.0)
    high = jnp.where(lane < half, -jnp.sin(angles), 0.0)
    return jnp.stack([cosine, low, high])


def turn(values, table):
    half = ROT // 2
    return (
        values * table[0]
        + pltpu.roll(values, half, 1) * table[1]
        + pltpu.roll(values, values.shape[1] - half, 1) * table[2]
    )


def turn_back(values, table):
    half = ROT // 2
    return (
        values * table[0]
        - pltpu.roll(values, half, 1) * table[1]
        - pltpu.roll(values, values.shape[1] - half, 1) * table[2]
    )


def project_body(x_ref, small_ref, weight_ref, bias_ref, table_ref, normed_ref, stats_ref, heads_ref):
    part = pl.program_id(0)

    @pl.when(part == 0)
    def _():
        gain, shift = (small_ref[k : k + 1, :].astype(F32) for k in (0, 1))
        norm_rows(x_ref, gain, shift, normed_ref, stats_ref)

    out = dot(normed_ref[...], weight_ref[0]) + bias_ref[0]
    width = out.shape[1]

    @pl.when(part < 2)
    def _():
        table = table_ref[...]
        for p in range(width // PAIR):
            heads_ref[0, :, p * PAIR : (p + 1) * PAIR] = turn(out[:, p * PAIR : (p + 1) * PAIR], table).astype(BF)

    @pl.when(part == 2)
    def _():
        heads_ref[0] = out.astype(BF)


def project(c, x, weight, bias, tables, previous):
    t, width = x.shape[0] - EXTRA, weight.shape[2]
    total = t * CHUNKS
    one = lambda k: (0, 0)
    return kernel_call(
        project_body,
        (3,),
        [x, x, weight, bias, tables],
        [
            still((t, D), one),
            pl.BlockSpec((EXTRA, D), lambda k: (t // EXTRA, 0)),
            pl.BlockSpec((1, D, width), lambda k: (k, 0, 0)),
            pl.BlockSpec((1, 1, width), lambda k: (k, 0, 0)),
            still((3, t, PAIR), lambda k: (0, c, 0)),
        ],
        [sds((total, D), BF), sds((total, 128), F32), sds((3, total, width), BF)],
        [
            pl.BlockSpec((t, D), lambda k: (c, 0)),
            pl.BlockSpec((t, 128), lambda k: (c, 0)),
            pl.BlockSpec((1, t, width), lambda k: (k, c, 0)),
        ],
        previous,
        mib=34,
        flops=2 * t * D * 3 * width,
        name="project",
    )


def lane_of(rows):
    return lax.broadcasted_iota(jnp.int32, (rows, PAIR), 1) < HEAD_DIM


def attend_body(c, owners_ref, q_ref, k_ref, v_ref, out_weight_ref, first_ref, rest_ref, ctx_ref, lse_ref):
    pair = pl.program_id(0)
    t = q_ref.shape[1]
    scale = HEAD_DIM ** (-0.5)
    low = lane_of(SUB)
    for r in range(t // SUB):
        start = c * t + r * SUB
        extent = start + SUB
        q = q_ref[0, r * SUB : (r + 1) * SUB, :].astype(F32) * scale
        keys = k_ref[0, :extent, :]
        values = v_ref[0, :extent, :]
        row = start + lax.broadcasted_iota(jnp.int32, (SUB, extent), 0)
        seen = lax.broadcasted_iota(jnp.int32, (SUB, extent), 1) <= row
        contexts, sums = [], []
        for h in range(2):
            own = jnp.where(low if h == 0 else ~low, q, 0.0).astype(BF)
            scores = jnp.where(seen, dot(own, keys, NT), -1000000000.0)
            top = jnp.max(scores, axis=-1, keepdims=True)
            raised = jnp.exp(scores - top)
            total = jnp.sum(raised, axis=-1, keepdims=True)
            contexts.append(dot(raised.astype(BF), values) / total)
            sums.append(top + jnp.log(total))
        at = pl.ds(pl.multiple_of(pair * PAIR, PAIR), PAIR)
        ctx_ref[r * SUB : (r + 1) * SUB, at] = jnp.where(low, contexts[0], contexts[1]).astype(BF)
        lse_ref[r * SUB : (r + 1) * SUB, :] = jnp.where(low, sums[0], sums[1])

    @pl.when(pair == pl.num_programs(0) - 1)
    def _():
        wide = first_ref.shape[1]
        for j in range(D // wide):
            at = pl.ds(pl.multiple_of(owners_ref[j] * wide, wide), wide)
            out = dot(ctx_ref[...], out_weight_ref[:, at]).astype(BF)
            if j == 0:
                first_ref[...] = out
            else:
                rest_ref[:, (j - 1) * wide : j * wide] = out


def attend(owners, heads, out_weight):
    t, width = heads.shape[1], heads.shape[2]
    here = lambda p, owners: (0, p)
    fixed = lambda p, owners: (0, 0)
    return prefetched(
        functools.partial(attend_body, 0),
        owners,
        (width // PAIR,),
        [heads, heads, heads, out_weight],
        [pl.BlockSpec((1, t, PAIR), lambda p, owners, k=k: (k, 0, p)) for k in range(3)]
        + [still((width, D), fixed)],
        [sds((t, width), BF), sds((t, D - width), BF), sds((t, width), BF), sds((t, width), F32)],
        [
            pl.BlockSpec((t, width), fixed),
            pl.BlockSpec((t, D - width), fixed),
            pl.BlockSpec((t, width), fixed),
            pl.BlockSpec((t, PAIR), here),
        ],
        mib=30,
        flops=(8 * t * t * width + 2 * t * width * D) * 4 * LIGHT,
        name="attend",
    )


def attend_back_body(c, *refs):
    q_ref, k_ref, v_ref, lse_ref, ctx_ref, dctx_ref, table_ref, with_ref, dq_ref, dk_ref, dv_ref, sums_ref, dk_sum, dv_sum = refs
    t = q_ref.shape[1]

    @pl.when(pl.program_id(0) == 0)
    def _():
        sums_ref[...] = jnp.zeros_like(sums_ref)

    def row_sums(k, gradient, values, at):
        first = gradient * with_ref[0, k : k + 1, :]
        second = gradient * (values - with_ref[1, k : k + 1, :])
        sums_ref[0:1, at] += jnp.sum(first.T, axis=0, keepdims=True)
        sums_ref[1:2, at] += jnp.sum(second.T, axis=0, keepdims=True)

    scale = HEAD_DIM ** (-0.5)
    low = lane_of(SUB)
    dk_sum[...] = jnp.zeros_like(dk_sum)
    dv_sum[...] = jnp.zeros_like(dv_sum)
    for r in range(t // SUB):
        here = slice(r * SUB, (r + 1) * SUB)
        start = c * t + r * SUB
        extent = start + SUB
        q = q_ref[0, here, :].astype(F32) * scale
        keys = k_ref[0, :extent, :]
        values = v_ref[0, :extent, :]
        dctx = dctx_ref[here, :]
        lse_t = lse_ref[here, :].T
        product_t = (ctx_ref[here, :].astype(F32) * dctx.astype(F32)).T
        low_keys = lane_of(extent)
        column = start + lax.broadcasted_iota(jnp.int32, (extent, SUB), 1)
        seen = lax.broadcasted_iota(jnp.int32, (extent, SUB), 0) <= column
        dq = jnp.zeros((SUB, PAIR), F32)
        for h in range(2):
            own = low if h == 0 else ~low
            q_own = jnp.where(own, q, 0.0).astype(BF)
            dctx_own = jnp.where(own, dctx, jnp.zeros_like(dctx))
            rows = slice(h * HEAD_DIM, (h + 1) * HEAD_DIM)
            row_dot = jnp.sum(product_t[rows, :], axis=0, keepdims=True)
            scores = dot(keys, q_own, NT) - lse_t[h * HEAD_DIM : h * HEAD_DIM + 1, :]
            probs = jnp.where(seen, jnp.exp(scores), 0.0)
            delta_probs = dot(values, dctx_own, NT)
            delta_scores = (probs * (delta_probs - row_dot)).astype(BF)
            dv_sum[:extent, :] += dot(probs.astype(BF), dctx_own)
            dk_sum[:extent, :] += dot(delta_scores, q_own)
            keys_own = jnp.where(low_keys if h == 0 else ~low_keys, keys, jnp.zeros_like(keys))
            dq = dq + dot(delta_scores, keys_own, TN)
        table = table_ref[:, start:extent, :]
        dq = turn_back(dq * scale, table)
        dq_ref[here, :] = dq.astype(BF)
        row_sums(0, dq, turn_back(q_ref[0, here, :].astype(F32), table), here)
    for r in range(t // SUB):
        here = slice(r * SUB, (r + 1) * SUB)
        table = table_ref[:, here, :]
        dk = turn_back(dk_sum[here, :], table)
        dk_ref[here, :] = dk.astype(BF)
        row_sums(1, dk, turn_back(k_ref[0, here, :].astype(F32), table), here)
        dv = dv_sum[here, :]
        dv_ref[here, :] = dv.astype(BF)
        row_sums(2, dv, v_ref[0, here, :].astype(F32), here)


def attend_back(heads, lse, ctx, dctx, tables, with_rows):
    t, width = heads.shape[1], heads.shape[2]
    own = pl.BlockSpec((t, PAIR), lambda p: (0, p))
    return kernel_call(
        functools.partial(attend_back_body, 0),
        (width // PAIR,),
        [heads, heads, heads, lse, ctx, dctx, tables, with_rows],
        [pl.BlockSpec((1, t, PAIR), lambda p, k=k: (k, 0, p)) for k in range(3)]
        + [own, own, own, still((3, t, PAIR), lambda p: (0, 0, 0)), pl.BlockSpec((2, 3, PAIR), lambda p: (0, 0, p))],
        [sds((t, width), BF)] * 3 + [sds((8, t), F32)],
        [own, own, own, pl.BlockSpec((8, t), lambda p: (0, 0))],
        scratch=[pltpu.VMEM((t, PAIR), F32)] * 2,
        mib=28,
        flops=20 * t * t * width,
        name="attend_back",
        weight=4 * LIGHT,
    )


def mlp_body(mid_ref, up_ref, gain_ref, shift_ref, gate_w_ref, up_w_ref, down_w_ref, normed_ref, stats_ref, hidden_ref, dgate_ref, dup_ref):
    @pl.when(pl.program_id(0) == 0)
    def _():
        norm_rows(mid_ref, gain_ref[...], shift_ref[...], normed_ref, stats_ref)

    normed = normed_ref[...]
    gate = dot(normed, gate_w_ref[...])
    upward = dot(normed, up_w_ref[...])
    delta_hidden = dot(up_ref[...], down_w_ref[...], NT)
    sigmoid = jax.nn.sigmoid(gate)
    silu = gate * sigmoid
    hidden_ref[...] = (silu * upward).astype(BF)
    dgate_ref[...] = (delta_hidden * upward * (sigmoid + silu * (1.0 - sigmoid))).astype(BF)
    dup_ref[...] = (delta_hidden * silu).astype(BF)


def mlp(c, mid, upstream, gain, shift, gate_w, up_w, down_w, previous):
    t, units = mid.shape[0], gate_w.shape[1]
    total = t * CHUNKS
    tile = 256
    one = lambda j: (0, 0)
    own = lambda j: (c, 0)
    column = pl.BlockSpec((t, tile), lambda j: (c, j))
    return kernel_call(
        mlp_body,
        (pl.cdiv(units, tile),),
        [mid, upstream, gain, shift, gate_w, up_w, down_w],
        [
            still((t, D), one),
            still((t, D), own),
            pl.BlockSpec((1, D), one),
            pl.BlockSpec((1, D), one),
            pl.BlockSpec((D, tile), lambda j: (0, j)),
            pl.BlockSpec((D, tile), lambda j: (0, j)),
            pl.BlockSpec((tile, D), lambda j: (j, 0)),
        ],
        [sds((total, D), BF), sds((total, 128), F32)] + [sds((total, units), BF)] * 3,
        [pl.BlockSpec((t, D), own), pl.BlockSpec((t, 128), own), column, column, column],
        previous,
        mib=46,
        flops=6 * t * D * units,
        name="mlp",
    )


def mlp_back_body(owners_ref, dgate_ref, dup_ref, gate_w_ref, up_w_ref, out_ref):
    out_ref[...] = (dot(dgate_ref[...], gate_w_ref[...], NT) + dot(dup_ref[...], up_w_ref[...], NT)).astype(BF)


def mlp_back(owners, width, dgate, dup, gate_w, up_w):
    t, units = dgate.shape
    whole = still((t, units), lambda j, owners: (0, 0))
    weight = pl.BlockSpec((width, units), lambda j, owners: (owners[j], 0))
    return prefetched(
        mlp_back_body,
        owners,
        (len(owners),),
        [dgate, dup, gate_w, up_w],
        [whole, whole, weight, weight],
        [sds((t, len(owners) * width), BF)],
        [pl.BlockSpec((t, width), lambda j, owners: (0, j))],
        mib=28,
        flops=4 * t * D * units,
        name="mlp_back",
    )[0]


def branch_back_body(e_ref, mid_ref, stats_ref, up_ref, weight_ref, means_ref, dbranch_ref, dctx_ref):
    rows = 64

    def step(i, carry):
        at = pl.ds(pl.multiple_of(i * rows, rows), rows)
        e = e_ref[at, :].astype(F32)
        mean, inverse = stats_ref[at, 0:1], stats_ref[at, 1:2]
        unit = (mid_ref[at, :].astype(F32) - mean) * inverse
        first = jnp.mean(e, axis=-1, keepdims=True)
        second = jnp.mean(e * unit, axis=-1, keepdims=True)
        dbranch_ref[at, :] = (up_ref[at, :].astype(F32) + inverse * (e - first - unit * second)).astype(BF)
        lane = lax.broadcasted_iota(jnp.int32, (rows, 128), 1)
        means_ref[at, :] = jnp.where(lane == 0, first, second)
        return carry

    lax.fori_loop(0, e_ref.shape[0] // rows, step, 0)
    dctx_ref[...] = dot(dbranch_ref[...], weight_ref[...], NT).astype(BF)


def branch_back(e, mid, stats, upstream, weight):
    t, width = e.shape[0], weight.shape[0]
    tile = SUB
    row = lambda i: (i, 0)
    return kernel_call(
        branch_back_body,
        (t // tile,),
        [e, mid, stats, upstream, weight],
        [
            pl.BlockSpec((tile, D), row),
            pl.BlockSpec((tile, D), row),
            pl.BlockSpec((tile, 128), row),
            pl.BlockSpec((tile, D), row),
            still((width, D), lambda i: (0, 0)),
        ],
        [sds((t, 128), F32), sds((t, D), BF), sds((t, width), BF)],
        [pl.BlockSpec((tile, 128), row), pl.BlockSpec((tile, D), row), pl.BlockSpec((tile, width), row)],
        mib=24,
        flops=2 * t * D * width,
        name="branch_back",
    )


def project_back_body(owners_ref, dq_ref, dk_ref, dv_ref, weight_ref, x_ref, stats_ref, below_ref, out_ref):
    n = dot(dq_ref[...], weight_ref[0], NT) + dot(dk_ref[...], weight_ref[1], NT) + dot(dv_ref[...], weight_ref[2], NT)
    out_ref[: n.shape[0], :] = n.astype(BF)
    unit = (x_ref[...].astype(F32) - stats_ref[:, 0:1]) * stats_ref[:, 1:2]
    with_unit = n * unit
    row = lax.broadcasted_iota(jnp.int32, (EXTRA, n.shape[1]), 0)
    gain_grad = jnp.sum(with_unit, axis=0, keepdims=True)
    shift_grad = jnp.sum(n, axis=0, keepdims=True)
    out_ref[n.shape[0] :, :] = jnp.where(row == 0, gain_grad, jnp.where(row == 1, shift_grad, below_ref[...])).astype(BF)


def project_back(owners, dq, dk, dv, weight, x, stats, below):
    t, width = dq.shape
    count = len(owners)
    whole = still((t, width), lambda j, owners: (0, 0))
    return prefetched(
        project_back_body,
        owners,
        (count,),
        [dq, dk, dv, weight, x, stats, below],
        [
            whole,
            whole,
            whole,
            pl.BlockSpec((3, width, width), lambda j, owners: (0, owners[j], 0)),
            pl.BlockSpec((t, width), lambda j, owners: (0, owners[j])),
            still((t, 128), lambda j, owners: (0, 0)),
            still((EXTRA, width), lambda j, owners: (0, 0)),
        ],
        [sds((t + EXTRA, count * width), BF)],
        [pl.BlockSpec((t + EXTRA, width), lambda j, owners: (0, j))],
        mib=34,
        flops=6 * t * D * width,
        name="project_back",
    )[0]


def add(a, b):
    return (a.astype(F32) + b.astype(F32)).astype(BF)


class Order:
    def __init__(self):
        self.before = ()

    def __call__(self, value):
        return after(value, *self.before) if self.before else value

    def done(self, *values):
        self.before = tuple(values)


class Gather:
    def __init__(self, share):
        self.n = lax.axis_size("tensor")
        self.pieces = [share]
        self.held = {(i, i): 0 for i in range(self.n)}
        self.steps = 0

    def send(self, piece, pairs, order):
        self.pieces.append(lax.ppermute(order(self.pieces[piece]), "tensor", pairs))

    def step(self, order):
        n, s = self.n, self.steps
        self.steps += 1
        before = len(self.pieces)
        if n == 4:
            outer, inner, out = [(0, 1), (1, 0), (2, 3), (3, 2)], [(1, 2), (2, 1)], [(1, 0), (2, 3)]
            for piece, pairs in (((0, outer), (0, inner)), ((2, out), (1, inner)), ((4, out),))[s]:
                self.send(piece, pairs, order)
            owners = ((1, None, 2, None, 3), (0, 2, None, 3, None), (3, 1, None, 0, None), (2, None, 1, None, 0))
            self.held = {(i, i): 0 for i in range(n)} | {
                (i, owner): 1 + k for i, row in enumerate(owners) for k, owner in enumerate(row) if owner is not None
            }
        else:
            up, down = (0, 0) if s == 0 else (before - 2, before - 1)
            self.held.update({(i + 1, i - s): before for i in range(s, n - 1)})
            self.held.update({(i, i + 1 + s): before + 1 for i in range(n - 1 - s)})
            self.send(up, [(i, i + 1) for i in range(s, n - 1)], order)
            self.send(down, [(i + 1, i) for i in range(n - 1 - s)], order)
        return self.pieces[before:]

    def last(self, order):
        got = self.step(order)
        while self.steps < self.n - 1:
            got = self.step(order)
        return got

    def whole(self):
        share = self.pieces[0]
        t, width = share.shape
        return prefetched(
            functools.partial(assemble_body, self.held),
            [lax.axis_index("tensor")],
            (self.n,),
            self.pieces,
            [still((t, width), lambda j, me: (0, 0))] * len(self.pieces),
            [sds((t, self.n * width), share.dtype)],
            [pl.BlockSpec((t, width), lambda j, me: (0, j))],
            mib=14,
            name="assemble",
        )[0]


def scatter_order(n):
    me = lax.axis_index("tensor")
    first = jnp.where(me < n // 2, n - 1, 0)
    return [(first + k) % n for k in range(n)]


class Scatter:
    def __init__(self, first, rest):
        self.n, self.me = lax.axis_size("tensor"), lax.axis_index("tensor")
        self.first, self.rest, self.steps, self.got = first, rest, 0, {}
        self.width = first.shape[1]

    def part(self, owner, *got):
        place = (owner - jnp.where(self.me < self.n // 2, self.n - 1, 0) - 1) % self.n
        place = jnp.clip(place, 0, self.n - 2)
        value = lax.dynamic_slice_in_dim(self.rest, place * self.width, self.width, 1)
        return functools.reduce(add, got, value)

    def any(self, owner, *got):
        first = jnp.where(self.me < self.n // 2, self.n - 1, 0)
        value = jnp.where(owner % self.n == first, self.first, self.part(owner % self.n))
        return functools.reduce(add, got, value)

    def send(self, name, value, pairs, order):
        self.got[name] = lax.ppermute(order(value), "tensor", pairs)

    def step(self, order):
        n, me, s = self.n, self.me, self.steps
        self.got = got = {name: order(value) for name, value in self.got.items()}
        self.steps += 1
        if n == 4:
            inward, inner, outer = [(0, 1), (3, 2)], [(1, 2), (2, 1)], [(0, 1), (1, 0), (2, 3), (3, 2)]
            if s == 0:
                self.send("far", self.first, inward, order)
                return [got["far"]]
            if s == 1:
                self.send("far", add(self.first, got["far"]), inner, order)
                self.send("next", self.part(jnp.where(me == 0, 2, 1)), inward, order)
            else:
                self.send("far", self.part(me ^ 1, got["far"]), outer, order)
                self.send("next", self.part(3 - me, got["next"]), inner, order)
            return [got["far"], got["next"]]
        up, down = ((got["up"],), (got["down"],)) if s else ((), ())
        self.send("up", self.any(me + n - 1 - s, *up), [(i, i + 1) for i in range(s + 1)], order)
        self.send("down", self.any(me - n + 1 + s, *down), [(i + 1, i) for i in range(n - 2 - s, n - 1)], order)
        return [got["up"], got["down"]]

    def last(self, order):
        got = self.step(order)
        while self.steps < self.n - 1:
            got = self.step(order)
        return got

    def total(self):
        own = self.any(self.me) if self.n != 4 else self.part(self.me)
        return sum((g.astype(F32) for g in self.got.values()), own.astype(F32))


def assemble_body(held, me_ref, *refs):
    out_ref, owner, me = refs[-1], pl.program_id(0), me_ref[0]
    for k, ref in enumerate(refs[:-1]):
        places = [(device, o) for (device, o), at in held.items() if at == k]
        here = functools.reduce(jnp.logical_or, [(me == device) & (owner == o) for device, o in places])

        @pl.when(here)
        def _(ref=ref):
            out_ref[...] = ref[...]


def swap(value, bit, axis="dp"):
    n = lax.axis_size(axis)
    return lax.ppermute(value, axis, [(i, i ^ (1 << bit)) for i in range(n)])


def split_body(groups, bits_ref, *refs):
    parts, outs = refs[: 4 * groups], refs[4 * groups :]
    for part in range(2):
        for phase in range(2):

            @pl.when(pl.program_id(0) == phase)
            def _(part=part, phase=phase):
                at = 0
                for g in range(groups):
                    keep, got = parts[2 * (part * groups + g)], parts[2 * (part * groups + g) + 1]
                    wide = keep.shape[1]
                    outs[2 * part + phase][:, at : at + wide] = add(keep[...], got[...])
                    at += wide


def split(upper, lower, bits, joined):
    groups = len(upper)
    rows = upper[0][0].shape[0] // (4 if joined else 2)
    block = min(128, rows)
    nb = rows // block
    columns = sum(keep.shape[1] for keep, _ in upper)
    ins, in_specs = [], []
    for part, pairs in enumerate((upper, lower)):
        first = 2 * nb * part if joined else 0

        def index(phase, j, bits, part=part, first=first):
            half = jnp.where(phase == 0, 1 - bits[part], bits[part])
            return (first + half * nb + j, 0)

        for pair in pairs:
            for array in pair:
                ins.append(array)
                in_specs.append(pl.BlockSpec((block, array.shape[1]), index))
    given = pl.BlockSpec((block, columns), lambda phase, j, bits: (jnp.where(phase == 0, j, nb - 1), 0))
    kept = pl.BlockSpec((block, columns), lambda phase, j, bits: (jnp.where(phase == 0, 0, j), 0))
    return prefetched(
        functools.partial(split_body, groups),
        bits,
        (2, nb),
        ins,
        in_specs,
        [sds((rows, columns), BF)] * 4,
        [given, kept] * 2,
        mib=28,
        name="split",
    )


def merge_body(joined, bits_ref, *refs):
    for part in range(2):
        for which in range(2):

            @pl.when((pl.program_id(0) == bits_ref[part]) == (which == 0))
            def _(part=part, which=which):
                value = refs[2 * part + which][...]
                if joined:
                    refs[4][part] = value
                else:
                    refs[4 + part][...] = value


def merge(upper, lower, bits, joined):
    rows, columns = upper[0].shape
    block = min(128, rows)
    nb = rows // block

    def spec(part, which):
        def index(i, j, bits):
            half = bits[part] if which == 0 else 1 - bits[part]
            return (jnp.where(i == half, j, jnp.where(i < half, 0, nb - 1)), 0)

        return pl.BlockSpec((block, columns), index)

    if joined:
        outs = [sds((2, 2 * rows, columns), BF)]
        out_specs = [pl.BlockSpec((2, block, columns), lambda i, j, bits: (0, i * nb + j, 0))]
    else:
        outs = [sds((2 * rows, columns), BF)] * 2
        out_specs = [pl.BlockSpec((block, columns), lambda i, j, bits: (i * nb + j, 0))] * 2
    return prefetched(
        functools.partial(merge_body, joined),
        bits,
        (2, nb),
        [*upper, *lower],
        [spec(part, which) for part in range(2) for which in range(2)],
        outs,
        out_specs,
        mib=22,
        name="merge",
    )


def sum_over_dp(given, order):
    me, n = lax.axis_index("dp"), lax.axis_size("dp")
    count = n.bit_length() - 1
    bit = lambda b: (me >> b) & 1
    orders = [list(range(1, count)), list(range(count - 1, 0, -1))]
    got = [swap(g, 0) for g in given]
    kept = yield got
    upper = lower = [(order(k), g) for k, g in zip(kept, got)]
    for s in range(count - 1):
        a, b = orders[0][s], orders[1][s]
        p_give, p_keep, q_give, q_keep = split(upper, lower, [bit(a), bit(b)], s == 0)
        upper, lower = [(p_keep, swap(p_give, a))], [(q_keep, swap(q_give, b))]
        yield p_keep
        upper, lower = [(order(upper[0][0]), upper[0][1])], [(order(lower[0][0]), lower[0][1])]
    p, q = add(*upper[0]), add(*lower[0])
    for s in reversed(range(count - 1)):
        a, b = orders[0][s], orders[1][s]
        got = swap(p, a), swap(q, b)
        yield p
        out = merge([order(p), got[0]], [q, got[1]], [bit(a), bit(b)], s == 0)
        if s:
            p, q = out
    own = out[0].reshape(-1, out[0].shape[2])
    other = swap(own, 0)
    yield own
    yield own, other


def halves(core, own, other, nb):
    def index(mine):
        def of(i, bits):
            half = bits[0] if mine else 1 - bits[0]
            return (jnp.clip(i - half * nb, 0, nb - 1), 0)

        return of

    return index(True), index(False)


def mlp_out_body(units, core_ref, own_ref, other_ref, gate_up_ref, down_ref):
    half = pl.program_id(0) // (pl.num_programs(0) // 2)
    for ref, mine in ((own_ref, True), (other_ref, False)):

        @pl.when((half == core_ref[0]) == mine)
        def _(ref=ref):
            gate_up_ref[:, 0, :] = ref[:, :units].astype(F32)
            gate_up_ref[:, 1, :] = ref[:, units : 2 * units].astype(F32)
            down_ref[...] = ref[:, 2 * units :].astype(F32).T


def mlp_out(core, own, other):
    columns = own.shape[1]
    units = columns // 3
    block = 128
    nb = own.shape[0] // block
    mine, theirs = halves(core, own, other, nb)
    return prefetched(
        functools.partial(mlp_out_body, units),
        [core],
        (2 * nb,),
        [own, other],
        [pl.BlockSpec((block, columns), mine), pl.BlockSpec((block, columns), theirs)],
        [sds((D, 2, units), F32), sds((units, D), F32)],
        [pl.BlockSpec((block, 2, units), lambda i, c: (i, 0, 0)), pl.BlockSpec((units, block), lambda i, c: (0, i))],
        mib=26,
        name="mlp_out",
    )


def attention_out_body(width, core_ref, own_ref, other_ref, project_ref, output_ref):
    half = pl.program_id(0) // (pl.num_programs(0) // 2)
    for ref, mine in ((own_ref, True), (other_ref, False)):

        @pl.when((half == core_ref[0]) == mine)
        def _(ref=ref):
            for k in range(3):
                project_ref[k] = ref[:, k * width : (k + 1) * width].astype(F32)
            output_ref[...] = ref[:, 3 * width :].astype(F32).T


def attention_out(core, own, other):
    columns = own.shape[1]
    width = columns // 4
    block = 256
    nb = own.shape[0] // block
    mine, theirs = halves(core, own, other, nb)
    return prefetched(
        functools.partial(attention_out_body, width),
        [core],
        (2 * nb,),
        [own, other],
        [pl.BlockSpec((block, columns), mine), pl.BlockSpec((block, columns), theirs)],
        [sds((3, D, width), F32), sds((width, D), F32)],
        [pl.BlockSpec((3, block, width), lambda i, c: (0, i, 0)), pl.BlockSpec((width, block), lambda i, c: (0, i))],
        mib=22,
        name="attention_out",
    )


def per_device(
    tokens,
    norm_one_gain,
    norm_one_shift,
    project_weight,
    project_bias,
    output_weight,
    norm_two_gain,
    norm_two_shift,
    gate_up_weight,
    down_weight,
    cotangent,
):
    width = tokens.shape[1]
    t = tokens.shape[0] // CHUNKS
    offset = lax.axis_index("tensor") * width
    core = lax.axis_index("dp") & 1
    mine = lambda full: lax.dynamic_slice_in_dim(full, offset, width, full.ndim - 1)
    half_of = lambda array, which: lax.dynamic_slice_in_dim(array, which * (D // 2), D // 2, 1)
    order = Order()

    small = jnp.stack([norm_one_gain, norm_one_shift, norm_two_gain, norm_two_shift])
    whole_x = Gather(jnp.concatenate([tokens, jnp.pad(small, ((0, EXTRA - 4), (0, 0)))]))
    whole_up = Gather(cotangent)
    got = whole_x.step(order)
    gate_w = order(gate_up_weight)[:, 0]
    order.done(*got, gate_w)
    got = whole_x.step(order)
    up_w = order(gate_up_weight)[:, 1]
    order.done(*got, up_w)
    whole_x.last(order)
    tables = rope_tables()
    x = whole_x.whole()
    gain_one, gain_two, shift_two = (x[t + i : t + i + 1].astype(F32) for i in (0, 2, 3))
    project_w = project_weight.transpose(1, 0, 2)
    bias = project_bias.astype(F32)[:, None, :]

    through = lambda row: jnp.einsum("d,kdc->kc", row[0].astype(BF), project_w, preferred_element_type=F32)
    with_rows = jnp.stack([through(gain_one), through(x[t + 1 : t + 2]) + bias[:, 0]])

    order.done(x)
    got = whole_up.step(order)
    normed_one, stats_one, heads = project(0, x, project_w, bias, tables, ())
    order.done(*got, stats_one)
    owners = scatter_order(whole_up.n)
    first, rest, context, lse = attend(owners, order(heads), output_weight)
    order.done(lse)
    branch = Scatter(first, rest)
    for _ in range(2):
        order.done(*whole_up.step(order), *branch.step(order))
    if whole_up.n > 4:
        whole_up.last(order)
    branch.last(order)
    upstream = whole_up.whole()
    middle_share = tokens.astype(F32) + branch.total()
    middle_sent = (middle_share - stats_one[:, 0:1]).astype(BF)
    order.done(middle_sent)
    whole_middle = Gather(middle_sent)
    while whole_middle.steps < whole_middle.n - 1:
        whole_middle.step(order)
    middle = whole_middle.whole()

    normed_two, stats_two, hidden, dgate, dup = mlp(
        0, middle, upstream, gain_two, shift_two, gate_w, up_w, down_weight, ()
    )
    first = mlp_back(owners[:1], width, dgate, dup, gate_w, up_w)
    rest = mlp_back(owners[1:], width, after(dgate, first), dup, gate_w, up_w)
    order.done(first)
    delta_two = Scatter(first, rest)
    got = delta_two.step(order)
    order.done(rest)
    mlp_half = lambda which: [
        dot(half_of(normed_two, which), order(jnp.concatenate([dgate, dup], axis=1)), TN).astype(BF),
        dot(half_of(upstream, which), order(hidden), TN).astype(BF),
    ]
    mlp_given = mlp_half(1 - core)
    mlp_sum = sum_over_dp(mlp_given, order)
    next(mlp_sum)
    order.done(*got, *mlp_given)
    got = delta_two.step(order)
    mlp_kept = mlp_half(core)
    order.done(*mlp_kept)
    held = mlp_sum.send(mlp_kept)
    order.done(*got, held)
    got = delta_two.last(order)
    mlp_parts = dot(order(hidden), down_weight).astype(BF)
    order.done(*got, mlp_parts)
    delta_two = order(delta_two.total())
    unit_two = (mine(middle).astype(F32) - stats_two[:, 0:1]) * stats_two[:, 1:2]
    two_grads = [jnp.sum(delta_two * unit_two, axis=0), jnp.sum(delta_two, axis=0)]
    e_own = delta_two * norm_two_gain.astype(F32)
    e_sent = e_own.astype(BF)
    order.done(e_sent)
    whole_e = Gather(e_sent)
    got = whole_e.step(order)
    held = next(mlp_sum)
    piece = lambda owner: lax.dynamic_slice_in_dim(mlp_parts, owner * width, width, 1)
    mlp_share = Scatter(piece(owners[0]), jnp.concatenate([piece(owner) for owner in owners[1:]], axis=1))
    order.done(*got, held, mlp_share.rest)
    got = whole_e.step(order) + mlp_share.step(order)
    order.done(*got)
    got = whole_e.last(order) + mlp_share.step(order)
    held = next(mlp_sum)
    e = whole_e.whole()

    order.done(e, held, *got)
    mlp_share.last(order)
    means_two, dbranch, dctx = branch_back(order(e), middle, stats_two, upstream, output_weight)
    order.done(dctx)
    dq, dk, dv, sums = attend_back(heads, lse, context, order(dctx), tables, with_rows)
    order.done(dq)
    mlp_share.got = {name: order(value) for name, value in mlp_share.got.items()}
    result = (middle_share + mlp_share.total()).astype(BF)
    held = next(mlp_sum)
    order.done(held, result)
    delta_heads = (dq, dk, dv)
    attention_half = lambda which: [
        dot(half_of(normed_one, which), order(jnp.concatenate(delta_heads, axis=1)), TN).astype(BF),
        dot(half_of(dbranch, which), order(context), TN).astype(BF),
    ]
    attention_given = attention_half(1 - core)
    attention_sum = sum_over_dp(attention_given, order)
    next(attention_sum)
    sum_rows = 2 * t // width
    below = jnp.pad(sums[:2].reshape(sum_rows, width), ((2, EXTRA - 2 - sum_rows), (0, 0)))
    order.done(*attention_given, below)
    back = lambda owners, dq: project_back(owners, dq, dk, dv, project_w, x, stats_one, below)
    first = back(owners[:1], order(dq))
    rest = back(owners[1:], after(dq, first))
    order.done(first)
    delta_one = Scatter(first, rest)
    got = delta_one.step(order)
    order.done(rest)
    attention_kept = attention_half(core)
    order.done(*attention_kept)
    held = attention_sum.send(attention_kept)
    order.done(held, *got)
    got = delta_one.step(order)
    held = next(mlp_sum)
    order.done(held)
    if lax.axis_size("dp") > 8:
        for _ in range(2):
            order.done(next(mlp_sum))
            order.done(next(attention_sum))
    held = next(attention_sum)
    order.done(held, *got)
    got = delta_one.last(order)
    held = next(attention_sum)
    order.done(held, *got)
    mlp_halves = next(mlp_sum)
    gate_up_grad, down_grad = mlp_out(core, order(mlp_halves[0]), mlp_halves[1])
    order.done(down_grad)
    delta_one = order(delta_one.total())
    bias_grad = [jnp.sum(a, axis=0, dtype=F32) for a in delta_heads]
    small = jnp.stack([delta_one[t], delta_one[t + 1], *two_grads, *bias_grad])
    devices = lax.axis_size("dp")
    others = [lax.ppermute(order(small), "dp", [(i, i ^ k) for i in range(devices)]) for k in range(1, devices)]
    held = next(attention_sum)
    order.done(held)
    sums = (delta_one[t + 2 : t + 2 + sum_rows] / D).reshape(2, t).T
    unit_one = (tokens.astype(F32) - stats_one[:, 0:1]) * stats_one[:, 1:2]
    dmid = cotangent.astype(F32) + stats_two[:, 1:2] * (e_own - means_two[:, 0:1] - unit_two * means_two[:, 1:2])
    tokens_grad = order(dmid) + stats_one[:, 1:2] * (
        delta_one[:t] * norm_one_gain.astype(F32) - sums[:, 0:1] - unit_one * sums[:, 1:2]
    )
    order.done(tokens_grad)
    small = sum((order(other) for other in others), small)
    order.done(small)
    held = next(attention_sum)
    order.done(held)
    attention_halves = next(attention_sum)
    project_grad, output_grad = attention_out(core, order(attention_halves[0]), attention_halves[1])
    return (
        result,
        tokens_grad,
        small[0],
        small[1],
        project_grad.transpose(1, 0, 2),
        small[4:7],
        output_grad,
        small[2],
        small[3],
        gate_up_grad,
        down_grad,
    )


def solution(mesh):
    return jax.shard_map(
        per_device,
        mesh=mesh,
        in_specs=(
            P("dp", "tensor"),
            P("tensor"),
            P("tensor"),
            P(None, None, "tensor"),
            P(None, "tensor"),
            P("tensor", None),
            P("tensor"),
            P("tensor"),
            P(None, None, "tensor"),
            P("tensor", None),
            P("dp", "tensor"),
        ),
        out_specs=(
            P("dp", "tensor"),
            P("dp", "tensor"),
            P("tensor"),
            P("tensor"),
            P(None, None, "tensor"),
            P(None, "tensor"),
            P("tensor", None),
            P("tensor"),
            P("tensor"),
            P(None, None, "tensor"),
            P("tensor", None),
        ),
        check_vma=False,
    )
```

time: 1760 us -> 785 us (0.45)
  waiting for transfers between devices: 1290 us -> 294 us
  Pallas kernels: 0 us -> 194 us
  matrix products: 192 us -> 53.6 us
  starting transfers between devices: 0.32 us -> 117 us
  blocking collectives: 100 us -> 0 us
  other arithmetic: 60.6 us -> 40.2 us
    psum x2 -> x0, waiting for transfers between devices: 816 us -> none  [the longest x1 554 us: per_device(): lax.psum((norm_one_gain_grad, norm_one_shift_grad, project_weight_grad, p...]
    reduce_scatter x3 -> x0, waiting for transfers between devices: 303 us -> none  [the longest x1 143 us: per_device(): lax.psum_scatter(delta_normed_one, 'tensor', scatter_dimension=1, tiled=T...]
    ppermute x0 -> x69, waiting for transfers between devices: none -> 294 us  [the longest x20 148 us: send(): self.pieces.append(lax.ppermute(order(self.pieces[piece]), 'tensor', pairs))]
    pallas_call x0 -> x23, Pallas kernels: none -> 194 us  [the longest x19 118 us: prefetched(): pl.pallas_call(body, grid_spec=pltpu.PrefetchScalarGridSpec(num_scalar_pr...]
    all_gather x3 -> x0, waiting for transfers between devices: 172 us -> none  [the longest x1 67.4 us: per_device(): lax.all_gather(delta_middle_share.astype(jnp.bfloat16), 'tensor', axis=1,...]
    dot_general x24 -> x11, matrix products: 192 us -> 53.6 us  [the longest x9 50.3 us: dot(): return lax.dot_general(a, b, dims, preferred_element_type=F32)]
    ppermute x0 -> x69, starting transfers between devices: none -> 117 us  [the longest x20 61.2 us: send(): self.got[name] = lax.ppermute(order(value), 'tensor', pairs)]
    all_gather x4 -> x0, blocking collectives: 52.1 us -> none  [the longest x1 14.4 us: per_device(): lax.all_gather(norm_two_gain, 'tensor', axis=0, tiled=True)]
  transfers between devices with their start and end apart: 8 -> 69, of which waited for: 8 -> 28; matrix products, arithmetic and copies ran while one was open for 10% -> 12% of each run, Pallas kernels for 0% -> 14%
where the time goes in v1:
time: 785 us; the launch traced here: 778 us
  waiting for transfers between devices  294 us (37%)
  Pallas kernels  194 us (25%)
  starting transfers between devices  117 us (15%)
  local copies, waits for them, and re-layouts  76.9 us (10%)
  matrix products  53.6 us (7%)
  other arithmetic  40.2 us (5%)
    ppermute x20, waiting for transfers between devices, send(): self.pieces.append(lax.ppermute(order(self.pieces[piece]), 'tensor', pairs))  148 us
    pallas_call x19, Pallas kernels, prefetched(): pl.pallas_call(body, grid_spec=pltpu.PrefetchScalarGridSpec(num_scalar_pr...  118 us
    pallas_call x4, Pallas kernels, kernel_call(): pl.pallas_call(run, grid=grid, in_specs=list(in_specs) + [ANY] * len(prev...  75.7 us
    ppermute x20, waiting for transfers between devices, send(): self.got[name] = lax.ppermute(order(value), 'tensor', pairs)  69 us
    ppermute x20, starting transfers between devices, send(): self.got[name] = lax.ppermute(order(value), 'tensor', pairs)  61.2 us
    ppermute x22, waiting for transfers between devices, swap(): return lax.ppermute(value, axis, [(i, i ^ 1 << bit) for i in range(n)])  56.6 us
    unnamed x174, local copies, waits for them, and re-layouts  50.3 us
    dot_general x9, matrix products, dot(): return lax.dot_general(a, b, dims, preferred_element_type=F32)  50.3 us
  transfers between devices with their start and end apart: 69, of which 28 were waited for; matrix products, arithmetic and copies ran while one was open for 12% of the time, Pallas kernels for 14%

profile of v1, /device:TPU:0, one launch (start us, length us, event | category | flops | bytes accessed | tf_op | source)
XLA Modules:
  0.0 777.7 jit_solution(18351552190963915903)
XLA Ops:
  19.0 15.5 %collective-permute-done.refs_1_ = bf16[1040,512]{1,0:T(8,128)(2,1)S(1)} collective-permute-done((bf16[1040,512]{1,0:T(8,128)(2,1)S(1)}, bf16[1040,512]{1,0:T(8,128)(2,1)S(1)}, u32[]{:S(2)}, u32[]{:S(2)}) %collective-permute-start) | collective-permute-done | bytes 1064992 | tf_op jit(solution)/shard_map/ppermute | solution.py:500
  47.9 12.8 %collective-permute-done.2.refs_3_ = bf16[1040,512]{1,0:T(8,128)(2,1)S(1)} collective-permute-done((bf16[1040,512]{1,0:T(8,128)(2,1)S(1)}, bf16[1040,512]{1,0:T(8,128)(2,1)S(1)}, u32[]{:S(2)}, u32[]{:S(2)}) %collective-permute-start.2) | collective-permute-done | bytes 1064992 | tf_op jit(solution)/shard_map/ppermute | solution.py:500
  63.1 24.5 %collective-permute-done.4.refs_5_ = bf16[1040,512]{1,0:T(8,128)(2,1)} collective-permute-done((bf16[1040,512]{1,0:T(8,128)(2,1)}, bf16[1040,512]{1,0:T(8,128)(2,1)}, u32[]{:S(2)}, u32[]{:S(2)}) %collective-permute-start.4) | collective-permute-done | bytes 1064992 | tf_op jit(solution)/shard_map/ppermute | solution.py:500
  102.4 14.2 %project.1 = (bf16[1024,2048]{1,0:T(8,128)(2,1)S(1)}, f32[1024,128]{1,0:T(8,128)S(1)}, bf16[3,1024,512]{2,1,0:T(8,128)(2,1)S(1)}) custom-call(bf16[1040,2048]{1,0:T(8,128)(2,1)S(1)} %copy-done.3, bf16[1040,2048]{1,0:T(8,128)(2,1)S(1)} %copy-done.3, bf16[3,2048,512]{2,1,0:T(8,128)(2,1)S(1)} %bitcast.57, f32[3,1,512]{2,1,0:T(1,128)S(1)} %copy.27.refs_3_, ...), custom_call_target="tpu_custom_call" | custom-call | flops 100663296 | bytes 378976 | tf_op jit(solution)/shard_map/project/pallas_call | solution.py:54
  118.7 17.8 %attend.1 = (bf16[1024,512]{1,0:T(8,128)(2,1)}, bf16[1024,1536]{1,0:T(8,128)(2,1)S(1)}, bf16[1024,512]{1,0:T(8,128)(2,1)S(1)}, f32[1024,512]{1,0:T(8,128)S(1)}) custom-call(s32[4]{0:T(128)S(1)} %pad_add_fusion.owners_ref, bf16[3,1024,512]{2,1,0:T(8,128)(2,1)S(1)} %get-tuple-element.154.q_ref.k_ref.v_ref.refs_0_.refs_1_.refs_2_, ...), custom_call_target="tpu_custom_call" | custom-call | flops 25769803776 | bytes 294912 | tf_op jit(solution)/shard_map/attend/pallas_call | solution.py:78
  150.1 12.3 %collective-permute-done.8.refs_3_ = bf16[1024,512]{1,0:T(8,128)(2,1)} collective-permute-done((bf16[1024,512]{1,0:T(8,128)(2,1)}, bf16[1024,512]{1,0:T(8,128)(2,1)}, u32[]{:S(2)}, u32[]{:S(2)}) %collective-permute-start.8) | collective-permute-done | bytes 1048608 | tf_op jit(solution)/shard_map/ppermute | solution.py:500
  180.5 14.2 %collective-permute-done.11.refs_5_ = bf16[1024,512]{1,0:T(8,128)(2,1)} collective-permute-done((bf16[1024,512]{1,0:T(8,128)(2,1)}, bf16[1024,512]{1,0:T(8,128)(2,1)}, u32[]{:S(2)}, u32[]{:S(2)}) %collective-permute-start.11) | collective-permute-done | bytes 1048608 | tf_op jit(solution)/shard_map/ppermute | solution.py:500
  207.5 16.7 %collective-permute-done.13 = bf16[1024,512]{1,0:T(8,128)(2,1)} collective-permute-done((bf16[1024,512]{1,0:T(8,128)(2,1)}, bf16[1024,512]{1,0:T(8,128)(2,1)}, u32[]{:S(2)}, u32[]{:S(2)}) %collective-permute-start.13) | collective-permute-done | bytes 1048608 | tf_op jit(solution)/shard_map/ppermute | solution.py:568
  230.3 15.4 %collective-permute-done.15.refs_1_ = bf16[1024,512]{1,0:T(8,128)(2,1)S(1)} collective-permute-done((bf16[1024,512]{1,0:T(8,128)(2,1)S(1)}, bf16[1024,512]{1,0:T(8,128)(2,1)S(1)}, u32[]{:S(2)}, u32[]{:S(2)}) %collective-permute-start.15) | collective-permute-done | bytes 1048608 | tf_op jit(solution)/shard_map/ppermute | solution.py:500
  256.9 12.0 %collective-permute-done.17.refs_3_ = bf16[1024,512]{1,0:T(8,128)(2,1)} collective-permute-done((bf16[1024,512]{1,0:T(8,128)(2,1)S(1)}, bf16[1024,512]{1,0:T(8,128)(2,1)}, u32[]{:S(2)}, u32[]{:S(2)}) %collective-permute-start.17) | collective-permute-done | bytes 1048608 | tf_op jit(solution)/shard_map/ppermute | solution.py:500
  268.9 20.6 %collective-permute-done.19.refs_5_ = bf16[1024,512]{1,0:T(8,128)(2,1)} collective-permute-done((bf16[1024,512]{1,0:T(8,128)(2,1)S(1)}, bf16[1024,512]{1,0:T(8,128)(2,1)}, u32[]{:S(2)}, u32[]{:S(2)}) %collective-permute-start.19) | collective-permute-done | bytes 1048608 | tf_op jit(solution)/shard_map/ppermute | solution.py:500
  294.0 32.3 %mlp.1 = (bf16[1024,2048]{1,0:T(8,128)(2,1)}, f32[1024,128]{1,0:T(8,128)S(1)}, bf16[1024,1408]{1,0:T(8,128)(2,1)S(1)}, bf16[1024,1408]{1,0:T(8,128)(2,1)S(1)}, bf16[1024,1408]{1,0:T(8,128)(2,1)}) custom-call(bf16[1024,2048]{1,0:T(8,128)(2,1)} %copy-done.5, bf16[1024,2048]{1,0:T(8,128)(2,1)} %copy-done.7, f32[1,2048]{1,0:T(1,128)S(1)} %get-tuple-element.293.refs_2_, ...), custom_call_target="tpu_custom_call" | custom-call | flops 276824064 | bytes 610560 | tf_op jit(solution)/shard_map/mlp/pallas_call | solution.py:54
  333.3 11.1 %mlp_back.3 = bf16[1024,1536]{1,0:T(8,128)(2,1)S(1)} custom-call(s32[3]{0:T(128)S(1)} %pad_add_fusion.1.owners_ref, bf16[1024,1408]{1,0:T(8,128)(2,1)S(1)} %get-tuple-element.178.dgate_ref, bf16[1024,1408]{1,0:T(8,128)(2,1)S(1)} %copy-done.10, bf16[2048,1408]{1,0:T(8,128)(2,1)S(1)} %bitcast.66, bf16[2048,1408]{1,0:T(8,128)(2,1)S(1)} %bitcast.68), custom_call_target="tpu_custom_call" | custom-call | flops 184549376 | bytes 319488 | tf_op jit(solution)/shard_map/mlp_back/pallas_call | solution.py:78
  364.7 14.6 %collective-permute-done.20 = bf16[1024,512]{1,0:T(8,128)(2,1)} collective-permute-done((bf16[1024,512]{1,0:T(8,128)(2,1)S(1)}, bf16[1024,512]{1,0:T(8,128)(2,1)}, u32[]{:S(2)}, u32[]{:S(2)}) %collective-permute-start.20) | collective-permute-done | bytes 1048608 | tf_op jit(solution)/shard_map/ppermute | solution.py:568
  422.4 11.1 %convolution_convert_fusion.2 = bf16[1024,2048]{1,0:T(8,128)(2,1)} fusion(bf16[1024,1408]{1,0:T(8,128)(2,1)S(1)} %copy-done.58, bf16[1408,2048]{1,0:T(8,128)(2,1)} %refs_6_.1), kind=kOutput, calls=%fused_computation.4 | convolution fusion | flops 5907677184 | bytes 12845056 | tf_op jit(solution)/shard_map/dot_general | solution.py:30
  451.0 15.7 %collective-permute-done.29.refs_1_ = bf16[256,4224]{1,0:T(8,128)(2,1)} collective-permute-done((bf16[256,4224]{1,0:T(8,128)(2,1)}, bf16[256,4224]{1,0:T(8,128)(2,1)}, u32[]{:S(2)}, u32[]{:S(2)}) %collective-permute-start.29) | collective-permute-done | bytes 2162720 | tf_op jit(solution)/shard_map/ppermute | solution.py:615
  481.3 12.0 %collective-permute-done.31 = bf16[1024,512]{1,0:T(8,128)(2,1)S(1)} collective-permute-done((bf16[1024,512]{1,0:T(8,128)(2,1)S(1)}, bf16[1024,512]{1,0:T(8,128)(2,1)S(1)}, u32[]{:S(2)}, u32[]{:S(2)}) %collective-permute-start.31) | collective-permute-done | bytes 1048608 | tf_op jit(solution)/shard_map/ppermute | solution.py:568
  511.2 13.9 %collective-permute-done.35.refs_5_ = bf16[1024,512]{1,0:T(8,128)(2,1)S(1)} collective-permute-done((bf16[1024,512]{1,0:T(8,128)(2,1)S(1)}, bf16[1024,512]{1,0:T(8,128)(2,1)S(1)}, u32[]{:S(2)}, u32[]{:S(2)}) %collective-permute-start.35) | collective-permute-done | bytes 1048608 | tf_op jit(solution)/shard_map/ppermute | solution.py:500
  541.9 21.4 %attend_back.1 = (bf16[1024,512]{1,0:T(8,128)(2,1)S(1)}, bf16[1024,512]{1,0:T(8,128)(2,1)S(1)}, bf16[1024,512]{1,0:T(8,128)(2,1)S(1)}, f32[8,1024]{1,0:T(8,128)S(1)}) custom-call(bf16[3,1024,512]{2,1,0:T(8,128)(2,1)S(1)} %copy-done.56, bf16[3,1024,512]{2,1,0:T(8,128)(2,1)S(1)} %copy-done.56, bf16[3,1024,512]{2,1,0:T(8,128)(2,1)S(1)} %copy-done.56, ...), custom_call_target="tpu_custom_call" | custom-call | flops 42949672960 | bytes 287424 | tf_op jit(solution)/shard_map/attend_back/pallas_call | solution.py:54
  617.1 8.5 %collective-permute-done.47.refs_3_ = bf16[256,4224]{1,0:T(8,128)(2,1)} collective-permute-done((bf16[256,4224]{1,0:T(8,128)(2,1)}, bf16[256,4224]{1,0:T(8,128)(2,1)}, u32[]{:S(2)}, u32[]{:S(2)}) %collective-permute-start.47) | collective-permute-done | bytes 2162720 | tf_op jit(solution)/shard_map/ppermute | solution.py:615
  652.5 16.6 %collective-permute-done.48.refs_1_ = bf16[256,2048]{1,0:T(8,128)(2,1)} collective-permute-done((bf16[256,2048]{1,0:T(8,128)(2,1)}, bf16[256,2048]{1,0:T(8,128)(2,1)}, u32[]{:S(2)}, u32[]{:S(2)}) %collective-permute-start.48) | collective-permute-done | bytes 1048608 | tf_op jit(solution)/shard_map/ppermute | solution.py:615
  688.2 11.5 %collective-permute-done.53 = bf16[1040,512]{1,0:T(8,128)(2,1)S(1)} collective-permute-done((bf16[1040,512]{1,0:T(8,128)(2,1)S(1)}, bf16[1040,512]{1,0:T(8,128)(2,1)S(1)}, u32[]{:S(2)}, u32[]{:S(2)}) %collective-permute-start.53) | collective-permute-done | bytes 1064992 | tf_op jit(solution)/shard_map/ppermute | solution.py:568
  700.1 24.0 %mlp_out.1 = (f32[2048,2,1408]{2,1,0:T(2,128)}, f32[1408,2048]{1,0:T(8,128)}) custom-call(s32[1]{0:T(128)} %bitcast.15.core_ref, bf16[1024,4224]{1,0:T(8,128)(2,1)} %bitcast.14.own_ref, bf16[1024,4224]{1,0:T(8,128)(2,1)} %collective-permute-done.55.other_ref), custom_call_target="tpu_custom_call" | custom-call | bytes 811008 | tf_op jit(solution)/shard_map/mlp_out/pallas_call | solution.py:78
  733.4 20.8 %collective-permute-done.64 = f32[7,512]{1,0:T(8,128)S(1)} collective-permute-done((f32[7,512]{1,0:T(8,128)S(1)}, f32[7,512]{1,0:T(8,128)S(1)}, u32[]{:S(2)}, u32[]{:S(2)}) %collective-permute-start.64) | collective-permute-done | bytes 14368 | tf_op jit(solution)/shard_map/ppermute | solution.py:965
  (394 shorter events, 385.6 us)
Async XLA Ops:
  5.4 29.1 %collective-permute-start = (bf16[1040,512]{1,0:T(8,128)(2,1)S(1)}, bf16[1040,512]{1,0:T(8,128)(2,1)S(1)}, u32[]{:S(2)}, u32[]{:S(2)}) collective-permute-start(bf16[1040,512]{1,0:T(8,128)(2,1)S(1)} %pad_maximum_fusion.2.refs_0_), channel_id=1, source_target_pairs={{0,1},{1,0},{2,3},{3,2},{4,5},{5,4},{6,7},{7,6},{8,9},{9,8},{10,11... | collective-permute-start | bytes 3194888 | tf_op jit(solution)/shard_map/ppermute | solution.py:500
  247.8 41.6 %collective-permute-start.19 = (bf16[1024,512]{1,0:T(8,128)(2,1)S(1)}, bf16[1024,512]{1,0:T(8,128)(2,1)}, u32[]{:S(2)}, u32[]{:S(2)}) collective-permute-start(bf16[1024,512]{1,0:T(8,128)(2,1)S(1)} %collective-permute-done.18.refs_4_), channel_id=1, source_target_pairs={{1,0},{2,3},{5,4},{6,7},{9,8},{10,11},{13,12},{14,15},{17,16},{18,... | collective-permute-start | bytes 3145736 | tf_op jit(solution)/shard_map/ppermute | solution.py:500
  354.6 48.6 %collective-permute-start.23 = (bf16[1024,2816]{1,0:T(8,128)(2,1)}, bf16[1024,2816]{1,0:T(8,128)(2,1)}, u32[]{:S(2)}, u32[]{:S(2)}) collective-permute-start(bf16[1024,2816]{1,0:T(8,128)(2,1)} %convolution_convert_fusion.1), channel_id=1, source_target_pairs={{0,4},{4,0},{8,12},{12,8},{16,20},{20,16},{24,28},{28,24},{1,5},{5... | collective-permute-start | bytes 17301512 | tf_op jit(solution)/shard_map/ppermute | solution.py:615
  363.1 38.5 %collective-permute-start.24 = (bf16[1024,1408]{1,0:T(8,128)(2,1)S(1)}, bf16[1024,1408]{1,0:T(8,128)(2,1)S(1)}, u32[]{:S(2)}, u32[]{:S(2)}) collective-permute-start(bf16[1024,1408]{1,0:T(8,128)(2,1)S(1)} %convolution_convert_fusion.6), channel_id=1, source_target_pairs={{0,4},{4,0},{8,12},{12,8},{16,20},{20,16},{24,28},{28,24},{1,5},{5... | collective-permute-start | bytes 8650760 | tf_op jit(solution)/shard_map/ppermute | solution.py:615
  381.7 30.4 %collective-permute-start.21 = (bf16[1024,512]{1,0:T(8,128)(2,1)}, bf16[1024,512]{1,0:T(8,128)(2,1)S(1)}, u32[]{:S(2)}, u32[]{:S(2)}) collective-permute-start(bf16[1024,512]{1,0:T(8,128)(2,1)} %add_convert_fusion.11), channel_id=1, source_target_pairs={{1,2},{2,1},{5,6},{6,5},{9,10},{10,9},{13,14},{14,13},{17,18},{18,... | collective-permute-start | bytes 3145736 | tf_op jit(solution)/shard_map/ppermute | solution.py:568
  382.6 29.9 %collective-permute-start.22 = (bf16[1024,512]{1,0:T(8,128)(2,1)}, bf16[1024,512]{1,0:T(8,128)(2,1)}, u32[]{:S(2)}, u32[]{:S(2)}) collective-permute-start(bf16[1024,512]{1,0:T(8,128)(2,1)} %constant_dynamic-slice_fusion.6), channel_id=1, source_target_pairs={{0,1},{3,2},{4,5},{7,6},{8,9},{11,10},{12,13},{15,14},{16,17},{19,... | collective-permute-start | bytes 3145736 | tf_op jit(solution)/shard_map/ppermute | solution.py:568
  419.4 47.4 %collective-permute-start.29 = (bf16[256,4224]{1,0:T(8,128)(2,1)}, bf16[256,4224]{1,0:T(8,128)(2,1)}, u32[]{:S(2)}, u32[]{:S(2)}) collective-permute-start(bf16[256,4224]{1,0:T(8,128)(2,1)} %get-tuple-element.197), channel_id=1, source_target_pairs={{0,8},{4,12},{8,0},{12,4},{16,24},{20,28},{24,16},{28,20},{1,9},{5... | collective-permute-start | bytes 6488072 | tf_op jit(solution)/shard_map/ppermute | solution.py:615
  420.9 47.1 %collective-permute-start.30 = (bf16[256,4224]{1,0:T(8,128)(2,1)}, bf16[256,4224]{1,0:T(8,128)(2,1)}, u32[]{:S(2)}, u32[]{:S(2)}) collective-permute-start(bf16[256,4224]{1,0:T(8,128)(2,1)} %get-tuple-element.200), channel_id=1, source_target_pairs={{0,16},{4,20},{8,24},{12,28},{16,0},{20,4},{24,8},{28,12},{1,17},{... | collective-permute-start | bytes 6488072 | tf_op jit(solution)/shard_map/ppermute | solution.py:615
  442.8 28.5 %collective-permute-start.28 = (bf16[1024,512]{1,0:T(8,128)(2,1)S(1)}, bf16[1024,512]{1,0:T(8,128)(2,1)}, u32[]{:S(2)}, u32[]{:S(2)}) collective-permute-start(bf16[1024,512]{1,0:T(8,128)(2,1)S(1)} %multiply_convert_fusion.refs_0_), channel_id=1, source_target_pairs={{1,2},{2,1},{5,6},{6,5},{9,10},{10,9},{13,14},{14,13},{17,18},{18,... | collective-permute-start | bytes 3145736 | tf_op jit(solution)/shard_map/ppermute | solution.py:500
  477.3 31.1 %collective-permute-start.36 = (bf16[128,4224]{1,0:T(8,128)(2,1)S(1)}, bf16[128,4224]{1,0:T(8,128)(2,1)S(1)}, u32[]{:S(2)}, u32[]{:S(2)}) collective-permute-start(bf16[128,4224]{1,0:T(8,128)(2,1)S(1)} %get-tuple-element.209), channel_id=1, source_target_pairs={{0,16},{4,20},{8,24},{12,28},{16,0},{20,4},{24,8},{28,12},{1,17},{... | collective-permute-start | bytes 3244040 | tf_op jit(solution)/shard_map/ppermute | solution.py:615
  480.7 29.6 %collective-permute-start.41 = (bf16[128,4224]{1,0:T(8,128)(2,1)S(1)}, bf16[128,4224]{1,0:T(8,128)(2,1)S(1)}, u32[]{:S(2)}, u32[]{:S(2)}) collective-permute-start(bf16[128,4224]{1,0:T(8,128)(2,1)S(1)} %get-tuple-element.229), channel_id=1, source_target_pairs={{0,8},{4,12},{8,0},{12,4},{16,24},{20,28},{24,16},{28,20},{1,9},{5... | collective-permute-start | bytes 3244040 | tf_op jit(solution)/shard_map/ppermute | solution.py:615
  498.0 29.7 %collective-permute-start.34 = (bf16[1024,512]{1,0:T(8,128)(2,1)S(1)}, bf16[1024,512]{1,0:T(8,128)(2,1)S(1)}, u32[]{:S(2)}, u32[]{:S(2)}) collective-permute-start(bf16[1024,512]{1,0:T(8,128)(2,1)S(1)} %add_convert_fusion.8), channel_id=1, source_target_pairs={{1,2},{2,1},{5,6},{6,5},{9,10},{10,9},{13,14},{14,13},{17,18},{18,... | collective-permute-start | bytes 3145736 | tf_op jit(solution)/shard_map/ppermute | solution.py:568
  508.7 54.9 %collective-permute-start.40 = (bf16[128,4224]{1,0:T(8,128)(2,1)S(1)}, bf16[128,4224]{1,0:T(8,128)(2,1)S(1)}, u32[]{:S(2)}, u32[]{:S(2)}) collective-permute-start(bf16[128,4224]{1,0:T(8,128)(2,1)S(1)} %add_convert_fusion.1.refs_0_), channel_id=1, source_target_pairs={{0,16},{4,20},{8,24},{12,28},{16,0},{20,4},{24,8},{28,12},{1,17},{... | collective-permute-start | bytes 3244040 | tf_op jit(solution)/shard_map/ppermute | solution.py:615
  510.6 53.1 %collective-permute-start.42 = (bf16[128,4224]{1,0:T(8,128)(2,1)S(1)}, bf16[128,4224]{1,0:T(8,128)(2,1)S(1)}, u32[]{:S(2)}, u32[]{:S(2)}) collective-permute-start(bf16[128,4224]{1,0:T(8,128)(2,1)S(1)} %add_convert_fusion.refs_2_), channel_id=1, source_target_pairs={{0,8},{4,12},{8,0},{12,4},{16,24},{20,28},{24,16},{28,20},{1,9},{5... | collective-permute-start | bytes 3244040 | tf_op jit(solution)/shard_map/ppermute | solution.py:615
  575.9 33.9 %collective-permute-start.43 = (bf16[1024,1536]{1,0:T(8,128)(2,1)}, bf16[1024,1536]{1,0:T(8,128)(2,1)}, u32[]{:S(2)}, u32[]{:S(2)}) collective-permute-start(bf16[1024,1536]{1,0:T(8,128)(2,1)} %convolution_convert_fusion.4), channel_id=1, source_target_pairs={{0,4},{4,0},{8,12},{12,8},{16,20},{20,16},{24,28},{28,24},{1,5},{5... | collective-permute-start | bytes 9437192 | tf_op jit(solution)/shard_map/ppermute | solution.py:615
  575.9 49.8 %collective-permute-start.47 = (bf16[256,4224]{1,0:T(8,128)(2,1)}, bf16[256,4224]{1,0:T(8,128)(2,1)}, u32[]{:S(2)}, u32[]{:S(2)}) collective-permute-start(bf16[256,4224]{1,0:T(8,128)(2,1)} %get-tuple-element.244.refs_2_), channel_id=1, source_target_pairs={{0,16},{4,20},{8,24},{12,28},{16,0},{20,4},{24,8},{28,12},{1,17},{... | collective-permute-start | bytes 6488072 | tf_op jit(solution)/shard_map/ppermute | solution.py:615
  577.4 49.5 %collective-permute-start.46 = (bf16[256,4224]{1,0:T(8,128)(2,1)}, bf16[256,4224]{1,0:T(8,128)(2,1)}, u32[]{:S(2)}, u32[]{:S(2)}) collective-permute-start(bf16[256,4224]{1,0:T(8,128)(2,1)} %get-tuple-element.243.refs_0_), channel_id=1, source_target_pairs={{0,8},{4,12},{8,0},{12,4},{16,24},{20,28},{24,16},{28,20},{1,9},{5... | collective-permute-start | bytes 6488072 | tf_op jit(solution)/shard_map/ppermute | solution.py:615
  635.1 65.1 %collective-permute-start.55 = (bf16[1024,4224]{1,0:T(8,128)(2,1)}, bf16[1024,4224]{1,0:T(8,128)(2,1)}, u32[]{:S(2)}, u32[]{:S(2)}) collective-permute-start(bf16[1024,4224]{1,0:T(8,128)(2,1)} %bitcast.14.own_ref), channel_id=1, source_target_pairs={{0,4},{4,0},{8,12},{12,8},{16,20},{20,16},{24,28},{28,24},{1,5},{5... | collective-permute-start | bytes 25952264 | tf_op jit(solution)/shard_map/ppermute | solution.py:615
  637.4 36.3 %collective-permute-start.50 = (bf16[1040,512]{1,0:T(8,128)(2,1)}, bf16[1040,512]{1,0:T(8,128)(2,1)}, u32[]{:S(2)}, u32[]{:S(2)}) collective-permute-start(bf16[1040,512]{1,0:T(8,128)(2,1)} %add_convert_fusion.4), channel_id=1, source_target_pairs={{1,2},{2,1},{5,6},{6,5},{9,10},{10,9},{13,14},{14,13},{17,18},{18,... | collective-permute-start | bytes 3194888 | tf_op jit(solution)/shard_map/ppermute | solution.py:568
  639.1 34.7 %collective-permute-start.51 = (bf16[1040,512]{1,0:T(8,128)(2,1)}, bf16[1040,512]{1,0:T(8,128)(2,1)}, u32[]{:S(2)}, u32[]{:S(2)}) collective-permute-start(bf16[1040,512]{1,0:T(8,128)(2,1)} %constant_dynamic-slice_fusion), channel_id=1, source_target_pairs={{0,1},{3,2},{4,5},{7,6},{8,9},{11,10},{12,13},{15,14},{16,17},{19,... | collective-permute-start | bytes 3194888 | tf_op jit(solution)/shard_map/ppermute | solution.py:568
  685.4 39.0 %collective-permute-start.56 = (bf16[128,2048]{1,0:T(8,128)(2,1)}, bf16[128,2048]{1,0:T(8,128)(2,1)}, u32[]{:S(2)}, u32[]{:S(2)}) collective-permute-start(bf16[128,2048]{1,0:T(8,128)(2,1)} %add_convert_fusion.16.refs_0_), channel_id=1, source_target_pairs={{0,16},{4,20},{8,24},{12,28},{16,0},{20,4},{24,8},{28,12},{1,17},{... | collective-permute-start | bytes 1572872 | tf_op jit(solution)/shard_map/ppermute | solution.py:615
  686.8 37.5 %collective-permute-start.58 = (bf16[128,2048]{1,0:T(8,128)(2,1)}, bf16[128,2048]{1,0:T(8,128)(2,1)}, u32[]{:S(2)}, u32[]{:S(2)}) collective-permute-start(bf16[128,2048]{1,0:T(8,128)(2,1)} %add_convert_fusion.15.refs_2_), channel_id=1, source_target_pairs={{0,8},{4,12},{8,0},{12,4},{16,24},{20,28},{24,16},{28,20},{1,9},{5... | collective-permute-start | bytes 1572872 | tf_op jit(solution)/shard_map/ppermute | solution.py:615
  726.6 33.4 %collective-permute-start.67 = (bf16[256,2048]{1,0:T(8,128)(2,1)S(1)}, bf16[256,2048]{1,0:T(8,128)(2,1)S(1)}, u32[]{:S(2)}, u32[]{:S(2)}) collective-permute-start(bf16[256,2048]{1,0:T(8,128)(2,1)S(1)} %get-tuple-element.278.refs_2_), channel_id=1, source_target_pairs={{0,16},{4,20},{8,24},{12,28},{16,0},{20,4},{24,8},{28,12},{1,17},{... | collective-permute-start | bytes 3145736 | tf_op jit(solution)/shard_map/ppermute | solution.py:615
  728.2 31.9 %collective-permute-start.66 = (bf16[256,2048]{1,0:T(8,128)(2,1)S(1)}, bf16[256,2048]{1,0:T(8,128)(2,1)}, u32[]{:S(2)}, u32[]{:S(2)}) collective-permute-start(bf16[256,2048]{1,0:T(8,128)(2,1)S(1)} %get-tuple-element.277.refs_0_), channel_id=1, source_target_pairs={{0,8},{4,12},{8,0},{12,4},{16,24},{20,28},{24,16},{28,20},{1,9},{5... | collective-permute-start | bytes 3145736 | tf_op jit(solution)/shard_map/ppermute | solution.py:615
  (130 other events, 2096.7 us)

commit v2 on v1

--- a/solution.py
+++ b/solution.py
@@ -14,7 +14,7 @@
 PAIR = 2 * HEAD_DIM
 CHUNKS = 1
 SUB = 256
-LIGHT = 64
+WEIGHTS = {"mlp_kept": 30}
 EXTRA = 16
 
 EPSILON = 1e-05
@@ -34,15 +34,15 @@
     return pltpu.CompilerParams(vmem_limit_bytes=mib << 20)
 
 
-def cost(flops, nbytes):
-    return pl.CostEstimate(flops=int(flops) // LIGHT, bytes_accessed=int(nbytes) // LIGHT, transcendentals=0)
+def cost(name):
+    return pl.CostEstimate(flops=int(WEIGHTS.get(name, 0) * 1e9), bytes_accessed=0, transcendentals=0)
 
 
 def after(value, *others):
     return lax.optimization_barrier((value, *others))[0]
 
 
-def kernel_call(body, grid, ins, in_specs, outs, out_specs, previous=(), scratch=(), mib=56, flops=0, name=None, weight=1):
+def kernel_call(body, grid, ins, in_specs, outs, out_specs, previous=(), scratch=(), mib=56, name=None):
     given = len(ins)
     previous = dict(previous)
     aliases = {given + i: out for i, out in enumerate(previous)}
@@ -50,7 +50,6 @@
     def run(*refs):
         body(*refs[:given], *refs[given + len(previous) :])
 
-    nbytes = sum(a.size * a.dtype.itemsize for a in ins) + sum(o.size * o.dtype.itemsize for o in outs)
     return pl.pallas_call(
         run,
         grid=grid,
@@ -60,7 +59,7 @@
         input_output_aliases=aliases,
         scratch_shapes=list(scratch),
         compiler_params=params(mib),
-        cost_estimate=cost(weight * flops, nbytes),
+        cost_estimate=cost(name),
         name=name,
     )(*ins, *previous.values())
 
@@ -73,8 +72,7 @@
     return jax.ShapeDtypeStruct(shape, dtype)
 
 
-def prefetched(body, scalars, grid, ins, in_specs, outs, out_specs, mib=56, flops=0, name=None):
-    nbytes = sum(a.size * a.dtype.itemsize for a in ins) + sum(o.size * o.dtype.itemsize for o in outs)
+def prefetched(body, scalars, grid, ins, in_specs, outs, out_specs, mib=56, name=None):
     return pl.pallas_call(
         body,
         grid_spec=pltpu.PrefetchScalarGridSpec(
@@ -82,7 +80,7 @@
         ),
         out_shape=outs,
         compiler_params=params(mib),
-        cost_estimate=cost(flops, nbytes),
+        cost_estimate=cost(name),
         name=name,
     )(jnp.stack(scalars).astype(jnp.int32), *ins)
 
@@ -177,7 +175,6 @@
         ],
         previous,
         mib=34,
-        flops=2 * t * D * 3 * width,
         name="project",
     )
 
@@ -243,7 +240,6 @@
             pl.BlockSpec((t, PAIR), here),
         ],
         mib=30,
-        flops=(8 * t * t * width + 2 * t * width * D) * 4 * LIGHT,
         name="attend",
     )
 
@@ -322,9 +318,7 @@
         [own, own, own, pl.BlockSpec((8, t), lambda p: (0, 0))],
         scratch=[pltpu.VMEM((t, PAIR), F32)] * 2,
         mib=28,
-        flops=20 * t * t * width,
         name="attend_back",
-        weight=4 * LIGHT,
     )
 
 
@@ -368,7 +362,6 @@
         [pl.BlockSpec((t, D), own), pl.BlockSpec((t, 128), own), column, column, column],
         previous,
         mib=46,
-        flops=6 * t * D * units,
         name="mlp",
     )
 
@@ -390,7 +383,6 @@
         [sds((t, len(owners) * width), BF)],
         [pl.BlockSpec((t, width), lambda j, owners: (0, j))],
         mib=28,
-        flops=4 * t * D * units,
         name="mlp_back",
     )[0]
 
@@ -432,7 +424,6 @@
         [sds((t, 128), F32), sds((t, D), BF), sds((t, width), BF)],
         [pl.BlockSpec((tile, 128), row), pl.BlockSpec((tile, D), row), pl.BlockSpec((tile, width), row)],
         mib=24,
-        flops=2 * t * D * width,
         name="branch_back",
     )
 
@@ -469,7 +460,6 @@
         [sds((t + EXTRA, count * width), BF)],
         [pl.BlockSpec((t + EXTRA, width), lambda j, owners: (0, j))],
         mib=34,
-        flops=6 * t * D * width,
         name="project_back",
     )[0]
 
@@ -539,6 +529,17 @@
             mib=14,
             name="assemble",
         )[0]
+
+
+def steps(order, *ops):
+    return [got for op in ops if op.steps < op.n - 1 for got in op.step(order)]
+
+
+def finish(order, *ops):
+    got = steps(order, *ops)
+    while any(op.steps < op.n - 1 for op in ops):
+        got = steps(order, *ops)
+    return got
 
 
 def scatter_order(n):
@@ -594,7 +595,8 @@
             got = self.step(order)
         return got
 
-    def total(self):
+    def total(self, order):
+        self.got = {name: order(value) for name, value in self.got.items()}
         own = self.any(self.me) if self.n != 4 else self.part(self.me)
         return sum((g.astype(F32) for g in self.got.values()), own.astype(F32))
 
@@ -608,6 +610,68 @@
         @pl.when(here)
         def _(ref=ref):
             out_ref[...] = ref[...]
+
+
+def gradients_body(groups, which_ref, *refs):
+    lefts, rest = refs[: len(groups)], refs[len(groups) :]
+    rights, outs = rest[: len(rest) // 2], rest[len(rest) // 2 :]
+    for left, count in zip(lefts, groups):
+        turned = left[...].T
+        for right, out in zip(rights[:count], outs[:count]):
+            out[...] = dot(turned, right[...]).astype(BF)
+        rights, outs = rights[count:], outs[count:]
+
+
+def gradients(which, pairs, name):
+    t = pairs[0][0].shape[0]
+    block = 256
+    nb = D // 2 // block
+    lefts, rights = [left for left, _ in pairs], [right for _, some in pairs for right in some]
+    return prefetched(
+        functools.partial(gradients_body, [len(some) for _, some in pairs]),
+        [which],
+        (nb,),
+        lefts + rights,
+        [pl.BlockSpec((t, block), lambda i, which: (0, which[0] * nb + i))] * len(lefts)
+        + [still(right.shape, lambda i, which: (0, 0)) for right in rights],
+        [sds((D // 2, right.shape[1]), BF) for right in rights],
+        [pl.BlockSpec((block, right.shape[1]), lambda i, which: (i, 0)) for right in rights],
+        mib=30,
+        name=name,
+    )
+
+
+def mlp_out_body(owners_ref, hidden_ref, weight_ref, first_ref, rest_ref):
+    out = dot(hidden_ref[...], weight_ref[...]).astype(BF)
+
+    @pl.when(pl.program_id(0) == 0)
+    def _():
+        first_ref[...] = out
+
+    @pl.when(pl.program_id(0) > 0)
+    def _():
+        rest_ref[...] = out
+
+
+def mlp_out(owners, width, hidden, weight):
+    t, units = hidden.shape
+    return prefetched(
+        mlp_out_body,
+        owners,
+        (len(owners),),
+        [hidden, weight],
+        [
+            still((t, units), lambda j, owners: (0, 0)),
+            pl.BlockSpec((units, width), lambda j, owners: (0, owners[j])),
+        ],
+        [sds((t, width), BF), sds((t, D - width), BF)],
+        [
+            pl.BlockSpec((t, width), lambda j, owners: (0, 0)),
+            pl.BlockSpec((t, width), lambda j, owners: (0, jnp.maximum(j - 1, 0))),
+        ],
+        mib=22,
+        name="mlp_out",
+    )
 
 
 def swap(value, bit, axis="dp"):
@@ -663,20 +727,23 @@
     )
 
 
-def merge_body(joined, bits_ref, *refs):
+def merge_body(widths, bits_ref, *refs):
     for part in range(2):
         for which in range(2):
 
             @pl.when((pl.program_id(0) == bits_ref[part]) == (which == 0))
             def _(part=part, which=which):
                 value = refs[2 * part + which][...]
-                if joined:
-                    refs[4][part] = value
+                if widths:
+                    at = 0
+                    for out, wide in zip(refs[4:], widths):
+                        out[part] = value[:, at : at + wide]
+                        at += wide
                 else:
                     refs[4 + part][...] = value
 
 
-def merge(upper, lower, bits, joined):
+def merge(upper, lower, bits, widths=()):
     rows, columns = upper[0].shape
     block = min(128, rows)
     nb = rows // block
@@ -688,14 +755,14 @@
 
         return pl.BlockSpec((block, columns), index)
 
-    if joined:
-        outs = [sds((2, 2 * rows, columns), BF)]
-        out_specs = [pl.BlockSpec((2, block, columns), lambda i, j, bits: (0, i * nb + j, 0))]
+    if widths:
+        outs = [sds((2, 2 * rows, wide), BF) for wide in widths]
+        out_specs = [pl.BlockSpec((2, block, wide), lambda i, j, bits: (0, i * nb + j, 0)) for wide in widths]
     else:
         outs = [sds((2 * rows, columns), BF)] * 2
         out_specs = [pl.BlockSpec((block, columns), lambda i, j, bits: (i * nb + j, 0))] * 2
     return prefetched(
-        functools.partial(merge_body, joined),
+        functools.partial(merge_body, widths),
         bits,
         (2, nb),
         [*upper, *lower],
@@ -724,15 +791,21 @@
     p, q = add(*upper[0]), add(*lower[0])
     for s in reversed(range(count - 1)):
         a, b = orders[0][s], orders[1][s]
+        p, q = lax.optimization_barrier((p, q))
         got = swap(p, a), swap(q, b)
         yield p
-        out = merge([order(p), got[0]], [q, got[1]], [bit(a), bit(b)], s == 0)
+        out = merge([order(p), got[0]], [q, got[1]], [bit(a), bit(b)], () if s else [g.shape[1] for g in given])
         if s:
             p, q = out
-    own = out[0].reshape(-1, out[0].shape[2])
-    other = swap(own, 0)
-    yield own
+    own = [array.reshape(-1, array.shape[2]) for array in out]
+    other = [swap(array, 0) for array in own]
+    yield own[0]
     yield own, other
+
+
+def finish_sum(steps_left):
+    *_, last = steps_left
+    return last
 
 
 def halves(core, own, other, nb):
@@ -746,64 +819,69 @@
     return index(True), index(False)
 
 
-def mlp_out_body(units, core_ref, own_ref, other_ref, gate_up_ref, down_ref):
+def halves_body(store, core_ref, *refs):
     half = pl.program_id(0) // (pl.num_programs(0) // 2)
-    for ref, mine in ((own_ref, True), (other_ref, False)):
+    groups = store.groups
+    own, other, outs = refs[:groups], refs[groups : 2 * groups], refs[2 * groups :]
+    for arrays, mine in ((own, True), (other, False)):
 
         @pl.when((half == core_ref[0]) == mine)
-        def _(ref=ref):
-            gate_up_ref[:, 0, :] = ref[:, :units].astype(F32)
-            gate_up_ref[:, 1, :] = ref[:, units : 2 * units].astype(F32)
-            down_ref[...] = ref[:, 2 * units :].astype(F32).T
-
-
-def mlp_out(core, own, other):
-    columns = own.shape[1]
-    units = columns // 3
-    block = 128
-    nb = own.shape[0] // block
-    mine, theirs = halves(core, own, other, nb)
+        def _(arrays=arrays):
+            store(arrays, outs)
+
+
+def from_halves(store, core, own, other, outs, out_specs, block, mib, name):
+    store.groups = len(own)
+    nb = own[0].shape[0] // block
     return prefetched(
-        functools.partial(mlp_out_body, units),
+        functools.partial(halves_body, store),
         [core],
         (2 * nb,),
-        [own, other],
-        [pl.BlockSpec((block, columns), mine), pl.BlockSpec((block, columns), theirs)],
-        [sds((D, 2, units), F32), sds((units, D), F32)],
-        [pl.BlockSpec((block, 2, units), lambda i, c: (i, 0, 0)), pl.BlockSpec((units, block), lambda i, c: (0, i))],
-        mib=26,
-        name="mlp_out",
-    )
-
-
-def attention_out_body(width, core_ref, own_ref, other_ref, project_ref, output_ref):
-    half = pl.program_id(0) // (pl.num_programs(0) // 2)
-    for ref, mine in ((own_ref, True), (other_ref, False)):
-
-        @pl.when((half == core_ref[0]) == mine)
-        def _(ref=ref):
-            for k in range(3):
-                project_ref[k] = ref[:, k * width : (k + 1) * width].astype(F32)
-            output_ref[...] = ref[:, 3 * width :].astype(F32).T
+        [*own, *other],
+        [
+            pl.BlockSpec((block, array.shape[1]), index)
+            for arrays, index in zip((own, other), halves(core, own, other, nb))
+            for array in arrays
+        ],
+        outs,
+        out_specs,
+        mib=mib,
+        name=name,
+    )
+
+
+def gate_up_out(core, own, other):
+    def store(arrays, outs):
+        for k in range(2):
+            outs[0][:, k, :] = arrays[k][...].astype(F32)
+
+    units, block = own[0].shape[1], 128
+    outs, spec = [sds((D, 2, units), F32)], [pl.BlockSpec((block, 2, units), lambda i, c: (i, 0, 0))]
+    return from_halves(store, core, own, other, outs, spec, block, 22, "gate_up_out")[0]
+
+
+def down_out(core, own, other):
+    def store(arrays, outs):
+        outs[0][...] = arrays[0][...].astype(F32).T
+
+    units, block = own[0].shape[1], 128
+    outs, spec = [sds((units, D), F32)], [pl.BlockSpec((units, block), lambda i, c: (0, i))]
+    return from_halves(store, core, own, other, outs, spec, block, 16, "down_out")[0]
 
 
 def attention_out(core, own, other):
-    columns = own.shape[1]
-    width = columns // 4
-    block = 256
-    nb = own.shape[0] // block
-    mine, theirs = halves(core, own, other, nb)
-    return prefetched(
-        functools.partial(attention_out_body, width),
-        [core],
-        (2 * nb,),
-        [own, other],
-        [pl.BlockSpec((block, columns), mine), pl.BlockSpec((block, columns), theirs)],
-        [sds((3, D, width), F32), sds((width, D), F32)],
-        [pl.BlockSpec((3, block, width), lambda i, c: (0, i, 0)), pl.BlockSpec((width, block), lambda i, c: (0, i))],
-        mib=22,
-        name="attention_out",
-    )
+    def store(arrays, outs):
+        for k in range(3):
+            outs[0][k] = arrays[k][...].astype(F32)
+        outs[1][...] = arrays[3][...].astype(F32).T
+
+    width, block = own[0].shape[1], 256
+    outs = [sds((3, D, width), F32), sds((width, D), F32)]
+    specs = [
+        pl.BlockSpec((3, block, width), lambda i, c: (0, i, 0)),
+        pl.BlockSpec((width, block), lambda i, c: (0, i)),
+    ]
+    return from_halves(store, core, own, other, outs, specs, block, 22, "attention_out")
 
 
 def per_device(
@@ -835,9 +913,9 @@
     order.done(*got, gate_w)
     got = whole_x.step(order)
     up_w = order(gate_up_weight)[:, 1]
-    order.done(*got, up_w)
+    tables = rope_tables()
+    order.done(*got, up_w, tables)
     whole_x.last(order)
-    tables = rope_tables()
     x = whole_x.whole()
     gain_one, gain_two, shift_two = (x[t + i : t + i + 1].astype(F32) for i in (0, 2, 3))
     project_w = project_weight.transpose(1, 0, 2)
@@ -855,12 +933,12 @@
     order.done(lse)
     branch = Scatter(first, rest)
     for _ in range(2):
-        order.done(*whole_up.step(order), *branch.step(order))
+        order.done(*whole_up.step(order), *branch.step(order), with_rows)
     if whole_up.n > 4:
         whole_up.last(order)
     branch.last(order)
     upstream = whole_up.whole()
-    middle_share = tokens.astype(F32) + branch.total()
+    middle_share = tokens.astype(F32) + branch.total(order)
     middle_sent = (middle_share - stats_one[:, 0:1]).astype(BF)
     order.done(middle_sent)
     whole_middle = Gather(middle_sent)
@@ -875,58 +953,50 @@
     rest = mlp_back(owners[1:], width, after(dgate, first), dup, gate_w, up_w)
     order.done(first)
     delta_two = Scatter(first, rest)
-    got = delta_two.step(order)
-    order.done(rest)
-    mlp_half = lambda which: [
-        dot(half_of(normed_two, which), order(jnp.concatenate([dgate, dup], axis=1)), TN).astype(BF),
-        dot(half_of(upstream, which), order(hidden), TN).astype(BF),
-    ]
-    mlp_given = mlp_half(1 - core)
+    got = steps(order, delta_two)
+    order.done(rest, *got)
+    got = steps(order, delta_two)
+    mlp_grads = lambda which, name: gradients(
+        which, [(normed_two, [order(dgate), dup]), (upstream, [hidden])], name
+    )
+    mlp_given = mlp_grads(1 - core, "mlp_given")
     mlp_sum = sum_over_dp(mlp_given, order)
     next(mlp_sum)
     order.done(*got, *mlp_given)
-    got = delta_two.step(order)
-    mlp_kept = mlp_half(core)
-    order.done(*mlp_kept)
-    held = mlp_sum.send(mlp_kept)
-    order.done(*got, held)
-    got = delta_two.last(order)
-    mlp_parts = dot(order(hidden), down_weight).astype(BF)
-    order.done(*got, mlp_parts)
-    delta_two = order(delta_two.total())
+    got = finish(order, delta_two)
+    mlp_kept = mlp_grads(core, "mlp_kept")
+    order.done(*got, *mlp_kept)
+    delta_two = delta_two.total(order)
     unit_two = (mine(middle).astype(F32) - stats_two[:, 0:1]) * stats_two[:, 1:2]
     two_grads = [jnp.sum(delta_two * unit_two, axis=0), jnp.sum(delta_two, axis=0)]
     e_own = delta_two * norm_two_gain.astype(F32)
     e_sent = e_own.astype(BF)
     order.done(e_sent)
     whole_e = Gather(e_sent)
-    got = whole_e.step(order)
-    held = next(mlp_sum)
-    piece = lambda owner: lax.dynamic_slice_in_dim(mlp_parts, owner * width, width, 1)
-    mlp_share = Scatter(piece(owners[0]), jnp.concatenate([piece(owner) for owner in owners[1:]], axis=1))
-    order.done(*got, held, mlp_share.rest)
-    got = whole_e.step(order) + mlp_share.step(order)
-    order.done(*got)
-    got = whole_e.last(order) + mlp_share.step(order)
+    got = steps(order, whole_e)
+    held = mlp_sum.send(mlp_kept)
+    order.done(*got, held)
+    got = steps(order, whole_e)
+    mlp_share = Scatter(*mlp_out(owners, width, order(hidden), down_weight))
+    order.done(*got, mlp_share.rest)
+    got = finish(order, whole_e) + steps(order, mlp_share)
     held = next(mlp_sum)
     e = whole_e.whole()
 
     order.done(e, held, *got)
-    mlp_share.last(order)
+    share_got = steps(order, mlp_share)
     means_two, dbranch, dctx = branch_back(order(e), middle, stats_two, upstream, output_weight)
     order.done(dctx)
+    held = next(mlp_sum)
+    order.done(held)
     dq, dk, dv, sums = attend_back(heads, lse, context, order(dctx), tables, with_rows)
-    order.done(dq)
-    mlp_share.got = {name: order(value) for name, value in mlp_share.got.items()}
-    result = (middle_share + mlp_share.total()).astype(BF)
     held = next(mlp_sum)
-    order.done(held, result)
+    order.done(dq, held, *share_got)
     delta_heads = (dq, dk, dv)
-    attention_half = lambda which: [
-        dot(half_of(normed_one, which), order(jnp.concatenate(delta_heads, axis=1)), TN).astype(BF),
-        dot(half_of(dbranch, which), order(context), TN).astype(BF),
-    ]
-    attention_given = attention_half(1 - core)
+    attention_grads = lambda which, name: gradients(
+        which, [(normed_one, [order(dq), dk, dv]), (dbranch, [context])], name
+    )
+    attention_given = attention_grads(1 - core, "attention_given")
     attention_sum = sum_over_dp(attention_given, order)
     next(attention_sum)
     sum_rows = 2 * t // width
@@ -937,47 +1007,54 @@
     rest = back(owners[1:], after(dq, first))
     order.done(first)
     delta_one = Scatter(first, rest)
-    got = delta_one.step(order)
+    got = steps(order, delta_one)
     order.done(rest)
-    attention_kept = attention_half(core)
+    attention_kept = attention_grads(core, "attention_kept")
     order.done(*attention_kept)
     held = attention_sum.send(attention_kept)
     order.done(held, *got)
-    got = delta_one.step(order)
+    got = steps(order, delta_one)
     held = next(mlp_sum)
     order.done(held)
+    held = next(attention_sum)
+    order.done(held, *got)
+    got = finish(order, delta_one)
     if lax.axis_size("dp") > 8:
         for _ in range(2):
             order.done(next(mlp_sum))
             order.done(next(attention_sum))
     held = next(attention_sum)
-    order.done(held, *got)
-    got = delta_one.last(order)
+    order.done(held)
+    mlp_halves = next(mlp_sum)
+    down_grad = down_out(core, [order(mlp_halves[0][2])], mlp_halves[1][2:])
+    order.done(down_grad)
     held = next(attention_sum)
     order.done(held, *got)
-    mlp_halves = next(mlp_sum)
-    gate_up_grad, down_grad = mlp_out(core, order(mlp_halves[0]), mlp_halves[1])
-    order.done(down_grad)
-    delta_one = order(delta_one.total())
+    delta_one = delta_one.total(order)
     bias_grad = [jnp.sum(a, axis=0, dtype=F32) for a in delta_heads]
     small = jnp.stack([delta_one[t], delta_one[t + 1], *two_grads, *bias_grad])
+    small = small + swap(order(small), 0)
+    order.done(small)
+    finish(order, mlp_share)
     devices = lax.axis_size("dp")
-    others = [lax.ppermute(order(small), "dp", [(i, i ^ k) for i in range(devices)]) for k in range(1, devices)]
+    others = [lax.ppermute(order(small), "dp", [(i, i ^ k) for i in range(devices)]) for k in range(2, devices, 2)]
+    gate_up_grad = gate_up_out(core, [order(mlp_halves[0][0]), mlp_halves[0][1]], mlp_halves[1][:2])
+    order.done(gate_up_grad)
     held = next(attention_sum)
     order.done(held)
+    result = (middle_share + mlp_share.total(order)).astype(BF)
     sums = (delta_one[t + 2 : t + 2 + sum_rows] / D).reshape(2, t).T
     unit_one = (tokens.astype(F32) - stats_one[:, 0:1]) * stats_one[:, 1:2]
     dmid = cotangent.astype(F32) + stats_two[:, 1:2] * (e_own - means_two[:, 0:1] - unit_two * means_two[:, 1:2])
     tokens_grad = order(dmid) + stats_one[:, 1:2] * (
         delta_one[:t] * norm_one_gain.astype(F32) - sums[:, 0:1] - unit_one * sums[:, 1:2]
     )
-    order.done(tokens_grad)
     small = sum((order(other) for other in others), small)
-    order.done(small)
-    held = next(attention_sum)
-    order.done(held)
+    order.done(tokens_grad, small, result)
     attention_halves = next(attention_sum)
-    project_grad, output_grad = attention_out(core, order(attention_halves[0]), attention_halves[1])
+    project_grad, output_grad = attention_out(
+        core, [order(attention_halves[0][0]), *attention_halves[0][1:]], attention_halves[1]
+    )
     return (
         result,
         tokens_grad,

time: 785 us -> 773 us (0.985)
  matrix products: 53.6 us -> 1.82 us
  Pallas kernels: 194 us -> 234 us
  local copies, waits for them, and re-layouts: 76.9 us -> 92 us
  starting transfers between devices: 117 us -> 106 us
  waiting for transfers between devices: 294 us -> 284 us
    dot_general x9 -> x0, matrix products: 50.3 us -> none  [dot(): return lax.dot_general(a, b, dims, preferred_element_type=F32)]
    ppermute x20, waiting for transfers between devices: 148 us -> 196 us  [send(): self.pieces.append(lax.ppermute(order(self.pieces[piece]), 'tensor', pairs))]
    pallas_call x19 -> x25, Pallas kernels: 118 us -> 158 us  [prefetched(): pl.pallas_call(body, grid_spec=pltpu.PrefetchScalarGridSpec(num_scalar_pr...]
    ppermute x20, waiting for transfers between devices: 69 us -> 33.4 us  [send(): self.got[name] = lax.ppermute(order(value), 'tensor', pairs)]
    ppermute x7 -> x3, waiting for transfers between devices: 20.8 us -> 0.01 us  [per_device(): lax.ppermute(order(small), 'dp', [(i, i ^ k) for i in range(devices)])]
    unnamed x174 -> x203, local copies, waits for them, and re-layouts: 50.3 us -> 70.8 us
    ppermute x22 -> x31, waiting for transfers between devices: 56.6 us -> 54.4 us  [swap(): return lax.ppermute(value, axis, [(i, i ^ 1 << bit) for i in range(n)])]
    ppermute x22 -> x31, starting transfers between devices: 17.8 us -> 17.3 us  [swap(): return lax.ppermute(value, axis, [(i, i ^ 1 << bit) for i in range(n)])]
  transfers between devices with their start and end apart: 69 -> 74, of which waited for: 28 -> 26; matrix products, arithmetic and copies ran while one was open for 12% -> 8% of each run, Pallas kernels for 14% -> 21%
where the time goes in v2:
time: 773 us; the launch traced here: 765 us
  waiting for transfers between devices  284 us (37%)
  Pallas kernels  234 us (30%)
  starting transfers between devices  106 us (14%)
  local copies, waits for them, and re-layouts  92 us (12%)
  other arithmetic  44.9 us (6%)
    ppermute x20, waiting for transfers between devices, send(): self.pieces.append(lax.ppermute(order(self.pieces[piece]), 'tensor', pairs))  196 us
    pallas_call x25, Pallas kernels, prefetched(): pl.pallas_call(body, grid_spec=pltpu.PrefetchScalarGridSpec(num_scalar_pr...  158 us
    pallas_call x4, Pallas kernels, kernel_call(): pl.pallas_call(run, grid=grid, in_specs=list(in_specs) + [ANY] * len(prev...  75.7 us
    unnamed x203, local copies, waits for them, and re-layouts  70.8 us
    ppermute x20, starting transfers between devices, send(): self.got[name] = lax.ppermute(order(value), 'tensor', pairs)  55.5 us
    ppermute x31, waiting for transfers between devices, swap(): return lax.ppermute(value, axis, [(i, i ^ 1 << bit) for i in range(n)])  54.4 us
    ppermute x20, waiting for transfers between devices, send(): self.got[name] = lax.ppermute(order(value), 'tensor', pairs)  33.4 us
    ppermute x20, starting transfers between devices, send(): self.pieces.append(lax.ppermute(order(self.pieces[piece]), 'tensor', pairs))  29.5 us
  transfers between devices with their start and end apart: 74, of which 26 were waited for; matrix products, arithmetic and copies ran while one was open for 8% of the time, Pallas kernels for 21%

profile of v2, /device:TPU:0, one launch (start us, length us, event | category | flops | bytes accessed | tf_op | source)
XLA Modules:
  0.0 765.5 jit_solution(18065370535048312022)
XLA Ops:
  19.6 11.7 %collective-permute-done.refs_1_ = bf16[1040,512]{1,0:T(8,128)(2,1)S(1)} collective-permute-done((bf16[1040,512]{1,0:T(8,128)(2,1)S(1)}, bf16[1040,512]{1,0:T(8,128)(2,1)S(1)}, u32[]{:S(2)}, u32[]{:S(2)}) %collective-permute-start) | collective-permute-done | bytes 1064992 | tf_op jit(solution)/shard_map/ppermute | solution.py:490
  44.6 26.3 %collective-permute-done.2.refs_3_ = bf16[1040,512]{1,0:T(8,128)(2,1)S(1)} collective-permute-done((bf16[1040,512]{1,0:T(8,128)(2,1)S(1)}, bf16[1040,512]{1,0:T(8,128)(2,1)S(1)}, u32[]{:S(2)}, u32[]{:S(2)}) %collective-permute-start.2) | collective-permute-done | bytes 1064992 | tf_op jit(solution)/shard_map/ppermute | solution.py:490
  74.2 22.9 %collective-permute-done.4.refs_5_ = bf16[1040,512]{1,0:T(8,128)(2,1)} collective-permute-done((bf16[1040,512]{1,0:T(8,128)(2,1)S(1)}, bf16[1040,512]{1,0:T(8,128)(2,1)}, u32[]{:S(2)}, u32[]{:S(2)}) %collective-permute-start.4) | collective-permute-done | bytes 1064992 | tf_op jit(solution)/shard_map/ppermute | solution.py:490
  114.7 14.2 %project.1 = (bf16[1024,2048]{1,0:T(8,128)(2,1)S(1)}, f32[1024,128]{1,0:T(8,128)S(1)}, bf16[3,1024,512]{2,1,0:T(8,128)(2,1)S(1)}) custom-call(bf16[1040,2048]{1,0:T(8,128)(2,1)S(1)} %copy-done.5, bf16[1040,2048]{1,0:T(8,128)(2,1)S(1)} %copy-done.5, bf16[3,2048,512]{2,1,0:T(8,128)(2,1)S(1)} %bitcast.53, f32[3,1,512]{2,1,0:T(1,128)S(1)} %copy.27.refs_3_, ...), custom_call_target="tpu_custom_call" | custom-call | tf_op jit(solution)/shard_map/project/pallas_call | solution.py:53
  129.0 16.9 %attend.1 = (bf16[1024,512]{1,0:T(8,128)(2,1)S(1)}, bf16[1024,1536]{1,0:T(8,128)(2,1)S(1)}, bf16[1024,512]{1,0:T(8,128)(2,1)S(1)}, f32[1024,512]{1,0:T(8,128)S(1)}) custom-call(s32[4]{0:T(128)S(1)} %pad_add_fusion.owners_ref, bf16[3,1024,512]{2,1,0:T(8,128)(2,1)S(1)} %get-tuple-element.181.q_ref.k_ref.v_ref.refs_0_.refs_1_.refs_2_, ...), custom_call_target="tpu_custom_call" | custom-call | tf_op jit(solution)/shard_map/attend/pallas_call | solution.py:76
  158.5 14.5 %collective-permute-done.8.refs_3_ = bf16[1024,512]{1,0:T(8,128)(2,1)S(1)} collective-permute-done((bf16[1024,512]{1,0:T(8,128)(2,1)}, bf16[1024,512]{1,0:T(8,128)(2,1)S(1)}, u32[]{:S(2)}, u32[]{:S(2)}) %collective-permute-start.8) | collective-permute-done | bytes 1048608 | tf_op jit(solution)/shard_map/ppermute | solution.py:490
  184.7 11.8 %collective-permute-done.11.refs_5_ = bf16[1024,512]{1,0:T(8,128)(2,1)} collective-permute-done((bf16[1024,512]{1,0:T(8,128)(2,1)}, bf16[1024,512]{1,0:T(8,128)(2,1)}, u32[]{:S(2)}, u32[]{:S(2)}) %collective-permute-start.11) | collective-permute-done | bytes 1048608 | tf_op jit(solution)/shard_map/ppermute | solution.py:490
  210.5 14.3 %collective-permute-done.13 = bf16[1024,512]{1,0:T(8,128)(2,1)} collective-permute-done((bf16[1024,512]{1,0:T(8,128)(2,1)}, bf16[1024,512]{1,0:T(8,128)(2,1)}, u32[]{:S(2)}, u32[]{:S(2)}) %collective-permute-start.13) | collective-permute-done | bytes 1048608 | tf_op jit(solution)/shard_map/ppermute | solution.py:569
  231.9 15.8 %collective-permute-done.15.refs_1_ = bf16[1024,512]{1,0:T(8,128)(2,1)S(1)} collective-permute-done((bf16[1024,512]{1,0:T(8,128)(2,1)S(1)}, bf16[1024,512]{1,0:T(8,128)(2,1)S(1)}, u32[]{:S(2)}, u32[]{:S(2)}) %collective-permute-start.15) | collective-permute-done | bytes 1048608 | tf_op jit(solution)/shard_map/ppermute | solution.py:490
  257.9 12.6 %collective-permute-done.17.refs_3_ = bf16[1024,512]{1,0:T(8,128)(2,1)S(1)} collective-permute-done((bf16[1024,512]{1,0:T(8,128)(2,1)S(1)}, bf16[1024,512]{1,0:T(8,128)(2,1)S(1)}, u32[]{:S(2)}, u32[]{:S(2)}) %collective-permute-start.17) | collective-permute-done | bytes 1048608 | tf_op jit(solution)/shard_map/ppermute | solution.py:490
  270.5 23.5 %collective-permute-done.19.refs_5_ = bf16[1024,512]{1,0:T(8,128)(2,1)S(1)} collective-permute-done((bf16[1024,512]{1,0:T(8,128)(2,1)S(1)}, bf16[1024,512]{1,0:T(8,128)(2,1)S(1)}, u32[]{:S(2)}, u32[]{:S(2)}) %collective-permute-start.19) | collective-permute-done | bytes 1048608 | tf_op jit(solution)/shard_map/ppermute | solution.py:490
  296.8 32.5 %mlp.1 = (bf16[1024,2048]{1,0:T(8,128)(2,1)}, f32[1024,128]{1,0:T(8,128)S(1)}, bf16[1024,1408]{1,0:T(8,128)(2,1)S(1)}, bf16[1024,1408]{1,0:T(8,128)(2,1)S(1)}, bf16[1024,1408]{1,0:T(8,128)(2,1)}) custom-call(bf16[1024,2048]{1,0:T(8,128)(2,1)} %copy-done.9, bf16[1024,2048]{1,0:T(8,128)(2,1)} %copy-done.7, f32[1,2048]{1,0:T(1,128)S(1)} %get-tuple-element.347.refs_2_, ...), custom_call_target="tpu_custom_call" | custom-call | tf_op jit(solution)/shard_map/mlp/pallas_call | solution.py:53
  338.4 11.1 %mlp_back.3 = bf16[1024,1536]{1,0:T(8,128)(2,1)S(1)} custom-call(s32[3]{0:T(128)S(1)} %pad_add_fusion.1.owners_ref, bf16[1024,1408]{1,0:T(8,128)(2,1)S(1)} %get-tuple-element.219.dgate_ref.refs_2_, bf16[1024,1408]{1,0:T(8,128)(2,1)S(1)} %copy-done.14, bf16[2048,1408]{1,0:T(8,128)(2,1)S(1)} %bitcast.62, bf16[2048,1408]{1,0:T(8,128)(2,1)S(1)} %bitcast.64), custom_call_target="tpu_custom_call" | custom-call | tf_op jit(solution)/shard_map/mlp_back/pallas_call | solution.py:76
  371.4 12.3 %mlp_given.1 = (bf16[1024,1408]{1,0:T(8,128)(2,1)}, bf16[1024,1408]{1,0:T(8,128)(2,1)}, bf16[1024,1408]{1,0:T(8,128)(2,1)S(1)}) custom-call(s32[1]{0:T(128)} %bitcast.12.which_ref, bf16[1024,2048]{1,0:T(8,128)(2,1)S(1)} %copy-done.53, bf16[1024,2048]{1,0:T(8,128)(2,1)} %copy-done.7, bf16[1024,1408]{1,0:T(8,128)(2,1)S(1)} %copy-done.12, ...), custom_call_target="tpu_custom_call" | custom-call | tf_op jit(solution)/shard_map/mlp_given/pallas_call | solution.py:76
  389.9 11.9 %mlp_kept.1 = (bf16[1024,1408]{1,0:T(8,128)(2,1)S(1)}, bf16[1024,1408]{1,0:T(8,128)(2,1)S(1)}, bf16[1024,1408]{1,0:T(8,128)(2,1)S(1)}) custom-call(s32[1]{0:T(128)} %bitcast.13.which_ref.core_ref, bf16[1024,2048]{1,0:T(8,128)(2,1)S(1)} %copy-done.54, bf16[1024,2048]{1,0:T(8,128)(2,1)} %copy-done.7, bf16[1024,1408]{1,0:T(8,128)(2,1)S(1)} %copy-done.12, ...), custom_call_target="tpu_custom_call" | custom-call | flops 30000001024 | tf_op jit(solution)/shard_map/mlp_kept/pallas_call | solution.py:76
  441.3 21.5 %collective-permute-done.25.refs_1_ = bf16[1024,512]{1,0:T(8,128)(2,1)S(1)} collective-permute-done((bf16[1024,512]{1,0:T(8,128)(2,1)S(1)}, bf16[1024,512]{1,0:T(8,128)(2,1)S(1)}, u32[]{:S(2)}, u32[]{:S(2)}) %collective-permute-start.25) | collective-permute-done | bytes 1048608 | tf_op jit(solution)/shard_map/ppermute | solution.py:490
  473.9 18.6 %collective-permute-done.30.refs_3_ = bf16[1024,512]{1,0:T(8,128)(2,1)S(1)} collective-permute-done((bf16[1024,512]{1,0:T(8,128)(2,1)S(1)}, bf16[1024,512]{1,0:T(8,128)(2,1)S(1)}, u32[]{:S(2)}, u32[]{:S(2)}) %collective-permute-start.30) | collective-permute-done | bytes 1048608 | tf_op jit(solution)/shard_map/ppermute | solution.py:490
  502.2 17.2 %collective-permute-done.33.refs_5_ = bf16[1024,512]{1,0:T(8,128)(2,1)S(1)} collective-permute-done((bf16[1024,512]{1,0:T(8,128)(2,1)S(1)}, bf16[1024,512]{1,0:T(8,128)(2,1)S(1)}, u32[]{:S(2)}, u32[]{:S(2)}) %collective-permute-start.33) | collective-permute-done | bytes 1048608 | tf_op jit(solution)/shard_map/ppermute | solution.py:490
  538.8 21.2 %attend_back.1 = (bf16[1024,512]{1,0:T(8,128)(2,1)S(1)}, bf16[1024,512]{1,0:T(8,128)(2,1)S(1)}, bf16[1024,512]{1,0:T(8,128)(2,1)S(1)}, f32[8,1024]{1,0:T(8,128)S(1)}) custom-call(bf16[3,1024,512]{2,1,0:T(8,128)(2,1)S(1)} %copy-done.3, bf16[3,1024,512]{2,1,0:T(8,128)(2,1)S(1)} %copy-done.3, bf16[3,1024,512]{2,1,0:T(8,128)(2,1)S(1)} %copy-done.3, ...), custom_call_target="tpu_custom_call" | custom-call | tf_op jit(solution)/shard_map/attend_back/pallas_call | solution.py:53
  633.1 10.5 %collective-permute-done.50.refs_1_ = bf16[256,2048]{1,0:T(8,128)(2,1)S(1)} collective-permute-done((bf16[256,2048]{1,0:T(8,128)(2,1)S(1)}, bf16[256,2048]{1,0:T(8,128)(2,1)S(1)}, u32[]{:S(2)}, u32[]{:S(2)}) %collective-permute-start.50) | collective-permute-done | bytes 1048608 | tf_op jit(solution)/shard_map/ppermute | solution.py:679
  649.6 12.0 %collective-permute-done.55 = bf16[128,2048]{1,0:T(8,128)(2,1)} collective-permute-done((bf16[128,2048]{1,0:T(8,128)(2,1)}, bf16[128,2048]{1,0:T(8,128)(2,1)}, u32[]{:S(2)}, u32[]{:S(2)}) %collective-permute-start.55) | collective-permute-done | bytes 524320 | tf_op jit(solution)/shard_map/ppermute | solution.py:679
  682.4 12.9 %down_out.1 = f32[1408,2048]{1,0:T(8,128)} custom-call(s32[1]{0:T(128)} %bitcast.13.which_ref.core_ref, bf16[1024,1408]{1,0:T(8,128)(2,1)} %bitcast.17.refs_0_, bf16[1024,1408]{1,0:T(8,128)(2,1)} %collective-permute-done.56.refs_1_), custom_call_target="tpu_custom_call" | custom-call | tf_op jit(solution)/shard_map/down_out/pallas_call | solution.py:76
  709.8 16.3 %collective-permute-done.64.refs_1_ = bf16[256,2048]{1,0:T(8,128)(2,1)} collective-permute-done((bf16[256,2048]{1,0:T(8,128)(2,1)}, bf16[256,2048]{1,0:T(8,128)(2,1)}, u32[]{:S(2)}, u32[]{:S(2)}) %collective-permute-start.64) | collective-permute-done | bytes 1048608 | tf_op jit(solution)/shard_map/ppermute | solution.py:679
  730.8 16.8 %gate_up_out.1 = f32[2048,2,1408]{2,1,0:T(2,128)} custom-call(s32[1]{0:T(128)} %bitcast.13.which_ref.core_ref, bf16[1024,1408]{1,0:T(8,128)(2,1)S(1)} %bitcast.68, bf16[1024,1408]{1,0:T(8,128)(2,1)} %bitcast.23.refs_1_, bf16[1024,1408]{1,0:T(8,128)(2,1)} %collective-permute-done.62.refs_2_, bf16[1024,1408]{1,0:T(8,128)(2,1)} %collective-permute-done.63.refs_3_), custom_call_target="tpu_custom_call" | custom-call | tf_op jit(solution)/shard_map/gate_up_out/pallas_call | solution.py:76
  (426 shorter events, 364.0 us)
Async XLA Ops:
  40.3 30.6 %collective-permute-start.2 = (bf16[1040,512]{1,0:T(8,128)(2,1)S(1)}, bf16[1040,512]{1,0:T(8,128)(2,1)S(1)}, u32[]{:S(2)}, u32[]{:S(2)}) collective-permute-start(bf16[1040,512]{1,0:T(8,128)(2,1)S(1)} %collective-permute-done.1.refs_2_), channel_id=1, source_target_pairs={{1,0},{2,3},{5,4},{6,7},{9,8},{10,11},{13,12},{14,15},{17,16},{18,... | collective-permute-start | bytes 3194888 | tf_op jit(solution)/shard_map/ppermute | solution.py:490
  250.3 43.6 %collective-permute-start.19 = (bf16[1024,512]{1,0:T(8,128)(2,1)S(1)}, bf16[1024,512]{1,0:T(8,128)(2,1)S(1)}, u32[]{:S(2)}, u32[]{:S(2)}) collective-permute-start(bf16[1024,512]{1,0:T(8,128)(2,1)S(1)} %collective-permute-done.18.refs_4_), channel_id=1, source_target_pairs={{1,0},{2,3},{5,4},{6,7},{9,8},{10,11},{13,12},{14,15},{17,16},{18,... | collective-permute-start | bytes 3145736 | tf_op jit(solution)/shard_map/ppermute | solution.py:490
  383.7 32.2 %collective-permute-start.27 = (bf16[1024,1408]{1,0:T(8,128)(2,1)}, bf16[1024,1408]{1,0:T(8,128)(2,1)S(1)}, u32[]{:S(2)}, u32[]{:S(2)}) collective-permute-start(bf16[1024,1408]{1,0:T(8,128)(2,1)} %get-tuple-element.212), channel_id=1, source_target_pairs={{0,4},{4,0},{8,12},{12,8},{16,20},{20,16},{24,28},{28,24},{1,5},{5... | collective-permute-start | bytes 8650760 | tf_op jit(solution)/shard_map/ppermute | solution.py:679
  383.7 33.8 %collective-permute-start.28 = (bf16[1024,1408]{1,0:T(8,128)(2,1)}, bf16[1024,1408]{1,0:T(8,128)(2,1)S(1)}, u32[]{:S(2)}, u32[]{:S(2)}) collective-permute-start(bf16[1024,1408]{1,0:T(8,128)(2,1)} %get-tuple-element.213), channel_id=1, source_target_pairs={{0,4},{4,0},{8,12},{12,8},{16,20},{20,16},{24,28},{28,24},{1,5},{5... | collective-permute-start | bytes 8650760 | tf_op jit(solution)/shard_map/ppermute | solution.py:679
  384.2 34.8 %collective-permute-start.29 = (bf16[1024,1408]{1,0:T(8,128)(2,1)S(1)}, bf16[1024,1408]{1,0:T(8,128)(2,1)}, u32[]{:S(2)}, u32[]{:S(2)}) collective-permute-start(bf16[1024,1408]{1,0:T(8,128)(2,1)S(1)} %get-tuple-element.214), channel_id=1, source_target_pairs={{0,4},{4,0},{8,12},{12,8},{16,20},{20,16},{24,28},{28,24},{1,5},{5... | collective-permute-start | bytes 8650760 | tf_op jit(solution)/shard_map/ppermute | solution.py:679
  434.1 58.4 %collective-permute-start.34 = (bf16[256,4224]{1,0:T(8,128)(2,1)S(1)}, bf16[256,4224]{1,0:T(8,128)(2,1)S(1)}, u32[]{:S(2)}, u32[]{:S(2)}) collective-permute-start(bf16[256,4224]{1,0:T(8,128)(2,1)S(1)} %get-tuple-element.238), channel_id=1, source_target_pairs={{0,8},{4,12},{8,0},{12,4},{16,24},{20,28},{24,16},{28,20},{1,9},{5... | collective-permute-start | bytes 6488072 | tf_op jit(solution)/shard_map/ppermute | solution.py:679
  435.6 56.8 %collective-permute-start.35 = (bf16[256,4224]{1,0:T(8,128)(2,1)}, bf16[256,4224]{1,0:T(8,128)(2,1)S(1)}, u32[]{:S(2)}, u32[]{:S(2)}) collective-permute-start(bf16[256,4224]{1,0:T(8,128)(2,1)} %copy-done.77), channel_id=1, source_target_pairs={{0,16},{4,20},{8,24},{12,28},{16,0},{20,4},{24,8},{28,12},{1,17},{... | collective-permute-start | bytes 6488072 | tf_op jit(solution)/shard_map/ppermute | solution.py:679
  463.6 28.8 %collective-permute-start.30 = (bf16[1024,512]{1,0:T(8,128)(2,1)S(1)}, bf16[1024,512]{1,0:T(8,128)(2,1)S(1)}, u32[]{:S(2)}, u32[]{:S(2)}) collective-permute-start(bf16[1024,512]{1,0:T(8,128)(2,1)S(1)} %collective-permute-done.26.refs_2_), channel_id=1, source_target_pairs={{1,0},{2,3},{5,4},{6,7},{9,8},{10,11},{13,12},{14,15},{17,16},{18,... | collective-permute-start | bytes 3145736 | tf_op jit(solution)/shard_map/ppermute | solution.py:490
  495.0 39.0 %collective-permute-start.38 = (bf16[128,4224]{1,0:T(8,128)(2,1)}, bf16[128,4224]{1,0:T(8,128)(2,1)S(1)}, u32[]{:S(2)}, u32[]{:S(2)}) collective-permute-start(bf16[128,4224]{1,0:T(8,128)(2,1)} %get-tuple-element.253), channel_id=1, source_target_pairs={{0,8},{4,12},{8,0},{12,4},{16,24},{20,28},{24,16},{28,20},{1,9},{5... | collective-permute-start | bytes 3244040 | tf_op jit(solution)/shard_map/ppermute | solution.py:679
  501.6 32.6 %collective-permute-start.37 = (bf16[128,4224]{1,0:T(8,128)(2,1)S(1)}, bf16[128,4224]{1,0:T(8,128)(2,1)S(1)}, u32[]{:S(2)}, u32[]{:S(2)}) collective-permute-start(bf16[128,4224]{1,0:T(8,128)(2,1)S(1)} %get-tuple-element.250), channel_id=1, source_target_pairs={{0,16},{4,20},{8,24},{12,28},{16,0},{20,4},{24,8},{28,12},{1,17},{... | collective-permute-start | bytes 3244040 | tf_op jit(solution)/shard_map/ppermute | solution.py:679
  520.6 42.2 %collective-permute-start.41 = (bf16[1024,512]{1,0:T(8,128)(2,1)S(1)}, bf16[1024,512]{1,0:T(8,128)(2,1)S(1)}, u32[]{:S(2)}, u32[]{:S(2)}) collective-permute-start(bf16[1024,512]{1,0:T(8,128)(2,1)S(1)} %constant_dynamic-slice_fusion.1), channel_id=1, source_target_pairs={{0,1},{3,2},{4,5},{7,6},{8,9},{11,10},{12,13},{15,14},{16,17},{19,... | collective-permute-start | bytes 3145736 | tf_op jit(solution)/shard_map/ppermute | solution.py:569
  572.0 50.2 %collective-permute-start.48 = (bf16[256,4224]{1,0:T(8,128)(2,1)}, bf16[256,4224]{1,0:T(8,128)(2,1)}, u32[]{:S(2)}, u32[]{:S(2)}) collective-permute-start(bf16[256,4224]{1,0:T(8,128)(2,1)} %get-tuple-element.286.refs_0_), channel_id=1, source_target_pairs={{0,8},{4,12},{8,0},{12,4},{16,24},{20,28},{24,16},{28,20},{1,9},{5... | collective-permute-start | bytes 6488072 | tf_op jit(solution)/shard_map/ppermute | solution.py:679
  573.5 50.4 %collective-permute-start.49 = (bf16[256,4224]{1,0:T(8,128)(2,1)}, bf16[256,4224]{1,0:T(8,128)(2,1)}, u32[]{:S(2)}, u32[]{:S(2)}) collective-permute-start(bf16[256,4224]{1,0:T(8,128)(2,1)} %get-tuple-element.287.refs_2_), channel_id=1, source_target_pairs={{0,16},{4,20},{8,24},{12,28},{16,0},{20,4},{24,8},{28,12},{1,17},{... | collective-permute-start | bytes 6488072 | tf_op jit(solution)/shard_map/ppermute | solution.py:679
  605.3 38.3 %collective-permute-start.50 = (bf16[256,2048]{1,0:T(8,128)(2,1)S(1)}, bf16[256,2048]{1,0:T(8,128)(2,1)S(1)}, u32[]{:S(2)}, u32[]{:S(2)}) collective-permute-start(bf16[256,2048]{1,0:T(8,128)(2,1)S(1)} %get-tuple-element.290), channel_id=1, source_target_pairs={{0,8},{4,12},{8,0},{12,4},{16,24},{20,28},{24,16},{28,20},{1,9},{5... | collective-permute-start | bytes 3145736 | tf_op jit(solution)/shard_map/ppermute | solution.py:679
  606.6 38.3 %collective-permute-start.51 = (bf16[256,2048]{1,0:T(8,128)(2,1)S(1)}, bf16[256,2048]{1,0:T(8,128)(2,1)S(1)}, u32[]{:S(2)}, u32[]{:S(2)}) collective-permute-start(bf16[256,2048]{1,0:T(8,128)(2,1)S(1)} %get-tuple-element.293), channel_id=1, source_target_pairs={{0,16},{4,20},{8,24},{12,28},{16,0},{20,4},{24,8},{28,12},{1,17},{... | collective-permute-start | bytes 3145736 | tf_op jit(solution)/shard_map/ppermute | solution.py:679
  607.8 41.8 %collective-permute-start.52 = (bf16[1040,512]{1,0:T(8,128)(2,1)}, bf16[1040,512]{1,0:T(8,128)(2,1)}, u32[]{:S(2)}, u32[]{:S(2)}) collective-permute-start(bf16[1040,512]{1,0:T(8,128)(2,1)} %constant_dynamic-slice_fusion), channel_id=1, source_target_pairs={{0,1},{3,2},{4,5},{7,6},{8,9},{11,10},{12,13},{15,14},{16,17},{19,... | collective-permute-start | bytes 3194888 | tf_op jit(solution)/shard_map/ppermute | solution.py:569
  633.1 44.0 %collective-permute-start.56 = (bf16[1024,1408]{1,0:T(8,128)(2,1)}, bf16[1024,1408]{1,0:T(8,128)(2,1)}, u32[]{:S(2)}, u32[]{:S(2)}) collective-permute-start(bf16[1024,1408]{1,0:T(8,128)(2,1)} %bitcast.17.refs_0_), channel_id=1, source_target_pairs={{0,4},{4,0},{8,12},{12,8},{16,20},{20,16},{24,28},{28,24},{1,5},{5... | collective-permute-start | bytes 8650760 | tf_op jit(solution)/shard_map/ppermute | solution.py:679
  649.6 56.3 %collective-permute-start.62 = (bf16[1024,1408]{1,0:T(8,128)(2,1)}, bf16[1024,1408]{1,0:T(8,128)(2,1)}, u32[]{:S(2)}, u32[]{:S(2)}) collective-permute-start(bf16[1024,1408]{1,0:T(8,128)(2,1)} %bitcast.67), channel_id=1, source_target_pairs={{0,4},{4,0},{8,12},{12,8},{16,20},{20,16},{24,28},{28,24},{1,5},{5... | collective-permute-start | bytes 8650760 | tf_op jit(solution)/shard_map/ppermute | solution.py:679
  667.7 28.4 %collective-permute-start.53 = (bf16[1040,512]{1,0:T(8,128)(2,1)S(1)}, bf16[1040,512]{1,0:T(8,128)(2,1)S(1)}, u32[]{:S(2)}, u32[]{:S(2)}) collective-permute-start(bf16[1040,512]{1,0:T(8,128)(2,1)S(1)} %get-tuple-element.297), channel_id=1, source_target_pairs={{0,1},{1,0},{2,3},{3,2},{4,5},{5,4},{6,7},{7,6},{8,9},{9,8},{10,11... | collective-permute-start | bytes 3194888 | tf_op jit(solution)/shard_map/ppermute | solution.py:569
  667.9 28.3 %collective-permute-start.59 = (bf16[1040,512]{1,0:T(8,128)(2,1)S(1)}, bf16[1040,512]{1,0:T(8,128)(2,1)S(1)}, u32[]{:S(2)}, u32[]{:S(2)}) collective-permute-start(bf16[1040,512]{1,0:T(8,128)(2,1)S(1)} %get-tuple-element.310), channel_id=1, source_target_pairs={{1,2},{2,1},{5,6},{6,5},{9,10},{10,9},{13,14},{14,13},{17,18},{18,... | collective-permute-start | bytes 3194888 | tf_op jit(solution)/shard_map/ppermute | solution.py:569
  676.1 32.5 %collective-permute-start.63 = (bf16[1024,1408]{1,0:T(8,128)(2,1)}, bf16[1024,1408]{1,0:T(8,128)(2,1)}, u32[]{:S(2)}, u32[]{:S(2)}) collective-permute-start(bf16[1024,1408]{1,0:T(8,128)(2,1)} %bitcast.23.refs_1_), channel_id=1, source_target_pairs={{0,4},{4,0},{8,12},{12,8},{16,20},{20,16},{24,28},{28,24},{1,5},{5... | collective-permute-start | bytes 8650760 | tf_op jit(solution)/shard_map/ppermute | solution.py:679
  705.6 46.5 %collective-permute-start.61 = (bf16[1024,512]{1,0:T(8,128)(2,1)}, bf16[1024,512]{1,0:T(8,128)(2,1)}, u32[]{:S(2)}, u32[]{:S(2)}) collective-permute-start(bf16[1024,512]{1,0:T(8,128)(2,1)} %get-tuple-element.315), channel_id=1, source_target_pairs={{0,1},{1,0},{2,3},{3,2},{4,5},{5,4},{6,7},{7,6},{8,9},{9,8},{10,11... | collective-permute-start | bytes 3145736 | tf_op jit(solution)/shard_map/ppermute | solution.py:569
  705.9 47.9 %collective-permute-start.66 = (bf16[1024,512]{1,0:T(8,128)(2,1)}, bf16[1024,512]{1,0:T(8,128)(2,1)}, u32[]{:S(2)}, u32[]{:S(2)}) collective-permute-start(bf16[1024,512]{1,0:T(8,128)(2,1)} %get-tuple-element.323), channel_id=1, source_target_pairs={{1,2},{2,1},{5,6},{6,5},{9,10},{10,9},{13,14},{14,13},{17,18},{18,... | collective-permute-start | bytes 3145736 | tf_op jit(solution)/shard_map/ppermute | solution.py:569
  708.5 42.9 %collective-permute-start.67 = (f32[7,512]{1,0:T(8,128)S(1)}, f32[7,512]{1,0:T(8,128)S(1)}, u32[]{:S(2)}, u32[]{:S(2)}) collective-permute-start(f32[7,512]{1,0:T(8,128)S(1)} %add.258), channel_id=1, source_target_pairs={{0,8},{4,12},{8,0},{12,4},{16,24},{20,28},{24,16},{28,20},{1,9},{5... | collective-permute-start | bytes 43016 | tf_op jit(solution)/shard_map/ppermute | solution.py:1040
  (151 other events, 2174.9 us)

commit v3 on v2

--- a/solution.py
+++ b/solution.py
@@ -14,7 +14,7 @@
 PAIR = 2 * HEAD_DIM
 CHUNKS = 1
 SUB = 256
-WEIGHTS = {"mlp_kept": 30}
+WEIGHTS = {"mlp_kept": 30, "mlp_out": 10, "project_back": 5, "attend_back": 20}
 EXTRA = 16
 
 EPSILON = 1e-05
@@ -382,7 +382,7 @@
         [whole, whole, weight, weight],
         [sds((t, len(owners) * width), BF)],
         [pl.BlockSpec((t, width), lambda j, owners: (0, j))],
-        mib=28,
+        mib=56,
         name="mlp_back",
     )[0]
 
@@ -459,7 +459,7 @@
         ],
         [sds((t + EXTRA, count * width), BF)],
         [pl.BlockSpec((t + EXTRA, width), lambda j, owners: (0, j))],
-        mib=34,
+        mib=56,
         name="project_back",
     )[0]
 
@@ -612,31 +612,35 @@
             out_ref[...] = ref[...]
 
 
-def gradients_body(groups, which_ref, *refs):
+def gradients_body(groups, join, which_ref, *refs):
     lefts, rest = refs[: len(groups)], refs[len(groups) :]
-    rights, outs = rest[: len(rest) // 2], rest[len(rest) // 2 :]
+    rights, outs = rest[: sum(groups)], rest[sum(groups) :]
+    k = 0
     for left, count in zip(lefts, groups):
         turned = left[...].T
-        for right, out in zip(rights[:count], outs[:count]):
-            out[...] = dot(turned, right[...]).astype(BF)
-        rights, outs = rights[count:], outs[count:]
-
-
-def gradients(which, pairs, name):
+        for right in rights[k : k + count]:
+            wide = right.shape[1]
+            at = k % join * wide
+            outs[k // join][:, at : at + wide] = dot(turned, right[...]).astype(BF)
+            k += 1
+
+
+def gradients(which, pairs, name, join=1):
     t = pairs[0][0].shape[0]
     block = 256
     nb = D // 2 // block
     lefts, rights = [left for left, _ in pairs], [right for _, some in pairs for right in some]
+    wide = join * rights[0].shape[1]
     return prefetched(
-        functools.partial(gradients_body, [len(some) for _, some in pairs]),
+        functools.partial(gradients_body, [len(some) for _, some in pairs], join),
         [which],
         (nb,),
         lefts + rights,
         [pl.BlockSpec((t, block), lambda i, which: (0, which[0] * nb + i))] * len(lefts)
         + [still(right.shape, lambda i, which: (0, 0)) for right in rights],
-        [sds((D // 2, right.shape[1]), BF) for right in rights],
-        [pl.BlockSpec((block, right.shape[1]), lambda i, which: (i, 0)) for right in rights],
-        mib=30,
+        [sds((D // 2, wide), BF)] * (len(rights) // join),
+        [pl.BlockSpec((block, wide), lambda i, which: (i, 0))] * (len(rights) // join),
+        mib=56,
         name=name,
     )
 
@@ -722,7 +726,7 @@
         in_specs,
         [sds((rows, columns), BF)] * 4,
         [given, kept] * 2,
-        mib=28,
+        mib=56,
         name="split",
     )
 
@@ -769,7 +773,7 @@
         [spec(part, which) for part in range(2) for which in range(2)],
         outs,
         out_specs,
-        mib=22,
+        mib=56,
         name="merge",
     )
 
@@ -857,7 +861,7 @@
 
     units, block = own[0].shape[1], 128
     outs, spec = [sds((D, 2, units), F32)], [pl.BlockSpec((block, 2, units), lambda i, c: (i, 0, 0))]
-    return from_halves(store, core, own, other, outs, spec, block, 22, "gate_up_out")[0]
+    return from_halves(store, core, own, other, outs, spec, block, 56, "gate_up_out")[0]
 
 
 def down_out(core, own, other):
@@ -866,22 +870,22 @@
 
     units, block = own[0].shape[1], 128
     outs, spec = [sds((units, D), F32)], [pl.BlockSpec((units, block), lambda i, c: (0, i))]
-    return from_halves(store, core, own, other, outs, spec, block, 16, "down_out")[0]
+    return from_halves(store, core, own, other, outs, spec, block, 56, "down_out")[0]
 
 
 def attention_out(core, own, other):
     def store(arrays, outs):
         for k in range(3):
-            outs[0][k] = arrays[k][...].astype(F32)
-        outs[1][...] = arrays[3][...].astype(F32).T
-
-    width, block = own[0].shape[1], 256
+            outs[0][k] = arrays[k // 2][:, k % 2 * width : (k % 2 + 1) * width].astype(F32)
+        outs[1][...] = arrays[1][:, width:].astype(F32).T
+
+    width, block = own[0].shape[1] // 2, 256
     outs = [sds((3, D, width), F32), sds((width, D), F32)]
     specs = [
         pl.BlockSpec((3, block, width), lambda i, c: (0, i, 0)),
         pl.BlockSpec((width, block), lambda i, c: (0, i)),
     ]
-    return from_halves(store, core, own, other, outs, specs, block, 22, "attention_out")
+    return from_halves(store, core, own, other, outs, specs, block, 56, "attention_out")
 
 
 def per_device(
@@ -993,15 +997,8 @@
     held = next(mlp_sum)
     order.done(dq, held, *share_got)
     delta_heads = (dq, dk, dv)
-    attention_grads = lambda which, name: gradients(
-        which, [(normed_one, [order(dq), dk, dv]), (dbranch, [context])], name
-    )
-    attention_given = attention_grads(1 - core, "attention_given")
-    attention_sum = sum_over_dp(attention_given, order)
-    next(attention_sum)
     sum_rows = 2 * t // width
     below = jnp.pad(sums[:2].reshape(sum_rows, width), ((2, EXTRA - 2 - sum_rows), (0, 0)))
-    order.done(*attention_given, below)
     back = lambda owners, dq: project_back(owners, dq, dk, dv, project_w, x, stats_one, below)
     first = back(owners[:1], order(dq))
     rest = back(owners[1:], after(dq, first))
@@ -1009,16 +1006,25 @@
     delta_one = Scatter(first, rest)
     got = steps(order, delta_one)
     order.done(rest)
+    attention_grads = lambda which, name: gradients(
+        which, [(normed_one, [order(dq), dk, dv]), (dbranch, [context])], name, join=2
+    )
+    attention_given = attention_grads(1 - core, "attention_given")
+    attention_sum = sum_over_dp(attention_given, order)
+    next(attention_sum)
+    order.done(*attention_given)
     attention_kept = attention_grads(core, "attention_kept")
-    order.done(*attention_kept)
+    order.done(*attention_kept, *got)
+    got = steps(order, delta_one)
     held = attention_sum.send(attention_kept)
+    order.done(held)
+    held = next(mlp_sum)
     order.done(held, *got)
-    got = steps(order, delta_one)
-    held = next(mlp_sum)
+    got = finish(order, delta_one)
+    held = next(attention_sum)
     order.done(held)
     held = next(attention_sum)
     order.done(held, *got)
-    got = finish(order, delta_one)
     if lax.axis_size("dp") > 8:
         for _ in range(2):
             order.done(next(mlp_sum))
@@ -1026,22 +1032,20 @@
     held = next(attention_sum)
     order.done(held)
     mlp_halves = next(mlp_sum)
-    down_grad = down_out(core, [order(mlp_halves[0][2])], mlp_halves[1][2:])
-    order.done(down_grad)
-    held = next(attention_sum)
-    order.done(held, *got)
+    gate_up_grad = gate_up_out(core, [order(mlp_halves[0][0]), mlp_halves[0][1]], mlp_halves[1][:2])
+    order.done(gate_up_grad)
     delta_one = delta_one.total(order)
     bias_grad = [jnp.sum(a, axis=0, dtype=F32) for a in delta_heads]
     small = jnp.stack([delta_one[t], delta_one[t + 1], *two_grads, *bias_grad])
-    small = small + swap(order(small), 0)
+    small = small + swap(small, 0)
     order.done(small)
+    held = next(attention_sum)
+    order.done(held)
     finish(order, mlp_share)
     devices = lax.axis_size("dp")
     others = [lax.ppermute(order(small), "dp", [(i, i ^ k) for i in range(devices)]) for k in range(2, devices, 2)]
-    gate_up_grad = gate_up_out(core, [order(mlp_halves[0][0]), mlp_halves[0][1]], mlp_halves[1][:2])
-    order.done(gate_up_grad)
-    held = next(attention_sum)
-    order.done(held)
+    down_grad = down_out(core, [order(mlp_halves[0][2])], mlp_halves[1][2:])
+    order.done(down_grad)
     result = (middle_share + mlp_share.total(order)).astype(BF)
     sums = (delta_one[t + 2 : t + 2 + sum_rows] / D).reshape(2, t).T
     unit_one = (tokens.astype(F32) - stats_one[:, 0:1]) * stats_one[:, 1:2]

time: 773 us -> 785 us (1.016)
  Pallas kernels: 234 us -> 292 us
  waiting for transfers between devices: 284 us -> 243 us
  local copies, waits for them, and re-layouts: 92 us -> 70.4 us
  starting transfers between devices: 106 us -> 119 us
    pallas_call x25, Pallas kernels: 158 us -> 217 us  [prefetched(): pl.pallas_call(body, grid_spec=pltpu.PrefetchScalarGridSpec(num_scalar_pr...]
    ppermute x20, waiting for transfers between devices: 196 us -> 138 us  [send(): self.pieces.append(lax.ppermute(order(self.pieces[piece]), 'tensor', pairs))]
    ppermute x20, waiting for transfers between devices: 33.4 us -> 63.5 us  [send(): self.got[name] = lax.ppermute(order(value), 'tensor', pairs)]
    unnamed x203 -> x177, local copies, waits for them, and re-layouts: 70.8 us -> 46.2 us
    ppermute x31 -> x27, waiting for transfers between devices: 54.4 us -> 35.3 us  [swap(): return lax.ppermute(value, axis, [(i, i ^ 1 << bit) for i in range(n)])]
    ppermute x20, starting transfers between devices: 55.5 us -> 69.3 us  [send(): self.got[name] = lax.ppermute(order(value), 'tensor', pairs)]
    ppermute x31 -> x27, starting transfers between devices: 17.3 us -> 21 us  [swap(): return lax.ppermute(value, axis, [(i, i ^ 1 << bit) for i in range(n)])]
  transfers between devices with their start and end apart: 74 -> 70, of which waited for: 26 -> 28; matrix products, arithmetic and copies ran while one was open for 8% -> 9% of each run, Pallas kernels for 21% -> 28%
where the time goes in v3:
time: 785 us; the launch traced here: 777 us
  Pallas kernels  292 us (37%)
  waiting for transfers between devices  243 us (31%)
  starting transfers between devices  119 us (15%)
  local copies, waits for them, and re-layouts  70.4 us (9%)
  other arithmetic  45.9 us (6%)
    pallas_call x25, Pallas kernels, prefetched(): pl.pallas_call(body, grid_spec=pltpu.PrefetchScalarGridSpec(num_scalar_pr...  217 us
    ppermute x20, waiting for transfers between devices, send(): self.pieces.append(lax.ppermute(order(self.pieces[piece]), 'tensor', pairs))  138 us
    pallas_call x4, Pallas kernels, kernel_call(): pl.pallas_call(run, grid=grid, in_specs=list(in_specs) + [ANY] * len(prev...  75.5 us
    ppermute x20, starting transfers between devices, send(): self.got[name] = lax.ppermute(order(value), 'tensor', pairs)  69.3 us
    ppermute x20, waiting for transfers between devices, send(): self.got[name] = lax.ppermute(order(value), 'tensor', pairs)  63.5 us
    unnamed x177, local copies, waits for them, and re-layouts  46.2 us
    ppermute x27, waiting for transfers between devices, swap(): return lax.ppermute(value, axis, [(i, i ^ 1 << bit) for i in range(n)])  35.3 us
    ppermute x20, starting transfers between devices, send(): self.pieces.append(lax.ppermute(order(self.pieces[piece]), 'tensor', pairs))  25.5 us
  transfers between devices with their start and end apart: 70, of which 28 were waited for; matrix products, arithmetic and copies ran while one was open for 9% of the time, Pallas kernels for 28%

profile of v3, /device:TPU:0, one launch (start us, length us, event | category | flops | bytes accessed | tf_op | source)
XLA Modules:
  0.0 776.6 jit_solution(3829530412918651869)
XLA Ops:
  19.6 11.7 %collective-permute-done.refs_1_ = bf16[1040,512]{1,0:T(8,128)(2,1)S(1)} collective-permute-done((bf16[1040,512]{1,0:T(8,128)(2,1)S(1)}, bf16[1040,512]{1,0:T(8,128)(2,1)S(1)}, u32[]{:S(2)}, u32[]{:S(2)}) %collective-permute-start) | collective-permute-done | bytes 1064992 | tf_op jit(solution)/shard_map/ppermute | solution.py:490
  43.8 16.1 %collective-permute-done.2.refs_3_ = bf16[1040,512]{1,0:T(8,128)(2,1)S(1)} collective-permute-done((bf16[1040,512]{1,0:T(8,128)(2,1)S(1)}, bf16[1040,512]{1,0:T(8,128)(2,1)S(1)}, u32[]{:S(2)}, u32[]{:S(2)}) %collective-permute-start.2) | collective-permute-done | bytes 1064992 | tf_op jit(solution)/shard_map/ppermute | solution.py:490
  63.2 23.6 %collective-permute-done.4.refs_5_ = bf16[1040,512]{1,0:T(8,128)(2,1)} collective-permute-done((bf16[1040,512]{1,0:T(8,128)(2,1)S(1)}, bf16[1040,512]{1,0:T(8,128)(2,1)}, u32[]{:S(2)}, u32[]{:S(2)}) %collective-permute-start.4) | collective-permute-done | bytes 1064992 | tf_op jit(solution)/shard_map/ppermute | solution.py:490
  104.4 14.2 %project.1 = (bf16[1024,2048]{1,0:T(8,128)(2,1)S(1)}, f32[1024,128]{1,0:T(8,128)S(1)}, bf16[3,1024,512]{2,1,0:T(8,128)(2,1)S(1)}) custom-call(bf16[1040,2048]{1,0:T(8,128)(2,1)S(1)} %copy-done.6, bf16[1040,2048]{1,0:T(8,128)(2,1)S(1)} %copy-done.6, bf16[3,2048,512]{2,1,0:T(8,128)(2,1)S(1)} %bitcast.53, f32[3,1,512]{2,1,0:T(1,128)S(1)} %copy.27.refs_3_, ...), custom_call_target="tpu_custom_call" | custom-call | tf_op jit(solution)/shard_map/project/pallas_call | solution.py:53
  119.4 16.9 %attend.1 = (bf16[1024,512]{1,0:T(8,128)(2,1)S(1)}, bf16[1024,1536]{1,0:T(8,128)(2,1)S(1)}, bf16[1024,512]{1,0:T(8,128)(2,1)S(1)}, f32[1024,512]{1,0:T(8,128)S(1)}) custom-call(s32[4]{0:T(128)S(1)} %pad_add_fusion.owners_ref, bf16[3,1024,512]{2,1,0:T(8,128)(2,1)S(1)} %get-tuple-element.172.q_ref.k_ref.v_ref.refs_0_.refs_1_.refs_2_, ...), custom_call_target="tpu_custom_call" | custom-call | tf_op jit(solution)/shard_map/attend/pallas_call | solution.py:76
  149.1 11.6 %collective-permute-done.7 = bf16[1024,512]{1,0:T(8,128)(2,1)S(1)} collective-permute-done((bf16[1024,512]{1,0:T(8,128)(2,1)S(1)}, bf16[1024,512]{1,0:T(8,128)(2,1)S(1)}, u32[]{:S(2)}, u32[]{:S(2)}) %collective-permute-start.7) | collective-permute-done | bytes 1048608 | tf_op jit(solution)/shard_map/ppermute | solution.py:569
  178.6 14.8 %collective-permute-done.11.refs_5_ = bf16[1024,512]{1,0:T(8,128)(2,1)} collective-permute-done((bf16[1024,512]{1,0:T(8,128)(2,1)}, bf16[1024,512]{1,0:T(8,128)(2,1)}, u32[]{:S(2)}, u32[]{:S(2)}) %collective-permute-start.11) | collective-permute-done | bytes 1048608 | tf_op jit(solution)/shard_map/ppermute | solution.py:490
  206.2 16.6 %collective-permute-done.13 = bf16[1024,512]{1,0:T(8,128)(2,1)} collective-permute-done((bf16[1024,512]{1,0:T(8,128)(2,1)}, bf16[1024,512]{1,0:T(8,128)(2,1)}, u32[]{:S(2)}, u32[]{:S(2)}) %collective-permute-start.13) | collective-permute-done | bytes 1048608 | tf_op jit(solution)/shard_map/ppermute | solution.py:569
  227.8 16.4 %collective-permute-done.15.refs_1_ = bf16[1024,512]{1,0:T(8,128)(2,1)S(1)} collective-permute-done((bf16[1024,512]{1,0:T(8,128)(2,1)S(1)}, bf16[1024,512]{1,0:T(8,128)(2,1)S(1)}, u32[]{:S(2)}, u32[]{:S(2)}) %collective-permute-start.15) | collective-permute-done | bytes 1048608 | tf_op jit(solution)/shard_map/ppermute | solution.py:490
  254.3 12.4 %collective-permute-done.17.refs_3_ = bf16[1024,512]{1,0:T(8,128)(2,1)S(1)} collective-permute-done((bf16[1024,512]{1,0:T(8,128)(2,1)S(1)}, bf16[1024,512]{1,0:T(8,128)(2,1)S(1)}, u32[]{:S(2)}, u32[]{:S(2)}) %collective-permute-start.17) | collective-permute-done | bytes 1048608 | tf_op jit(solution)/shard_map/ppermute | solution.py:490
  266.7 21.9 %collective-permute-done.19.refs_5_ = bf16[1024,512]{1,0:T(8,128)(2,1)S(1)} collective-permute-done((bf16[1024,512]{1,0:T(8,128)(2,1)S(1)}, bf16[1024,512]{1,0:T(8,128)(2,1)S(1)}, u32[]{:S(2)}, u32[]{:S(2)}) %collective-permute-start.19) | collective-permute-done | bytes 1048608 | tf_op jit(solution)/shard_map/ppermute | solution.py:490
  291.4 32.3 %mlp.1 = (bf16[1024,2048]{1,0:T(8,128)(2,1)}, f32[1024,128]{1,0:T(8,128)S(1)}, bf16[1024,1408]{1,0:T(8,128)(2,1)S(1)}, bf16[1024,1408]{1,0:T(8,128)(2,1)S(1)}, bf16[1024,1408]{1,0:T(8,128)(2,1)}) custom-call(bf16[1024,2048]{1,0:T(8,128)(2,1)} %copy-done.3, bf16[1024,2048]{1,0:T(8,128)(2,1)} %copy-done, f32[1,2048]{1,0:T(1,128)S(1)} %get-tuple-element.329.refs_2_, ...), custom_call_target="tpu_custom_call" | custom-call | tf_op jit(solution)/shard_map/mlp/pallas_call | solution.py:53
  337.7 15.7 %mlp_back.3 = bf16[1024,1536]{1,0:T(8,128)(2,1)} custom-call(s32[3]{0:T(128)} %pad_add_fusion.1.owners_ref, bf16[1024,1408]{1,0:T(8,128)(2,1)} %copy-done.9, bf16[1024,1408]{1,0:T(8,128)(2,1)} %get-tuple-element.195.dup_ref.refs_3_, bf16[2048,1408]{1,0:T(8,128)(2,1)} %bitcast.60, bf16[2048,1408]{1,0:T(8,128)(2,1)} %slice_bitcast_fusion.refs_5_.up_w_ref), custom_call_target="tpu_custom_call" | custom-call | tf_op jit(solution)/shard_map/mlp_back/pallas_call | solution.py:76
  364.5 15.6 %mlp_given.1 = (bf16[1024,1408]{1,0:T(8,128)(2,1)}, bf16[1024,1408]{1,0:T(8,128)(2,1)}, bf16[1024,1408]{1,0:T(8,128)(2,1)}) custom-call(s32[1]{0:T(128)} %bitcast.12.which_ref, bf16[1024,2048]{1,0:T(8,128)(2,1)} %get-tuple-element.201.refs_0_, bf16[1024,2048]{1,0:T(8,128)(2,1)} %copy-done, bf16[1024,1408]{1,0:T(8,128)(2,1)} %copy-done.9, ...), custom_call_target="tpu_custom_call" | custom-call | tf_op jit(solution)/shard_map/mlp_given/pallas_call | solution.py:76
  387.5 15.4 %mlp_kept.1 = (bf16[1024,1408]{1,0:T(8,128)(2,1)}, bf16[1024,1408]{1,0:T(8,128)(2,1)}, bf16[1024,1408]{1,0:T(8,128)(2,1)}) custom-call(s32[1]{0:T(128)} %bitcast.13.which_ref.core_ref, bf16[1024,2048]{1,0:T(8,128)(2,1)} %get-tuple-element.201.refs_0_, bf16[1024,2048]{1,0:T(8,128)(2,1)} %copy-done, bf16[1024,1408]{1,0:T(8,128)(2,1)} %copy-done.9, ...), custom_call_target="tpu_custom_call" | custom-call | flops 30000001024 | tf_op jit(solution)/shard_map/mlp_kept/pallas_call | solution.py:76
  413.2 10.7 %split.4 = (bf16[256,4224]{1,0:T(8,128)(2,1)}, bf16[256,4224]{1,0:T(8,128)(2,1)}, bf16[256,4224]{1,0:T(8,128)(2,1)}, bf16[256,4224]{1,0:T(8,128)(2,1)}) custom-call(s32[2]{0:T(128)} %pad_add_fusion.2.bits_ref, bf16[1024,1408]{1,0:T(8,128)(2,1)} %get-tuple-element.217.refs_0_.refs_6_, bf16[1024,1408]{1,0:T(8,128)(2,1)} %collective-permute-done.27.refs_1_.refs_7_, ...), custom_call_target="tpu_custom_call" | custom-call | tf_op jit(solution)/shard_map/split/pallas_call | solution.py:76
  438.7 9.8 %mlp_out.1 = (bf16[1024,512]{1,0:T(8,128)(2,1)}, bf16[1024,1536]{1,0:T(8,128)(2,1)S(1)}) custom-call(s32[4]{0:T(128)S(1)} %pad_add_fusion.owners_ref, bf16[1024,1408]{1,0:T(8,128)(2,1)S(1)} %copy-done.34, bf16[1408,2048]{1,0:T(8,128)(2,1)S(1)} %bitcast.57), custom_call_target="tpu_custom_call" | custom-call | flops 10000000000 | tf_op jit(solution)/shard_map/mlp_out/pallas_call | solution.py:76
  512.6 21.2 %attend_back.1 = (bf16[1024,512]{1,0:T(8,128)(2,1)S(1)}, bf16[1024,512]{1,0:T(8,128)(2,1)S(1)}, bf16[1024,512]{1,0:T(8,128)(2,1)S(1)}, f32[8,1024]{1,0:T(8,128)S(1)}) custom-call(bf16[3,1024,512]{2,1,0:T(8,128)(2,1)S(1)} %copy-done.8, bf16[3,1024,512]{2,1,0:T(8,128)(2,1)S(1)} %copy-done.8, bf16[3,1024,512]{2,1,0:T(8,128)(2,1)S(1)} %copy-done.8, ...), custom_call_target="tpu_custom_call" | custom-call | flops 20000000000 | tf_op jit(solution)/shard_map/attend_back/pallas_call | solution.py:53
  549.5 10.5 %project_back.3 = bf16[1040,1536]{1,0:T(8,128)(2,1)} custom-call(s32[3]{0:T(128)} %pad_add_fusion.1.owners_ref, bf16[1024,512]{1,0:T(8,128)(2,1)} %copy-done.16, bf16[1024,512]{1,0:T(8,128)(2,1)} %copy-done.14, bf16[1024,512]{1,0:T(8,128)(2,1)} %copy-done.12, bf16[3,2048,512]{2,1,0:T(8,128)(2,1)} %bitcast.52, bf16[1040,2048]{1,0:T(8,128)(2,1)} %copy-done.5, ...), custom_call_target="tpu_custom_call" | custom-call | flops 5000000000 | tf_op jit(solution)/shard_map/project_back/pallas_call | solution.py:76
  581.4 12.5 %collective-permute-done.42 = bf16[1040,512]{1,0:T(8,128)(2,1)} collective-permute-done((bf16[1040,512]{1,0:T(8,128)(2,1)}, bf16[1040,512]{1,0:T(8,128)(2,1)}, u32[]{:S(2)}, u32[]{:S(2)}) %collective-permute-start.42) | collective-permute-done | bytes 1064992 | tf_op jit(solution)/shard_map/ppermute | solution.py:569
  662.5 13.6 %collective-permute-done.53 = bf16[1040,512]{1,0:T(8,128)(2,1)S(1)} collective-permute-done((bf16[1040,512]{1,0:T(8,128)(2,1)S(1)}, bf16[1040,512]{1,0:T(8,128)(2,1)S(1)}, u32[]{:S(2)}, u32[]{:S(2)}) %collective-permute-start.53) | collective-permute-done | bytes 1064992 | tf_op jit(solution)/shard_map/ppermute | solution.py:569
  695.1 17.4 %gate_up_out.1 = f32[2048,2,1408]{2,1,0:T(2,128)} custom-call(s32[1]{0:T(128)} %bitcast.13.which_ref.core_ref, bf16[1024,1408]{1,0:T(8,128)(2,1)} %bitcast.63, bf16[1024,1408]{1,0:T(8,128)(2,1)} %bitcast.65, bf16[1024,1408]{1,0:T(8,128)(2,1)} %collective-permute-done.57.refs_2_, bf16[1024,1408]{1,0:T(8,128)(2,1)} %collective-permute-done.58.refs_3_), custom_call_target="tpu_custom_call" | custom-call | tf_op jit(solution)/shard_map/gate_up_out/pallas_call | solution.py:76
  745.6 13.1 %down_out.1 = f32[1408,2048]{1,0:T(8,128)} custom-call(s32[1]{0:T(128)} %bitcast.13.which_ref.core_ref, bf16[1024,1408]{1,0:T(8,128)(2,1)} %bitcast.24.refs_0_, bf16[1024,1408]{1,0:T(8,128)(2,1)} %collective-permute-done.63.refs_1_), custom_call_target="tpu_custom_call" | custom-call | tf_op jit(solution)/shard_map/down_out/pallas_call | solution.py:76
  765.0 11.1 %attention_out.1 = (f32[3,2048,512]{2,1,0:T(8,128)}, f32[512,2048]{1,0:T(8,128)}) custom-call(s32[1]{0:T(128)} %bitcast.13.which_ref.core_ref, bf16[1024,1024]{1,0:T(8,128)(2,1)} %bitcast.67, bf16[1024,1024]{1,0:T(8,128)(2,1)} %bitcast.69, bf16[1024,1024]{1,0:T(8,128)(2,1)} %collective-permute-done.68.refs_2_, bf16[1024,1024]{1,0:T(8,128)(2,1)} %collective-permute-done.69.refs_3_), custom_call_target="tpu_custom_call" | custom-call | tf_op jit(solution)/shard_map/attention_out/pallas_call | solution.py:76
  (390 shorter events, 399.3 us)
Async XLA Ops:
  31.3 28.7 %collective-permute-start.2 = (bf16[1040,512]{1,0:T(8,128)(2,1)S(1)}, bf16[1040,512]{1,0:T(8,128)(2,1)S(1)}, u32[]{:S(2)}, u32[]{:S(2)}) collective-permute-start(bf16[1040,512]{1,0:T(8,128)(2,1)S(1)} %collective-permute-done.1.refs_2_), channel_id=1, source_target_pairs={{1,0},{2,3},{5,4},{6,7},{9,8},{10,11},{13,12},{14,15},{17,16},{18,... | collective-permute-start | bytes 3194888 | tf_op jit(solution)/shard_map/ppermute | solution.py:490
  32.6 28.3 %collective-permute-start.3 = (bf16[1040,512]{1,0:T(8,128)(2,1)S(1)}, bf16[1040,512]{1,0:T(8,128)(2,1)S(1)}, u32[]{:S(2)}, u32[]{:S(2)}) collective-permute-start(bf16[1040,512]{1,0:T(8,128)(2,1)S(1)} %collective-permute-done.refs_1_), channel_id=1, source_target_pairs={{1,2},{2,1},{5,6},{6,5},{9,10},{10,9},{13,14},{14,13},{17,18},{18,... | collective-permute-start | bytes 3194888 | tf_op jit(solution)/shard_map/ppermute | solution.py:490
  246.7 41.9 %collective-permute-start.19 = (bf16[1024,512]{1,0:T(8,128)(2,1)S(1)}, bf16[1024,512]{1,0:T(8,128)(2,1)S(1)}, u32[]{:S(2)}, u32[]{:S(2)}) collective-permute-start(bf16[1024,512]{1,0:T(8,128)(2,1)S(1)} %collective-permute-done.18.refs_4_), channel_id=1, source_target_pairs={{1,0},{2,3},{5,4},{6,7},{9,8},{10,11},{13,12},{14,15},{17,16},{18,... | collective-permute-start | bytes 3145736 | tf_op jit(solution)/shard_map/ppermute | solution.py:490
  380.0 33.2 %collective-permute-start.27 = (bf16[1024,1408]{1,0:T(8,128)(2,1)}, bf16[1024,1408]{1,0:T(8,128)(2,1)}, u32[]{:S(2)}, u32[]{:S(2)}) collective-permute-start(bf16[1024,1408]{1,0:T(8,128)(2,1)} %get-tuple-element.203), channel_id=1, source_target_pairs={{0,4},{4,0},{8,12},{12,8},{16,20},{20,16},{24,28},{28,24},{1,5},{5... | collective-permute-start | bytes 8650760 | tf_op jit(solution)/shard_map/ppermute | solution.py:683
  380.0 33.2 %collective-permute-start.28 = (bf16[1024,1408]{1,0:T(8,128)(2,1)}, bf16[1024,1408]{1,0:T(8,128)(2,1)}, u32[]{:S(2)}, u32[]{:S(2)}) collective-permute-start(bf16[1024,1408]{1,0:T(8,128)(2,1)} %get-tuple-element.204), channel_id=1, source_target_pairs={{0,4},{4,0},{8,12},{12,8},{16,20},{20,16},{24,28},{28,24},{1,5},{5... | collective-permute-start | bytes 8650760 | tf_op jit(solution)/shard_map/ppermute | solution.py:683
  380.5 32.7 %collective-permute-start.29 = (bf16[1024,1408]{1,0:T(8,128)(2,1)}, bf16[1024,1408]{1,0:T(8,128)(2,1)}, u32[]{:S(2)}, u32[]{:S(2)}) collective-permute-start(bf16[1024,1408]{1,0:T(8,128)(2,1)} %get-tuple-element.205), channel_id=1, source_target_pairs={{0,4},{4,0},{8,12},{12,8},{16,20},{20,16},{24,28},{28,24},{1,5},{5... | collective-permute-start | bytes 8650760 | tf_op jit(solution)/shard_map/ppermute | solution.py:683
  423.9 47.1 %collective-permute-start.34 = (bf16[256,4224]{1,0:T(8,128)(2,1)}, bf16[256,4224]{1,0:T(8,128)(2,1)S(1)}, u32[]{:S(2)}, u32[]{:S(2)}) collective-permute-start(bf16[256,4224]{1,0:T(8,128)(2,1)} %get-tuple-element.229), channel_id=1, source_target_pairs={{0,8},{4,12},{8,0},{12,4},{16,24},{20,28},{24,16},{28,20},{1,9},{5... | collective-permute-start | bytes 6488072 | tf_op jit(solution)/shard_map/ppermute | solution.py:683
  425.5 46.9 %collective-permute-start.35 = (bf16[256,4224]{1,0:T(8,128)(2,1)}, bf16[256,4224]{1,0:T(8,128)(2,1)}, u32[]{:S(2)}, u32[]{:S(2)}) collective-permute-start(bf16[256,4224]{1,0:T(8,128)(2,1)} %get-tuple-element.232), channel_id=1, source_target_pairs={{0,16},{4,20},{8,24},{12,28},{16,0},{20,4},{24,8},{28,12},{1,17},{... | collective-permute-start | bytes 6488072 | tf_op jit(solution)/shard_map/ppermute | solution.py:683
  479.3 29.4 %collective-permute-start.37 = (bf16[128,4224]{1,0:T(8,128)(2,1)}, bf16[128,4224]{1,0:T(8,128)(2,1)S(1)}, u32[]{:S(2)}, u32[]{:S(2)}) collective-permute-start(bf16[128,4224]{1,0:T(8,128)(2,1)} %get-tuple-element.243), channel_id=1, source_target_pairs={{0,16},{4,20},{8,24},{12,28},{16,0},{20,4},{24,8},{28,12},{1,17},{... | collective-permute-start | bytes 3244040 | tf_op jit(solution)/shard_map/ppermute | solution.py:683
  500.7 43.1 %collective-permute-start.36 = (bf16[1024,512]{1,0:T(8,128)(2,1)}, bf16[1024,512]{1,0:T(8,128)(2,1)}, u32[]{:S(2)}, u32[]{:S(2)}) collective-permute-start(bf16[1024,512]{1,0:T(8,128)(2,1)} %add_convert_fusion.8), channel_id=1, source_target_pairs={{1,2},{2,1},{5,6},{6,5},{9,10},{10,9},{13,14},{14,13},{17,18},{18,... | collective-permute-start | bytes 3145736 | tf_op jit(solution)/shard_map/ppermute | solution.py:569
  502.3 41.4 %collective-permute-start.41 = (bf16[1024,512]{1,0:T(8,128)(2,1)}, bf16[1024,512]{1,0:T(8,128)(2,1)}, u32[]{:S(2)}, u32[]{:S(2)}) collective-permute-start(bf16[1024,512]{1,0:T(8,128)(2,1)} %constant_dynamic-slice_fusion.1), channel_id=1, source_target_pairs={{0,1},{3,2},{4,5},{7,6},{8,9},{11,10},{12,13},{15,14},{16,17},{19,... | collective-permute-start | bytes 3145736 | tf_op jit(solution)/shard_map/ppermute | solution.py:569
  542.5 73.4 %collective-permute-start.45 = (bf16[256,4224]{1,0:T(8,128)(2,1)}, bf16[256,4224]{1,0:T(8,128)(2,1)}, u32[]{:S(2)}, u32[]{:S(2)}) collective-permute-start(bf16[256,4224]{1,0:T(8,128)(2,1)} %get-tuple-element.269.refs_0_), channel_id=1, source_target_pairs={{0,8},{4,12},{8,0},{12,4},{16,24},{20,28},{24,16},{28,20},{1,9},{5... | collective-permute-start | bytes 6488072 | tf_op jit(solution)/shard_map/ppermute | solution.py:683
  568.6 32.1 %collective-permute-start.43 = (bf16[1024,1024]{1,0:T(8,128)(2,1)}, bf16[1024,1024]{1,0:T(8,128)(2,1)S(1)}, u32[]{:S(2)}, u32[]{:S(2)}) collective-permute-start(bf16[1024,1024]{1,0:T(8,128)(2,1)} %get-tuple-element.260), channel_id=1, source_target_pairs={{0,4},{4,0},{8,12},{12,8},{16,20},{20,16},{24,28},{28,24},{1,5},{5... | collective-permute-start | bytes 6291464 | tf_op jit(solution)/shard_map/ppermute | solution.py:683
  568.6 38.3 %collective-permute-start.44 = (bf16[1024,1024]{1,0:T(8,128)(2,1)}, bf16[1024,1024]{1,0:T(8,128)(2,1)S(1)}, u32[]{:S(2)}, u32[]{:S(2)}) collective-permute-start(bf16[1024,1024]{1,0:T(8,128)(2,1)} %get-tuple-element.261), channel_id=1, source_target_pairs={{0,4},{4,0},{8,12},{12,8},{16,20},{20,16},{24,28},{28,24},{1,5},{5... | collective-permute-start | bytes 6291464 | tf_op jit(solution)/shard_map/ppermute | solution.py:683
  571.4 50.2 %collective-permute-start.46 = (bf16[256,4224]{1,0:T(8,128)(2,1)}, bf16[256,4224]{1,0:T(8,128)(2,1)}, u32[]{:S(2)}, u32[]{:S(2)}) collective-permute-start(bf16[256,4224]{1,0:T(8,128)(2,1)} %get-tuple-element.270.refs_2_), channel_id=1, source_target_pairs={{0,16},{4,20},{8,24},{12,28},{16,0},{20,4},{24,8},{28,12},{1,17},{... | collective-permute-start | bytes 6488072 | tf_op jit(solution)/shard_map/ppermute | solution.py:683
  596.8 33.2 %collective-permute-start.47 = (bf16[1040,512]{1,0:T(8,128)(2,1)}, bf16[1040,512]{1,0:T(8,128)(2,1)}, u32[]{:S(2)}, u32[]{:S(2)}) collective-permute-start(bf16[1040,512]{1,0:T(8,128)(2,1)} %add_convert_fusion.4), channel_id=1, source_target_pairs={{1,2},{2,1},{5,6},{6,5},{9,10},{10,9},{13,14},{14,13},{17,18},{18,... | collective-permute-start | bytes 3194888 | tf_op jit(solution)/shard_map/ppermute | solution.py:569
  600.8 29.7 %collective-permute-start.48 = (bf16[1040,512]{1,0:T(8,128)(2,1)}, bf16[1040,512]{1,0:T(8,128)(2,1)}, u32[]{:S(2)}, u32[]{:S(2)}) collective-permute-start(bf16[1040,512]{1,0:T(8,128)(2,1)} %constant_dynamic-slice_fusion), channel_id=1, source_target_pairs={{0,1},{3,2},{4,5},{7,6},{8,9},{11,10},{12,13},{15,14},{16,17},{19,... | collective-permute-start | bytes 3194888 | tf_op jit(solution)/shard_map/ppermute | solution.py:569
  629.9 65.1 %collective-permute-start.57 = (bf16[1024,1408]{1,0:T(8,128)(2,1)}, bf16[1024,1408]{1,0:T(8,128)(2,1)}, u32[]{:S(2)}, u32[]{:S(2)}) collective-permute-start(bf16[1024,1408]{1,0:T(8,128)(2,1)} %bitcast.62), channel_id=1, source_target_pairs={{0,4},{4,0},{8,12},{12,8},{16,20},{20,16},{24,28},{28,24},{1,5},{5... | collective-permute-start | bytes 8650760 | tf_op jit(solution)/shard_map/ppermute | solution.py:683
  630.0 65.1 %collective-permute-start.58 = (bf16[1024,1408]{1,0:T(8,128)(2,1)}, bf16[1024,1408]{1,0:T(8,128)(2,1)}, u32[]{:S(2)}, u32[]{:S(2)}) collective-permute-start(bf16[1024,1408]{1,0:T(8,128)(2,1)} %bitcast.64), channel_id=1, source_target_pairs={{0,4},{4,0},{8,12},{12,8},{16,20},{20,16},{24,28},{28,24},{1,5},{5... | collective-permute-start | bytes 8650760 | tf_op jit(solution)/shard_map/ppermute | solution.py:683
  662.1 73.8 %collective-permute-start.63 = (bf16[1024,1408]{1,0:T(8,128)(2,1)}, bf16[1024,1408]{1,0:T(8,128)(2,1)}, u32[]{:S(2)}, u32[]{:S(2)}) collective-permute-start(bf16[1024,1408]{1,0:T(8,128)(2,1)} %bitcast.24.refs_0_), channel_id=1, source_target_pairs={{0,4},{4,0},{8,12},{12,8},{16,20},{20,16},{24,28},{28,24},{1,5},{5... | collective-permute-start | bytes 8650760 | tf_op jit(solution)/shard_map/ppermute | solution.py:683
  722.8 42.2 %collective-permute-start.68 = (bf16[1024,1024]{1,0:T(8,128)(2,1)}, bf16[1024,1024]{1,0:T(8,128)(2,1)}, u32[]{:S(2)}, u32[]{:S(2)}) collective-permute-start(bf16[1024,1024]{1,0:T(8,128)(2,1)} %bitcast.66), channel_id=1, source_target_pairs={{0,4},{4,0},{8,12},{12,8},{16,20},{20,16},{24,28},{28,24},{1,5},{5... | collective-permute-start | bytes 6291464 | tf_op jit(solution)/shard_map/ppermute | solution.py:683
  722.9 42.1 %collective-permute-start.69 = (bf16[1024,1024]{1,0:T(8,128)(2,1)}, bf16[1024,1024]{1,0:T(8,128)(2,1)}, u32[]{:S(2)}, u32[]{:S(2)}) collective-permute-start(bf16[1024,1024]{1,0:T(8,128)(2,1)} %bitcast.68), channel_id=1, source_target_pairs={{0,4},{4,0},{8,12},{12,8},{16,20},{20,16},{24,28},{28,24},{1,5},{5... | collective-permute-start | bytes 6291464 | tf_op jit(solution)/shard_map/ppermute | solution.py:683
  726.7 33.2 %collective-permute-start.64 = (bf16[1024,512]{1,0:T(8,128)(2,1)}, bf16[1024,512]{1,0:T(8,128)(2,1)}, u32[]{:S(2)}, u32[]{:S(2)}) collective-permute-start(bf16[1024,512]{1,0:T(8,128)(2,1)} %get-tuple-element.307), channel_id=1, source_target_pairs={{1,2},{2,1},{5,6},{6,5},{9,10},{10,9},{13,14},{14,13},{17,18},{18,... | collective-permute-start | bytes 3145736 | tf_op jit(solution)/shard_map/ppermute | solution.py:569
  728.4 31.5 %collective-permute-start.62 = (bf16[1024,512]{1,0:T(8,128)(2,1)}, bf16[1024,512]{1,0:T(8,128)(2,1)}, u32[]{:S(2)}, u32[]{:S(2)}) collective-permute-start(bf16[1024,512]{1,0:T(8,128)(2,1)} %get-tuple-element.302), channel_id=1, source_target_pairs={{0,1},{1,0},{2,3},{3,2},{4,5},{5,4},{6,7},{7,6},{8,9},{9,8},{10,11... | collective-permute-start | bytes 3145736 | tf_op jit(solution)/shard_map/ppermute | solution.py:569
  (134 other events, 1824.0 us)

commit v4 on v3

--- a/solution.py
+++ b/solution.py
@@ -14,7 +14,7 @@
 PAIR = 2 * HEAD_DIM
 CHUNKS = 1
 SUB = 256
-WEIGHTS = {"mlp_kept": 30, "mlp_out": 10, "project_back": 5, "attend_back": 20}
+WEIGHTS = {"mlp_kept": 30, "mlp_out": 10, "attend_back": 20, "attention_kept": 40}
 EXTRA = 16
 
 EPSILON = 1e-05
@@ -459,7 +459,7 @@
         ],
         [sds((t + EXTRA, count * width), BF)],
         [pl.BlockSpec((t + EXTRA, width), lambda j, owners: (0, j))],
-        mib=56,
+        mib=34,
         name="project_back",
     )[0]
 
@@ -640,7 +640,7 @@
         + [still(right.shape, lambda i, which: (0, 0)) for right in rights],
         [sds((D // 2, wide), BF)] * (len(rights) // join),
         [pl.BlockSpec((block, wide), lambda i, which: (i, 0))] * (len(rights) // join),
-        mib=56,
+        mib=30 if join > 1 else 56,
         name=name,
     )
 
@@ -726,7 +726,7 @@
         in_specs,
         [sds((rows, columns), BF)] * 4,
         [given, kept] * 2,
-        mib=56,
+        mib=56 if groups > 2 else 28,
         name="split",
     )
 
@@ -876,16 +876,16 @@
 def attention_out(core, own, other):
     def store(arrays, outs):
         for k in range(3):
-            outs[0][k] = arrays[k // 2][:, k % 2 * width : (k % 2 + 1) * width].astype(F32)
-        outs[1][...] = arrays[1][:, width:].astype(F32).T
-
-    width, block = own[0].shape[1] // 2, 256
+            outs[0][k] = arrays[0][:, k * width : (k + 1) * width].astype(F32)
+        outs[1][...] = arrays[0][:, 3 * width :].astype(F32).T
+
+    width, block = own[0].shape[1] // 4, 256
     outs = [sds((3, D, width), F32), sds((width, D), F32)]
     specs = [
         pl.BlockSpec((3, block, width), lambda i, c: (0, i, 0)),
         pl.BlockSpec((width, block), lambda i, c: (0, i)),
     ]
-    return from_halves(store, core, own, other, outs, specs, block, 56, "attention_out")
+    return from_halves(store, core, own, other, outs, specs, block, 22, "attention_out")
 
 
 def per_device(
@@ -1007,15 +1007,15 @@
     got = steps(order, delta_one)
     order.done(rest)
     attention_grads = lambda which, name: gradients(
-        which, [(normed_one, [order(dq), dk, dv]), (dbranch, [context])], name, join=2
+        which, [(normed_one, [order(dq), dk, dv]), (dbranch, [context])], name, join=4
     )
     attention_given = attention_grads(1 - core, "attention_given")
     attention_sum = sum_over_dp(attention_given, order)
     next(attention_sum)
-    order.done(*attention_given)
+    order.done(*attention_given, *got)
+    got = steps(order, delta_one)
     attention_kept = attention_grads(core, "attention_kept")
-    order.done(*attention_kept, *got)
-    got = steps(order, delta_one)
+    order.done(*attention_kept)
     held = attention_sum.send(attention_kept)
     order.done(held)
     held = next(mlp_sum)
@@ -1031,6 +1031,7 @@
             order.done(next(attention_sum))
     held = next(attention_sum)
     order.done(held)
+    share_got = finish(order, mlp_share)
     mlp_halves = next(mlp_sum)
     gate_up_grad = gate_up_out(core, [order(mlp_halves[0][0]), mlp_halves[0][1]], mlp_halves[1][:2])
     order.done(gate_up_grad)
@@ -1038,21 +1039,20 @@
     bias_grad = [jnp.sum(a, axis=0, dtype=F32) for a in delta_heads]
     small = jnp.stack([delta_one[t], delta_one[t + 1], *two_grads, *bias_grad])
     small = small + swap(small, 0)
-    order.done(small)
+    sums = (delta_one[t + 2 : t + 2 + sum_rows] / D).reshape(2, t).T
+    unit_one = (tokens.astype(F32) - stats_one[:, 0:1]) * stats_one[:, 1:2]
+    dmid = cotangent.astype(F32) + stats_two[:, 1:2] * (e_own - means_two[:, 0:1] - unit_two * means_two[:, 1:2])
+    tokens_grad = order(dmid) + stats_one[:, 1:2] * (
+        delta_one[:t] * norm_one_gain.astype(F32) - sums[:, 0:1] - unit_one * sums[:, 1:2]
+    )
+    order.done(small, tokens_grad, *share_got)
     held = next(attention_sum)
     order.done(held)
-    finish(order, mlp_share)
     devices = lax.axis_size("dp")
     others = [lax.ppermute(order(small), "dp", [(i, i ^ k) for i in range(devices)]) for k in range(2, devices, 2)]
     down_grad = down_out(core, [order(mlp_halves[0][2])], mlp_halves[1][2:])
     order.done(down_grad)
     result = (middle_share + mlp_share.total(order)).astype(BF)
-    sums = (delta_one[t + 2 : t + 2 + sum_rows] / D).reshape(2, t).T
-    unit_one = (tokens.astype(F32) - stats_one[:, 0:1]) * stats_one[:, 1:2]
-    dmid = cotangent.astype(F32) + stats_two[:, 1:2] * (e_own - means_two[:, 0:1] - unit_two * means_two[:, 1:2])
-    tokens_grad = order(dmid) + stats_one[:, 1:2] * (
-        delta_one[:t] * norm_one_gain.astype(F32) - sums[:, 0:1] - unit_one * sums[:, 1:2]
-    )
     small = sum((order(other) for other in others), small)
     order.done(tokens_grad, small, result)
     attention_halves = next(attention_sum)

time: 785 us -> 774 us (0.986)
  waiting for transfers between devices: 243 us -> 272 us
  Pallas kernels: 292 us -> 265 us
  starting transfers between devices: 119 us -> 103 us
    ppermute x20, waiting for transfers between devices: 138 us -> 172 us  [send(): self.pieces.append(lax.ppermute(order(self.pieces[piece]), 'tensor', pairs))]
    pallas_call x25, Pallas kernels: 217 us -> 190 us  [prefetched(): pl.pallas_call(body, grid_spec=pltpu.PrefetchScalarGridSpec(num_scalar_pr...]
    ppermute x27 -> x25, waiting for transfers between devices: 35.3 us -> 61.5 us  [swap(): return lax.ppermute(value, axis, [(i, i ^ 1 << bit) for i in range(n)])]
    ppermute x20, waiting for transfers between devices: 63.5 us -> 38.8 us  [send(): self.got[name] = lax.ppermute(order(value), 'tensor', pairs)]
    ppermute x20, starting transfers between devices: 69.3 us -> 51.4 us  [send(): self.got[name] = lax.ppermute(order(value), 'tensor', pairs)]
    unnamed x177 -> x195, local copies, waits for them, and re-layouts: 46.2 us -> 49.9 us
    ppermute x27 -> x25, starting transfers between devices: 21 us -> 17.7 us  [swap(): return lax.ppermute(value, axis, [(i, i ^ 1 << bit) for i in range(n)])]
  transfers between devices with their start and end apart: 70 -> 68, of which waited for: 28 -> 25; matrix products, arithmetic and copies ran while one was open for 9% -> 8% of each run, Pallas kernels for 28% -> 25%
where the time goes in v4:
time: 774 us; the launch traced here: 766 us
  waiting for transfers between devices  272 us (35%)
  Pallas kernels  265 us (34%)
  starting transfers between devices  103 us (13%)
  local copies, waits for them, and re-layouts  75.3 us (10%)
  other arithmetic  45.1 us (6%)
    pallas_call x25, Pallas kernels, prefetched(): pl.pallas_call(body, grid_spec=pltpu.PrefetchScalarGridSpec(num_scalar_pr...  190 us
    ppermute x20, waiting for transfers between devices, send(): self.pieces.append(lax.ppermute(order(self.pieces[piece]), 'tensor', pairs))  172 us
    pallas_call x4, Pallas kernels, kernel_call(): pl.pallas_call(run, grid=grid, in_specs=list(in_specs) + [ANY] * len(prev...  75.5 us
    ppermute x25, waiting for transfers between devices, swap(): return lax.ppermute(value, axis, [(i, i ^ 1 << bit) for i in range(n)])  61.5 us
    ppermute x20, starting transfers between devices, send(): self.got[name] = lax.ppermute(order(value), 'tensor', pairs)  51.4 us
    unnamed x195, local copies, waits for them, and re-layouts  49.9 us
    ppermute x20, waiting for transfers between devices, send(): self.got[name] = lax.ppermute(order(value), 'tensor', pairs)  38.8 us
    ppermute x20, starting transfers between devices, send(): self.pieces.append(lax.ppermute(order(self.pieces[piece]), 'tensor', pairs))  30.2 us
  transfers between devices with their start and end apart: 68, of which 25 were waited for; matrix products, arithmetic and copies ran while one was open for 8% of the time, Pallas kernels for 25%

profile of v4, /device:TPU:0, one launch (start us, length us, event | category | flops | bytes accessed | tf_op | source)
XLA Modules:
  0.0 766.1 jit_solution(4966273829225062629)
XLA Ops:
  19.6 11.7 %collective-permute-done.refs_1_ = bf16[1040,512]{1,0:T(8,128)(2,1)S(1)} collective-permute-done((bf16[1040,512]{1,0:T(8,128)(2,1)S(1)}, bf16[1040,512]{1,0:T(8,128)(2,1)S(1)}, u32[]{:S(2)}, u32[]{:S(2)}) %collective-permute-start) | collective-permute-done | bytes 1064992 | tf_op jit(solution)/shard_map/ppermute | solution.py:490
  44.6 26.3 %collective-permute-done.2.refs_3_ = bf16[1040,512]{1,0:T(8,128)(2,1)S(1)} collective-permute-done((bf16[1040,512]{1,0:T(8,128)(2,1)S(1)}, bf16[1040,512]{1,0:T(8,128)(2,1)S(1)}, u32[]{:S(2)}, u32[]{:S(2)}) %collective-permute-start.2) | collective-permute-done | bytes 1064992 | tf_op jit(solution)/shard_map/ppermute | solution.py:490
  74.2 22.8 %collective-permute-done.4.refs_5_ = bf16[1040,512]{1,0:T(8,128)(2,1)} collective-permute-done((bf16[1040,512]{1,0:T(8,128)(2,1)S(1)}, bf16[1040,512]{1,0:T(8,128)(2,1)}, u32[]{:S(2)}, u32[]{:S(2)}) %collective-permute-start.4) | collective-permute-done | bytes 1064992 | tf_op jit(solution)/shard_map/ppermute | solution.py:490
  114.8 14.2 %project.1 = (bf16[1024,2048]{1,0:T(8,128)(2,1)S(1)}, f32[1024,128]{1,0:T(8,128)S(1)}, bf16[3,1024,512]{2,1,0:T(8,128)(2,1)S(1)}) custom-call(bf16[1040,2048]{1,0:T(8,128)(2,1)S(1)} %copy-done.3, bf16[1040,2048]{1,0:T(8,128)(2,1)S(1)} %copy-done.3, bf16[3,2048,512]{2,1,0:T(8,128)(2,1)S(1)} %bitcast.50, f32[3,1,512]{2,1,0:T(1,128)S(1)} %copy.27.refs_3_, ...), custom_call_target="tpu_custom_call" | custom-call | tf_op jit(solution)/shard_map/project/pallas_call | solution.py:53
  129.0 16.9 %attend.1 = (bf16[1024,512]{1,0:T(8,128)(2,1)S(1)}, bf16[1024,1536]{1,0:T(8,128)(2,1)S(1)}, bf16[1024,512]{1,0:T(8,128)(2,1)S(1)}, f32[1024,512]{1,0:T(8,128)S(1)}) custom-call(s32[4]{0:T(128)S(1)} %pad_add_fusion.owners_ref, bf16[3,1024,512]{2,1,0:T(8,128)(2,1)S(1)} %get-tuple-element.164.q_ref.k_ref.v_ref.refs_0_.refs_1_.refs_2_, ...), custom_call_target="tpu_custom_call" | custom-call | tf_op jit(solution)/shard_map/attend/pallas_call | solution.py:76
  160.0 12.9 %collective-permute-done.8.refs_3_ = bf16[1024,512]{1,0:T(8,128)(2,1)S(1)} collective-permute-done((bf16[1024,512]{1,0:T(8,128)(2,1)}, bf16[1024,512]{1,0:T(8,128)(2,1)S(1)}, u32[]{:S(2)}, u32[]{:S(2)}) %collective-permute-start.8) | collective-permute-done | bytes 1048608 | tf_op jit(solution)/shard_map/ppermute | solution.py:490
  184.7 11.9 %collective-permute-done.11.refs_5_ = bf16[1024,512]{1,0:T(8,128)(2,1)} collective-permute-done((bf16[1024,512]{1,0:T(8,128)(2,1)}, bf16[1024,512]{1,0:T(8,128)(2,1)}, u32[]{:S(2)}, u32[]{:S(2)}) %collective-permute-start.11) | collective-permute-done | bytes 1048608 | tf_op jit(solution)/shard_map/ppermute | solution.py:490
  211.2 13.7 %collective-permute-done.13 = bf16[1024,512]{1,0:T(8,128)(2,1)} collective-permute-done((bf16[1024,512]{1,0:T(8,128)(2,1)}, bf16[1024,512]{1,0:T(8,128)(2,1)}, u32[]{:S(2)}, u32[]{:S(2)}) %collective-permute-start.13) | collective-permute-done | bytes 1048608 | tf_op jit(solution)/shard_map/ppermute | solution.py:569
  231.9 15.9 %collective-permute-done.15.refs_1_ = bf16[1024,512]{1,0:T(8,128)(2,1)S(1)} collective-permute-done((bf16[1024,512]{1,0:T(8,128)(2,1)S(1)}, bf16[1024,512]{1,0:T(8,128)(2,1)S(1)}, u32[]{:S(2)}, u32[]{:S(2)}) %collective-permute-start.15) | collective-permute-done | bytes 1048608 | tf_op jit(solution)/shard_map/ppermute | solution.py:490
  258.0 12.5 %collective-permute-done.17.refs_3_ = bf16[1024,512]{1,0:T(8,128)(2,1)S(1)} collective-permute-done((bf16[1024,512]{1,0:T(8,128)(2,1)S(1)}, bf16[1024,512]{1,0:T(8,128)(2,1)S(1)}, u32[]{:S(2)}, u32[]{:S(2)}) %collective-permute-start.17) | collective-permute-done | bytes 1048608 | tf_op jit(solution)/shard_map/ppermute | solution.py:490
  270.5 23.5 %collective-permute-done.19.refs_5_ = bf16[1024,512]{1,0:T(8,128)(2,1)S(1)} collective-permute-done((bf16[1024,512]{1,0:T(8,128)(2,1)S(1)}, bf16[1024,512]{1,0:T(8,128)(2,1)S(1)}, u32[]{:S(2)}, u32[]{:S(2)}) %collective-permute-start.19) | collective-permute-done | bytes 1048608 | tf_op jit(solution)/shard_map/ppermute | solution.py:490
  296.8 32.2 %mlp.1 = (bf16[1024,2048]{1,0:T(8,128)(2,1)}, f32[1024,128]{1,0:T(8,128)S(1)}, bf16[1024,1408]{1,0:T(8,128)(2,1)S(1)}, bf16[1024,1408]{1,0:T(8,128)(2,1)S(1)}, bf16[1024,1408]{1,0:T(8,128)(2,1)}) custom-call(bf16[1024,2048]{1,0:T(8,128)(2,1)} %copy-done.7, bf16[1024,2048]{1,0:T(8,128)(2,1)} %copy-done.5, f32[1,2048]{1,0:T(1,128)S(1)} %get-tuple-element.313.refs_2_, ...), custom_call_target="tpu_custom_call" | custom-call | tf_op jit(solution)/shard_map/mlp/pallas_call | solution.py:53
  342.4 15.7 %mlp_back.3 = bf16[1024,1536]{1,0:T(8,128)(2,1)} custom-call(s32[3]{0:T(128)} %pad_add_fusion.1.owners_ref, bf16[1024,1408]{1,0:T(8,128)(2,1)} %copy-done.11, bf16[1024,1408]{1,0:T(8,128)(2,1)} %get-tuple-element.187.dup_ref.refs_3_, bf16[2048,1408]{1,0:T(8,128)(2,1)} %bitcast.61, bf16[2048,1408]{1,0:T(8,128)(2,1)} %slice_bitcast_fusion.refs_5_.up_w_ref), custom_call_target="tpu_custom_call" | custom-call | tf_op jit(solution)/shard_map/mlp_back/pallas_call | solution.py:76
  368.3 15.6 %mlp_given.1 = (bf16[1024,1408]{1,0:T(8,128)(2,1)}, bf16[1024,1408]{1,0:T(8,128)(2,1)}, bf16[1024,1408]{1,0:T(8,128)(2,1)}) custom-call(s32[1]{0:T(128)} %bitcast.12.which_ref, bf16[1024,2048]{1,0:T(8,128)(2,1)} %get-tuple-element.193.refs_0_, bf16[1024,2048]{1,0:T(8,128)(2,1)} %copy-done.5, bf16[1024,1408]{1,0:T(8,128)(2,1)} %copy-done.11, ...), custom_call_target="tpu_custom_call" | custom-call | tf_op jit(solution)/shard_map/mlp_given/pallas_call | solution.py:76
  389.6 15.4 %mlp_kept.1 = (bf16[1024,1408]{1,0:T(8,128)(2,1)}, bf16[1024,1408]{1,0:T(8,128)(2,1)}, bf16[1024,1408]{1,0:T(8,128)(2,1)}) custom-call(s32[1]{0:T(128)} %bitcast.13.which_ref.core_ref, bf16[1024,2048]{1,0:T(8,128)(2,1)} %get-tuple-element.193.refs_0_, bf16[1024,2048]{1,0:T(8,128)(2,1)} %copy-done.5, bf16[1024,1408]{1,0:T(8,128)(2,1)} %copy-done.11, ...), custom_call_target="tpu_custom_call" | custom-call | flops 30000001024 | tf_op jit(solution)/shard_map/mlp_kept/pallas_call | solution.py:76
  420.2 10.6 %split.4 = (bf16[256,4224]{1,0:T(8,128)(2,1)}, bf16[256,4224]{1,0:T(8,128)(2,1)}, bf16[256,4224]{1,0:T(8,128)(2,1)}, bf16[256,4224]{1,0:T(8,128)(2,1)}) custom-call(s32[2]{0:T(128)} %pad_add_fusion.2.bits_ref, bf16[1024,1408]{1,0:T(8,128)(2,1)} %get-tuple-element.209.refs_0_.refs_6_, bf16[1024,1408]{1,0:T(8,128)(2,1)} %collective-permute-done.27.refs_1_.refs_7_, ...), custom_call_target="tpu_custom_call" | custom-call | tf_op jit(solution)/shard_map/split/pallas_call | solution.py:76
  453.4 17.4 %collective-permute-done.30.refs_3_ = bf16[1024,512]{1,0:T(8,128)(2,1)S(1)} collective-permute-done((bf16[1024,512]{1,0:T(8,128)(2,1)}, bf16[1024,512]{1,0:T(8,128)(2,1)S(1)}, u32[]{:S(2)}, u32[]{:S(2)}) %collective-permute-start.30) | collective-permute-done | bytes 1048608 | tf_op jit(solution)/shard_map/ppermute | solution.py:490
  485.2 10.1 %collective-permute-done.33.refs_5_ = bf16[1024,512]{1,0:T(8,128)(2,1)S(1)} collective-permute-done((bf16[1024,512]{1,0:T(8,128)(2,1)S(1)}, bf16[1024,512]{1,0:T(8,128)(2,1)S(1)}, u32[]{:S(2)}, u32[]{:S(2)}) %collective-permute-start.33) | collective-permute-done | bytes 1048608 | tf_op jit(solution)/shard_map/ppermute | solution.py:490
  518.8 21.2 %attend_back.1 = (bf16[1024,512]{1,0:T(8,128)(2,1)S(1)}, bf16[1024,512]{1,0:T(8,128)(2,1)S(1)}, bf16[1024,512]{1,0:T(8,128)(2,1)S(1)}, f32[8,1024]{1,0:T(8,128)S(1)}) custom-call(bf16[3,1024,512]{2,1,0:T(8,128)(2,1)S(1)} %copy-done.10, bf16[3,1024,512]{2,1,0:T(8,128)(2,1)S(1)} %copy-done.10, bf16[3,1024,512]{2,1,0:T(8,128)(2,1)S(1)} %copy-done.10, ...), custom_call_target="tpu_custom_call" | custom-call | flops 20000000000 | tf_op jit(solution)/shard_map/attend_back/pallas_call | solution.py:53
  603.5 20.3 %collective-permute-done.45.refs_3_ = bf16[256,4224]{1,0:T(8,128)(2,1)} collective-permute-done((bf16[256,4224]{1,0:T(8,128)(2,1)}, bf16[256,4224]{1,0:T(8,128)(2,1)}, u32[]{:S(2)}, u32[]{:S(2)}) %collective-permute-start.45) | collective-permute-done | bytes 2162720 | tf_op jit(solution)/shard_map/ppermute | solution.py:683
  632.7 13.2 %collective-permute-done.49.refs_3_ = bf16[256,2048]{1,0:T(8,128)(2,1)} collective-permute-done((bf16[256,2048]{1,0:T(8,128)(2,1)}, bf16[256,2048]{1,0:T(8,128)(2,1)}, u32[]{:S(2)}, u32[]{:S(2)}) %collective-permute-start.49) | collective-permute-done | bytes 1048608 | tf_op jit(solution)/shard_map/ppermute | solution.py:683
  672.8 13.3 %collective-permute-done.52 = bf16[1040,512]{1,0:T(8,128)(2,1)S(1)} collective-permute-done((bf16[1040,512]{1,0:T(8,128)(2,1)S(1)}, bf16[1040,512]{1,0:T(8,128)(2,1)S(1)}, u32[]{:S(2)}, u32[]{:S(2)}) %collective-permute-start.52) | collective-permute-done | bytes 1064992 | tf_op jit(solution)/shard_map/ppermute | solution.py:569
  699.6 17.3 %gate_up_out.1 = f32[2048,2,1408]{2,1,0:T(2,128)} custom-call(s32[1]{0:T(128)} %bitcast.13.which_ref.core_ref, bf16[1024,1408]{1,0:T(8,128)(2,1)} %bitcast.66, bf16[1024,1408]{1,0:T(8,128)(2,1)} %bitcast.68, bf16[1024,1408]{1,0:T(8,128)(2,1)} %collective-permute-done.57.refs_2_, bf16[1024,1408]{1,0:T(8,128)(2,1)} %collective-permute-done.58.refs_3_), custom_call_target="tpu_custom_call" | custom-call | tf_op jit(solution)/shard_map/gate_up_out/pallas_call | solution.py:76
  740.2 12.9 %down_out.1 = f32[1408,2048]{1,0:T(8,128)} custom-call(s32[1]{0:T(128)} %bitcast.13.which_ref.core_ref, bf16[1024,1408]{1,0:T(8,128)(2,1)} %bitcast.63, bf16[1024,1408]{1,0:T(8,128)(2,1)} %collective-permute-done.63.refs_1_), custom_call_target="tpu_custom_call" | custom-call | tf_op jit(solution)/shard_map/down_out/pallas_call | solution.py:76
  (405 shorter events, 366.3 us)
Async XLA Ops:
  40.3 30.6 %collective-permute-start.2 = (bf16[1040,512]{1,0:T(8,128)(2,1)S(1)}, bf16[1040,512]{1,0:T(8,128)(2,1)S(1)}, u32[]{:S(2)}, u32[]{:S(2)}) collective-permute-start(bf16[1040,512]{1,0:T(8,128)(2,1)S(1)} %collective-permute-done.1.refs_2_), channel_id=1, source_target_pairs={{1,0},{2,3},{5,4},{6,7},{9,8},{10,11},{13,12},{14,15},{17,16},{18,... | collective-permute-start | bytes 3194888 | tf_op jit(solution)/shard_map/ppermute | solution.py:490
  250.4 43.6 %collective-permute-start.19 = (bf16[1024,512]{1,0:T(8,128)(2,1)S(1)}, bf16[1024,512]{1,0:T(8,128)(2,1)S(1)}, u32[]{:S(2)}, u32[]{:S(2)}) collective-permute-start(bf16[1024,512]{1,0:T(8,128)(2,1)S(1)} %collective-permute-done.18.refs_4_), channel_id=1, source_target_pairs={{1,0},{2,3},{5,4},{6,7},{9,8},{10,11},{13,12},{14,15},{17,16},{18,... | collective-permute-start | bytes 3145736 | tf_op jit(solution)/shard_map/ppermute | solution.py:490
  383.8 36.3 %collective-permute-start.27 = (bf16[1024,1408]{1,0:T(8,128)(2,1)}, bf16[1024,1408]{1,0:T(8,128)(2,1)}, u32[]{:S(2)}, u32[]{:S(2)}) collective-permute-start(bf16[1024,1408]{1,0:T(8,128)(2,1)} %get-tuple-element.195), channel_id=1, source_target_pairs={{0,4},{4,0},{8,12},{12,8},{16,20},{20,16},{24,28},{28,24},{1,5},{5... | collective-permute-start | bytes 8650760 | tf_op jit(solution)/shard_map/ppermute | solution.py:683
  383.8 36.3 %collective-permute-start.28 = (bf16[1024,1408]{1,0:T(8,128)(2,1)}, bf16[1024,1408]{1,0:T(8,128)(2,1)}, u32[]{:S(2)}, u32[]{:S(2)}) collective-permute-start(bf16[1024,1408]{1,0:T(8,128)(2,1)} %get-tuple-element.196), channel_id=1, source_target_pairs={{0,4},{4,0},{8,12},{12,8},{16,20},{20,16},{24,28},{28,24},{1,5},{5... | collective-permute-start | bytes 8650760 | tf_op jit(solution)/shard_map/ppermute | solution.py:683
  384.3 35.8 %collective-permute-start.29 = (bf16[1024,1408]{1,0:T(8,128)(2,1)}, bf16[1024,1408]{1,0:T(8,128)(2,1)}, u32[]{:S(2)}, u32[]{:S(2)}) collective-permute-start(bf16[1024,1408]{1,0:T(8,128)(2,1)} %get-tuple-element.197), channel_id=1, source_target_pairs={{0,4},{4,0},{8,12},{12,8},{16,20},{20,16},{24,28},{28,24},{1,5},{5... | collective-permute-start | bytes 8650760 | tf_op jit(solution)/shard_map/ppermute | solution.py:683
  430.8 48.3 %collective-permute-start.34 = (bf16[256,4224]{1,0:T(8,128)(2,1)}, bf16[256,4224]{1,0:T(8,128)(2,1)S(1)}, u32[]{:S(2)}, u32[]{:S(2)}) collective-permute-start(bf16[256,4224]{1,0:T(8,128)(2,1)} %get-tuple-element.221), channel_id=1, source_target_pairs={{0,8},{4,12},{8,0},{12,4},{16,24},{20,28},{24,16},{28,20},{1,9},{5... | collective-permute-start | bytes 6488072 | tf_op jit(solution)/shard_map/ppermute | solution.py:683
  432.4 47.9 %collective-permute-start.35 = (bf16[256,4224]{1,0:T(8,128)(2,1)}, bf16[256,4224]{1,0:T(8,128)(2,1)S(1)}, u32[]{:S(2)}, u32[]{:S(2)}) collective-permute-start(bf16[256,4224]{1,0:T(8,128)(2,1)} %get-tuple-element.224), channel_id=1, source_target_pairs={{0,16},{4,20},{8,24},{12,28},{16,0},{20,4},{24,8},{28,12},{1,17},{... | collective-permute-start | bytes 6488072 | tf_op jit(solution)/shard_map/ppermute | solution.py:683
  441.4 29.4 %collective-permute-start.30 = (bf16[1024,512]{1,0:T(8,128)(2,1)}, bf16[1024,512]{1,0:T(8,128)(2,1)S(1)}, u32[]{:S(2)}, u32[]{:S(2)}) collective-permute-start(bf16[1024,512]{1,0:T(8,128)(2,1)} %collective-permute-done.26.refs_2_), channel_id=1, source_target_pairs={{1,0},{2,3},{5,4},{6,7},{9,8},{10,11},{13,12},{14,15},{17,16},{18,... | collective-permute-start | bytes 3145736 | tf_op jit(solution)/shard_map/ppermute | solution.py:490
  482.0 31.2 %collective-permute-start.38 = (bf16[128,4224]{1,0:T(8,128)(2,1)S(1)}, bf16[128,4224]{1,0:T(8,128)(2,1)S(1)}, u32[]{:S(2)}, u32[]{:S(2)}) collective-permute-start(bf16[128,4224]{1,0:T(8,128)(2,1)S(1)} %get-tuple-element.238), channel_id=1, source_target_pairs={{0,8},{4,12},{8,0},{12,4},{16,24},{20,28},{24,16},{28,20},{1,9},{5... | collective-permute-start | bytes 3244040 | tf_op jit(solution)/shard_map/ppermute | solution.py:683
  483.6 30.9 %collective-permute-start.37 = (bf16[128,4224]{1,0:T(8,128)(2,1)S(1)}, bf16[128,4224]{1,0:T(8,128)(2,1)S(1)}, u32[]{:S(2)}, u32[]{:S(2)}) collective-permute-start(bf16[128,4224]{1,0:T(8,128)(2,1)S(1)} %get-tuple-element.235), channel_id=1, source_target_pairs={{0,16},{4,20},{8,24},{12,28},{16,0},{20,4},{24,8},{28,12},{1,17},{... | collective-permute-start | bytes 3244040 | tf_op jit(solution)/shard_map/ppermute | solution.py:683
  497.9 47.8 %collective-permute-start.41 = (bf16[1024,512]{1,0:T(8,128)(2,1)}, bf16[1024,512]{1,0:T(8,128)(2,1)}, u32[]{:S(2)}, u32[]{:S(2)}) collective-permute-start(bf16[1024,512]{1,0:T(8,128)(2,1)} %constant_dynamic-slice_fusion.1), channel_id=1, source_target_pairs={{0,1},{3,2},{4,5},{7,6},{8,9},{11,10},{12,13},{15,14},{16,17},{19,... | collective-permute-start | bytes 3145736 | tf_op jit(solution)/shard_map/ppermute | solution.py:569
  511.4 34.3 %collective-permute-start.36 = (bf16[1024,512]{1,0:T(8,128)(2,1)}, bf16[1024,512]{1,0:T(8,128)(2,1)}, u32[]{:S(2)}, u32[]{:S(2)}) collective-permute-start(bf16[1024,512]{1,0:T(8,128)(2,1)} %add_convert_fusion.8), channel_id=1, source_target_pairs={{1,2},{2,1},{5,6},{6,5},{9,10},{10,9},{13,14},{14,13},{17,18},{18,... | collective-permute-start | bytes 3145736 | tf_op jit(solution)/shard_map/ppermute | solution.py:569
  555.4 46.4 %collective-permute-start.44 = (bf16[256,4224]{1,0:T(8,128)(2,1)}, bf16[256,4224]{1,0:T(8,128)(2,1)}, u32[]{:S(2)}, u32[]{:S(2)}) collective-permute-start(bf16[256,4224]{1,0:T(8,128)(2,1)} %get-tuple-element.255.refs_0_), channel_id=1, source_target_pairs={{0,8},{4,12},{8,0},{12,4},{16,24},{20,28},{24,16},{28,20},{1,9},{5... | collective-permute-start | bytes 6488072 | tf_op jit(solution)/shard_map/ppermute | solution.py:683
  573.7 50.1 %collective-permute-start.45 = (bf16[256,4224]{1,0:T(8,128)(2,1)}, bf16[256,4224]{1,0:T(8,128)(2,1)}, u32[]{:S(2)}, u32[]{:S(2)}) collective-permute-start(bf16[256,4224]{1,0:T(8,128)(2,1)} %get-tuple-element.256.refs_2_), channel_id=1, source_target_pairs={{0,16},{4,20},{8,24},{12,28},{16,0},{20,4},{24,8},{28,12},{1,17},{... | collective-permute-start | bytes 6488072 | tf_op jit(solution)/shard_map/ppermute | solution.py:683
  575.3 56.9 %collective-permute-start.47 = (bf16[1040,512]{1,0:T(8,128)(2,1)}, bf16[1040,512]{1,0:T(8,128)(2,1)}, u32[]{:S(2)}, u32[]{:S(2)}) collective-permute-start(bf16[1040,512]{1,0:T(8,128)(2,1)} %constant_dynamic-slice_fusion), channel_id=1, source_target_pairs={{0,1},{3,2},{4,5},{7,6},{8,9},{11,10},{12,13},{15,14},{16,17},{19,... | collective-permute-start | bytes 3194888 | tf_op jit(solution)/shard_map/ppermute | solution.py:569
  580.6 51.6 %collective-permute-start.46 = (bf16[1040,512]{1,0:T(8,128)(2,1)}, bf16[1040,512]{1,0:T(8,128)(2,1)}, u32[]{:S(2)}, u32[]{:S(2)}) collective-permute-start(bf16[1040,512]{1,0:T(8,128)(2,1)} %add_convert_fusion.4), channel_id=1, source_target_pairs={{1,2},{2,1},{5,6},{6,5},{9,10},{10,9},{13,14},{14,13},{17,18},{18,... | collective-permute-start | bytes 3194888 | tf_op jit(solution)/shard_map/ppermute | solution.py:569
  595.5 37.2 %collective-permute-start.48 = (bf16[256,2048]{1,0:T(8,128)(2,1)}, bf16[256,2048]{1,0:T(8,128)(2,1)}, u32[]{:S(2)}, u32[]{:S(2)}) collective-permute-start(bf16[256,2048]{1,0:T(8,128)(2,1)} %get-tuple-element.262), channel_id=1, source_target_pairs={{0,8},{4,12},{8,0},{12,4},{16,24},{20,28},{24,16},{28,20},{1,9},{5... | collective-permute-start | bytes 3145736 | tf_op jit(solution)/shard_map/ppermute | solution.py:683
  601.7 44.2 %collective-permute-start.49 = (bf16[256,2048]{1,0:T(8,128)(2,1)}, bf16[256,2048]{1,0:T(8,128)(2,1)}, u32[]{:S(2)}, u32[]{:S(2)}) collective-permute-start(bf16[256,2048]{1,0:T(8,128)(2,1)} %get-tuple-element.265), channel_id=1, source_target_pairs={{0,16},{4,20},{8,24},{12,28},{16,0},{20,4},{24,8},{28,12},{1,17},{... | collective-permute-start | bytes 3145736 | tf_op jit(solution)/shard_map/ppermute | solution.py:683
  632.2 66.7 %collective-permute-start.57 = (bf16[1024,1408]{1,0:T(8,128)(2,1)}, bf16[1024,1408]{1,0:T(8,128)(2,1)}, u32[]{:S(2)}, u32[]{:S(2)}) collective-permute-start(bf16[1024,1408]{1,0:T(8,128)(2,1)} %bitcast.65), channel_id=1, source_target_pairs={{0,4},{4,0},{8,12},{12,8},{16,20},{20,16},{24,28},{28,24},{1,5},{5... | collective-permute-start | bytes 8650760 | tf_op jit(solution)/shard_map/ppermute | solution.py:683
  632.2 67.4 %collective-permute-start.58 = (bf16[1024,1408]{1,0:T(8,128)(2,1)}, bf16[1024,1408]{1,0:T(8,128)(2,1)}, u32[]{:S(2)}, u32[]{:S(2)}) collective-permute-start(bf16[1024,1408]{1,0:T(8,128)(2,1)} %bitcast.67), channel_id=1, source_target_pairs={{0,4},{4,0},{8,12},{12,8},{16,20},{20,16},{24,28},{28,24},{1,5},{5... | collective-permute-start | bytes 8650760 | tf_op jit(solution)/shard_map/ppermute | solution.py:683
  691.5 31.3 %collective-permute-start.61 = (bf16[256,2048]{1,0:T(8,128)(2,1)}, bf16[256,2048]{1,0:T(8,128)(2,1)}, u32[]{:S(2)}, u32[]{:S(2)}) collective-permute-start(bf16[256,2048]{1,0:T(8,128)(2,1)} %get-tuple-element.291.refs_0_), channel_id=1, source_target_pairs={{0,8},{4,12},{8,0},{12,4},{16,24},{20,28},{24,16},{28,20},{1,9},{5... | collective-permute-start | bytes 3145736 | tf_op jit(solution)/shard_map/ppermute | solution.py:683
  728.8 30.5 %collective-permute-start.67 = (bf16[1024,2048]{1,0:T(8,128)(2,1)}, bf16[1024,2048]{1,0:T(8,128)(2,1)S(1)}, u32[]{:S(2)}, u32[]{:S(2)}) collective-permute-start(bf16[1024,2048]{1,0:T(8,128)(2,1)} %bitcast.55), channel_id=1, source_target_pairs={{0,4},{4,0},{8,12},{12,8},{16,20},{20,16},{24,28},{28,24},{1,5},{5... | collective-permute-start | bytes 12582920 | tf_op jit(solution)/shard_map/ppermute | solution.py:683
  729.4 28.7 %collective-permute-start.64 = (f32[7,512]{1,0:T(8,128)S(1)}, f32[7,512]{1,0:T(8,128)S(1)}, u32[]{:S(2)}, u32[]{:S(2)}) collective-permute-start(f32[7,512]{1,0:T(8,128)S(1)} %add.259), channel_id=1, source_target_pairs={{0,8},{4,12},{8,0},{12,4},{16,24},{20,28},{24,16},{28,20},{1,9},{5... | collective-permute-start | bytes 43016 | tf_op jit(solution)/shard_map/ppermute | solution.py:1052
  730.8 27.3 %collective-permute-start.65 = (f32[7,512]{1,0:T(8,128)S(1)}, f32[7,512]{1,0:T(8,128)S(1)}, u32[]{:S(2)}, u32[]{:S(2)}) collective-permute-start(f32[7,512]{1,0:T(8,128)S(1)} %add.259), channel_id=1, source_target_pairs={{0,16},{4,20},{8,24},{12,28},{16,0},{20,4},{24,8},{28,12},{1,17},{... | collective-permute-start | bytes 43016 | tf_op jit(solution)/shard_map/ppermute | solution.py:1052
  (141 other events, 2050.8 us)

commit v5 on v4

--- a/solution.py
+++ b/solution.py
@@ -14,7 +14,7 @@
 PAIR = 2 * HEAD_DIM
 CHUNKS = 1
 SUB = 256
-WEIGHTS = {"mlp_kept": 30, "mlp_out": 10, "attend_back": 20, "attention_kept": 40}
+WEIGHTS = {"mlp_kept": 30, "mlp_out": 10, "attend_back": 20, "merge": 15, "attention_kept": 40}
 EXTRA = 16
 
 EPSILON = 1e-05
@@ -773,7 +773,7 @@
         [spec(part, which) for part in range(2) for which in range(2)],
         outs,
         out_specs,
-        mib=56,
+        mib=56 if widths and columns > D else 22,
         name="merge",
     )
 
@@ -1017,22 +1017,24 @@
     attention_kept = attention_grads(core, "attention_kept")
     order.done(*attention_kept)
     held = attention_sum.send(attention_kept)
-    order.done(held)
-    held = next(mlp_sum)
     order.done(held, *got)
     got = finish(order, delta_one)
-    held = next(attention_sum)
+    held = next(mlp_sum)
     order.done(held)
     held = next(attention_sum)
     order.done(held, *got)
+    held = next(attention_sum)
+    order.done(held)
     if lax.axis_size("dp") > 8:
         for _ in range(2):
             order.done(next(mlp_sum))
             order.done(next(attention_sum))
+    mlp_halves = next(mlp_sum)
+    down_grad = down_out(core, [order(mlp_halves[0][2])], mlp_halves[1][2:])
+    order.done(down_grad, *got)
     held = next(attention_sum)
     order.done(held)
     share_got = finish(order, mlp_share)
-    mlp_halves = next(mlp_sum)
     gate_up_grad = gate_up_out(core, [order(mlp_halves[0][0]), mlp_halves[0][1]], mlp_halves[1][:2])
     order.done(gate_up_grad)
     delta_one = delta_one.total(order)
@@ -1050,8 +1052,6 @@
     order.done(held)
     devices = lax.axis_size("dp")
     others = [lax.ppermute(order(small), "dp", [(i, i ^ k) for i in range(devices)]) for k in range(2, devices, 2)]
-    down_grad = down_out(core, [order(mlp_halves[0][2])], mlp_halves[1][2:])
-    order.done(down_grad)
     result = (middle_share + mlp_share.total(order)).astype(BF)
     small = sum((order(other) for other in others), small)
     order.done(tokens_grad, small, result)

time: 774 us -> 722 us (0.933)
  waiting for transfers between devices: 272 us -> 214 us
  starting transfers between devices: 103 us -> 114 us
    ppermute x25, waiting for transfers between devices: 61.5 us -> 24.3 us  [swap(): return lax.ppermute(value, axis, [(i, i ^ 1 << bit) for i in range(n)])]
    ppermute x20, waiting for transfers between devices: 172 us -> 148 us  [send(): self.pieces.append(lax.ppermute(order(self.pieces[piece]), 'tensor', pairs))]
    ppermute x20, starting transfers between devices: 51.4 us -> 61.2 us  [send(): self.got[name] = lax.ppermute(order(value), 'tensor', pairs)]
    unnamed x195 -> x181, local copies, waits for them, and re-layouts: 49.9 us -> 47.4 us
  transfers between devices with their start and end apart: 68 -> 68, of which waited for: 25 -> 23; matrix products, arithmetic and copies ran while one was open for 8% -> 10% of each run, Pallas kernels for 25% -> 26%
where the time goes in v5:
time: 722 us; the launch traced here: 714 us
  Pallas kernels  262 us (36%)
  waiting for transfers between devices  214 us (30%)
  starting transfers between devices  114 us (16%)
  local copies, waits for them, and re-layouts  72.4 us (10%)
  other arithmetic  46.6 us (6%)
    pallas_call x25, Pallas kernels, prefetched(): pl.pallas_call(body, grid_spec=pltpu.PrefetchScalarGridSpec(num_scalar_pr...  186 us
    ppermute x20, waiting for transfers between devices, send(): self.pieces.append(lax.ppermute(order(self.pieces[piece]), 'tensor', pairs))  148 us
    pallas_call x4, Pallas kernels, kernel_call(): pl.pallas_call(run, grid=grid, in_specs=list(in_specs) + [ANY] * len(prev...  75.4 us
    ppermute x20, starting transfers between devices, send(): self.got[name] = lax.ppermute(order(value), 'tensor', pairs)  61.2 us
    unnamed x181, local copies, waits for them, and re-layouts  47.4 us
    ppermute x20, waiting for transfers between devices, send(): self.got[name] = lax.ppermute(order(value), 'tensor', pairs)  41.9 us
    ppermute x20, starting transfers between devices, send(): self.pieces.append(lax.ppermute(order(self.pieces[piece]), 'tensor', pairs))  29.3 us
    ppermute x25, waiting for transfers between devices, swap(): return lax.ppermute(value, axis, [(i, i ^ 1 << bit) for i in range(n)])  24.3 us
  transfers between devices with their start and end apart: 68, of which 23 were waited for; matrix products, arithmetic and copies ran while one was open for 10% of the time, Pallas kernels for 26%

profile of v5, /device:TPU:0, one launch (start us, length us, event | category | flops | bytes accessed | tf_op | source)
XLA Modules:
  0.0 714.4 jit_solution(18345783387911502126)
XLA Ops:
  22.4 12.1 %collective-permute-done.refs_1_ = bf16[1040,512]{1,0:T(8,128)(2,1)S(1)} collective-permute-done((bf16[1040,512]{1,0:T(8,128)(2,1)S(1)}, bf16[1040,512]{1,0:T(8,128)(2,1)S(1)}, u32[]{:S(2)}, u32[]{:S(2)}) %collective-permute-start) | collective-permute-done | bytes 1064992 | tf_op jit(solution)/shard_map/ppermute | solution.py:490
  47.0 13.7 %collective-permute-done.2.refs_3_ = bf16[1040,512]{1,0:T(8,128)(2,1)S(1)} collective-permute-done((bf16[1040,512]{1,0:T(8,128)(2,1)S(1)}, bf16[1040,512]{1,0:T(8,128)(2,1)S(1)}, u32[]{:S(2)}, u32[]{:S(2)}) %collective-permute-start.2) | collective-permute-done | bytes 1064992 | tf_op jit(solution)/shard_map/ppermute | solution.py:490
  64.0 23.3 %collective-permute-done.4.refs_5_ = bf16[1040,512]{1,0:T(8,128)(2,1)} collective-permute-done((bf16[1040,512]{1,0:T(8,128)(2,1)S(1)}, bf16[1040,512]{1,0:T(8,128)(2,1)}, u32[]{:S(2)}, u32[]{:S(2)}) %collective-permute-start.4) | collective-permute-done | bytes 1064992 | tf_op jit(solution)/shard_map/ppermute | solution.py:490
  105.1 14.2 %project.1 = (bf16[1024,2048]{1,0:T(8,128)(2,1)S(1)}, f32[1024,128]{1,0:T(8,128)S(1)}, bf16[3,1024,512]{2,1,0:T(8,128)(2,1)S(1)}) custom-call(bf16[1040,2048]{1,0:T(8,128)(2,1)S(1)} %copy-done.2, bf16[1040,2048]{1,0:T(8,128)(2,1)S(1)} %copy-done.2, bf16[3,2048,512]{2,1,0:T(8,128)(2,1)S(1)} %bitcast.50, f32[3,1,512]{2,1,0:T(1,128)S(1)} %copy.27.refs_3_, ...), custom_call_target="tpu_custom_call" | custom-call | tf_op jit(solution)/shard_map/project/pallas_call | solution.py:53
  121.0 16.9 %attend.1 = (bf16[1024,512]{1,0:T(8,128)(2,1)S(1)}, bf16[1024,1536]{1,0:T(8,128)(2,1)S(1)}, bf16[1024,512]{1,0:T(8,128)(2,1)S(1)}, f32[1024,512]{1,0:T(8,128)S(1)}) custom-call(s32[4]{0:T(128)S(1)} %pad_add_fusion.owners_ref, bf16[3,1024,512]{2,1,0:T(8,128)(2,1)S(1)} %get-tuple-element.164.q_ref.k_ref.v_ref.refs_0_.refs_1_.refs_2_, ...), custom_call_target="tpu_custom_call" | custom-call | tf_op jit(solution)/shard_map/attend/pallas_call | solution.py:76
  150.8 10.6 %collective-permute-done.8.refs_3_ = bf16[1024,512]{1,0:T(8,128)(2,1)S(1)} collective-permute-done((bf16[1024,512]{1,0:T(8,128)(2,1)}, bf16[1024,512]{1,0:T(8,128)(2,1)S(1)}, u32[]{:S(2)}, u32[]{:S(2)}) %collective-permute-start.8) | collective-permute-done | bytes 1048608 | tf_op jit(solution)/shard_map/ppermute | solution.py:490
  168.6 8.2 %collective-permute-start.12 = (bf16[1024,512]{1,0:T(8,128)(2,1)}, bf16[1024,512]{1,0:T(8,128)(2,1)}, u32[]{:S(2)}, u32[]{:S(2)}) collective-permute-start(bf16[1024,512]{1,0:T(8,128)(2,1)} %constant_dynamic-slice_fusion.3), channel_id=1, source_target_pairs={{0,1},{3,2},{4,5},{7,6},{8,9},{11,10},{12,13},{15,14},{16,17},{19,... | collective-permute-start | bytes 3145736 | tf_op jit(solution)/shard_map/ppermute | solution.py:569
  176.8 14.3 %collective-permute-done.11.refs_5_ = bf16[1024,512]{1,0:T(8,128)(2,1)} collective-permute-done((bf16[1024,512]{1,0:T(8,128)(2,1)}, bf16[1024,512]{1,0:T(8,128)(2,1)}, u32[]{:S(2)}, u32[]{:S(2)}) %collective-permute-start.11) | collective-permute-done | bytes 1048608 | tf_op jit(solution)/shard_map/ppermute | solution.py:490
  203.9 16.6 %collective-permute-done.13 = bf16[1024,512]{1,0:T(8,128)(2,1)} collective-permute-done((bf16[1024,512]{1,0:T(8,128)(2,1)}, bf16[1024,512]{1,0:T(8,128)(2,1)}, u32[]{:S(2)}, u32[]{:S(2)}) %collective-permute-start.13) | collective-permute-done | bytes 1048608 | tf_op jit(solution)/shard_map/ppermute | solution.py:569
  225.8 16.4 %collective-permute-done.15.refs_1_ = bf16[1024,512]{1,0:T(8,128)(2,1)S(1)} collective-permute-done((bf16[1024,512]{1,0:T(8,128)(2,1)S(1)}, bf16[1024,512]{1,0:T(8,128)(2,1)S(1)}, u32[]{:S(2)}, u32[]{:S(2)}) %collective-permute-start.15) | collective-permute-done | bytes 1048608 | tf_op jit(solution)/shard_map/ppermute | solution.py:490
  252.4 12.7 %collective-permute-done.17.refs_3_ = bf16[1024,512]{1,0:T(8,128)(2,1)S(1)} collective-permute-done((bf16[1024,512]{1,0:T(8,128)(2,1)S(1)}, bf16[1024,512]{1,0:T(8,128)(2,1)S(1)}, u32[]{:S(2)}, u32[]{:S(2)}) %collective-permute-start.17) | collective-permute-done | bytes 1048608 | tf_op jit(solution)/shard_map/ppermute | solution.py:490
  265.1 20.8 %collective-permute-done.19.refs_5_ = bf16[1024,512]{1,0:T(8,128)(2,1)S(1)} collective-permute-done((bf16[1024,512]{1,0:T(8,128)(2,1)S(1)}, bf16[1024,512]{1,0:T(8,128)(2,1)S(1)}, u32[]{:S(2)}, u32[]{:S(2)}) %collective-permute-start.19) | collective-permute-done | bytes 1048608 | tf_op jit(solution)/shard_map/ppermute | solution.py:490
  288.7 32.2 %mlp.1 = (bf16[1024,2048]{1,0:T(8,128)(2,1)}, f32[1024,128]{1,0:T(8,128)S(1)}, bf16[1024,1408]{1,0:T(8,128)(2,1)S(1)}, bf16[1024,1408]{1,0:T(8,128)(2,1)S(1)}, bf16[1024,1408]{1,0:T(8,128)(2,1)}) custom-call(bf16[1024,2048]{1,0:T(8,128)(2,1)} %copy-done.5, bf16[1024,2048]{1,0:T(8,128)(2,1)} %copy-done.3, f32[1,2048]{1,0:T(1,128)S(1)} %get-tuple-element.313.refs_2_, ...), custom_call_target="tpu_custom_call" | custom-call | tf_op jit(solution)/shard_map/mlp/pallas_call | solution.py:53
  334.3 15.7 %mlp_back.3 = bf16[1024,1536]{1,0:T(8,128)(2,1)} custom-call(s32[3]{0:T(128)} %pad_add_fusion.1.owners_ref, bf16[1024,1408]{1,0:T(8,128)(2,1)} %copy-done.9, bf16[1024,1408]{1,0:T(8,128)(2,1)} %get-tuple-element.187.dup_ref.refs_3_, bf16[2048,1408]{1,0:T(8,128)(2,1)} %bitcast.65, bf16[2048,1408]{1,0:T(8,128)(2,1)} %slice_bitcast_fusion.refs_5_.up_w_ref), custom_call_target="tpu_custom_call" | custom-call | tf_op jit(solution)/shard_map/mlp_back/pallas_call | solution.py:76
  362.5 15.6 %mlp_given.1 = (bf16[1024,1408]{1,0:T(8,128)(2,1)}, bf16[1024,1408]{1,0:T(8,128)(2,1)}, bf16[1024,1408]{1,0:T(8,128)(2,1)}) custom-call(s32[1]{0:T(128)} %bitcast.12.which_ref, bf16[1024,2048]{1,0:T(8,128)(2,1)} %get-tuple-element.193.refs_0_, bf16[1024,2048]{1,0:T(8,128)(2,1)} %copy-done.3, bf16[1024,1408]{1,0:T(8,128)(2,1)} %copy-done.9, ...), custom_call_target="tpu_custom_call" | custom-call | tf_op jit(solution)/shard_map/mlp_given/pallas_call | solution.py:76
  386.8 15.4 %mlp_kept.1 = (bf16[1024,1408]{1,0:T(8,128)(2,1)}, bf16[1024,1408]{1,0:T(8,128)(2,1)}, bf16[1024,1408]{1,0:T(8,128)(2,1)}) custom-call(s32[1]{0:T(128)} %bitcast.13.which_ref.core_ref, bf16[1024,2048]{1,0:T(8,128)(2,1)} %get-tuple-element.193.refs_0_, bf16[1024,2048]{1,0:T(8,128)(2,1)} %copy-done.3, bf16[1024,1408]{1,0:T(8,128)(2,1)} %copy-done.9, ...), custom_call_target="tpu_custom_call" | custom-call | flops 30000001024 | tf_op jit(solution)/shard_map/mlp_kept/pallas_call | solution.py:76
  413.3 10.7 %split.4 = (bf16[256,4224]{1,0:T(8,128)(2,1)}, bf16[256,4224]{1,0:T(8,128)(2,1)}, bf16[256,4224]{1,0:T(8,128)(2,1)}, bf16[256,4224]{1,0:T(8,128)(2,1)}) custom-call(s32[2]{0:T(128)} %pad_add_fusion.2.bits_ref, bf16[1024,1408]{1,0:T(8,128)(2,1)} %get-tuple-element.209.refs_0_.refs_6_, bf16[1024,1408]{1,0:T(8,128)(2,1)} %collective-permute-done.27.refs_1_.refs_7_, ...), custom_call_target="tpu_custom_call" | custom-call | tf_op jit(solution)/shard_map/split/pallas_call | solution.py:76
  437.4 8.8 %mlp_out.1 = (bf16[1024,512]{1,0:T(8,128)(2,1)S(1)}, bf16[1024,1536]{1,0:T(8,128)(2,1)S(1)}) custom-call(s32[4]{0:T(128)S(1)} %pad_add_fusion.owners_ref, bf16[1024,1408]{1,0:T(8,128)(2,1)S(1)} %copy-done.38, bf16[1408,2048]{1,0:T(8,128)(2,1)S(1)} %bitcast.60), custom_call_target="tpu_custom_call" | custom-call | flops 10000000000 | tf_op jit(solution)/shard_map/mlp_out/pallas_call | solution.py:76
  446.3 10.9 %collective-permute-done.30.refs_3_ = bf16[1024,512]{1,0:T(8,128)(2,1)S(1)} collective-permute-done((bf16[1024,512]{1,0:T(8,128)(2,1)}, bf16[1024,512]{1,0:T(8,128)(2,1)S(1)}, u32[]{:S(2)}, u32[]{:S(2)}) %collective-permute-start.30) | collective-permute-done | bytes 1048608 | tf_op jit(solution)/shard_map/ppermute | solution.py:490
  504.7 21.2 %attend_back.1 = (bf16[1024,512]{1,0:T(8,128)(2,1)S(1)}, bf16[1024,512]{1,0:T(8,128)(2,1)S(1)}, bf16[1024,512]{1,0:T(8,128)(2,1)S(1)}, f32[8,1024]{1,0:T(8,128)S(1)}) custom-call(bf16[3,1024,512]{2,1,0:T(8,128)(2,1)S(1)} %copy-done.8, bf16[3,1024,512]{2,1,0:T(8,128)(2,1)S(1)} %copy-done.8, bf16[3,1024,512]{2,1,0:T(8,128)(2,1)S(1)} %copy-done.8, ...), custom_call_target="tpu_custom_call" | custom-call | flops 20000000000 | tf_op jit(solution)/shard_map/attend_back/pallas_call | solution.py:53
  575.1 13.9 %collective-permute-done.45 = bf16[1040,512]{1,0:T(8,128)(2,1)S(1)} collective-permute-done((bf16[1040,512]{1,0:T(8,128)(2,1)S(1)}, bf16[1040,512]{1,0:T(8,128)(2,1)S(1)}, u32[]{:S(2)}, u32[]{:S(2)}) %collective-permute-start.45) | collective-permute-done | bytes 1064992 | tf_op jit(solution)/shard_map/ppermute | solution.py:569
  597.9 8.3 %merge.5 = (bf16[2,512,1408]{2,1,0:T(8,128)(2,1)}, bf16[2,512,1408]{2,1,0:T(8,128)(2,1)}, bf16[2,512,1408]{2,1,0:T(8,128)(2,1)}) custom-call(s32[2]{0:T(128)} %pad_add_fusion.2.bits_ref, bf16[256,4224]{1,0:T(8,128)(2,1)} %get-tuple-element.258.refs_0_, bf16[256,4224]{1,0:T(8,128)(2,1)} %collective-permute-done.46.refs_1_, ...), custom_call_target="tpu_custom_call" | custom-call | flops 15000000512 | tf_op jit(solution)/shard_map/merge/pallas_call | solution.py:76
  644.0 12.9 %down_out.1 = f32[1408,2048]{1,0:T(8,128)} custom-call(s32[1]{0:T(128)} %bitcast.13.which_ref.core_ref, bf16[1024,1408]{1,0:T(8,128)(2,1)} %bitcast.68, bf16[1024,1408]{1,0:T(8,128)(2,1)} %collective-permute-done.54.refs_1_), custom_call_target="tpu_custom_call" | custom-call | tf_op jit(solution)/shard_map/down_out/pallas_call | solution.py:76
  668.8 17.3 %gate_up_out.1 = f32[2048,2,1408]{2,1,0:T(2,128)} custom-call(s32[1]{0:T(128)} %bitcast.13.which_ref.core_ref, bf16[1024,1408]{1,0:T(8,128)(2,1)} %bitcast.70, bf16[1024,1408]{1,0:T(8,128)(2,1)} %bitcast.72, bf16[1024,1408]{1,0:T(8,128)(2,1)} %collective-permute-done.58.refs_2_, bf16[1024,1408]{1,0:T(8,128)(2,1)} %collective-permute-done.59.refs_3_), custom_call_target="tpu_custom_call" | custom-call | tf_op jit(solution)/shard_map/gate_up_out/pallas_call | solution.py:76
  (393 shorter events, 349.7 us)
Async XLA Ops:
  5.4 29.1 %collective-permute-start = (bf16[1040,512]{1,0:T(8,128)(2,1)S(1)}, bf16[1040,512]{1,0:T(8,128)(2,1)S(1)}, u32[]{:S(2)}, u32[]{:S(2)}) collective-permute-start(bf16[1040,512]{1,0:T(8,128)(2,1)S(1)} %pad_maximum_fusion.1.refs_0_), channel_id=1, source_target_pairs={{0,1},{1,0},{2,3},{3,2},{4,5},{5,4},{6,7},{7,6},{8,9},{9,8},{10,11... | collective-permute-start | bytes 3194888 | tf_op jit(solution)/shard_map/ppermute | solution.py:490
  34.5 26.3 %collective-permute-start.2 = (bf16[1040,512]{1,0:T(8,128)(2,1)S(1)}, bf16[1040,512]{1,0:T(8,128)(2,1)S(1)}, u32[]{:S(2)}, u32[]{:S(2)}) collective-permute-start(bf16[1040,512]{1,0:T(8,128)(2,1)S(1)} %collective-permute-done.1.refs_2_), channel_id=1, source_target_pairs={{1,0},{2,3},{5,4},{6,7},{9,8},{10,11},{13,12},{14,15},{17,16},{18,... | collective-permute-start | bytes 3194888 | tf_op jit(solution)/shard_map/ppermute | solution.py:490
  35.8 26.0 %collective-permute-start.3 = (bf16[1040,512]{1,0:T(8,128)(2,1)S(1)}, bf16[1040,512]{1,0:T(8,128)(2,1)S(1)}, u32[]{:S(2)}, u32[]{:S(2)}) collective-permute-start(bf16[1040,512]{1,0:T(8,128)(2,1)S(1)} %collective-permute-done.refs_1_), channel_id=1, source_target_pairs={{1,2},{2,1},{5,6},{6,5},{9,10},{10,9},{13,14},{14,13},{17,18},{18,... | collective-permute-start | bytes 3194888 | tf_op jit(solution)/shard_map/ppermute | solution.py:490
  244.8 41.1 %collective-permute-start.19 = (bf16[1024,512]{1,0:T(8,128)(2,1)S(1)}, bf16[1024,512]{1,0:T(8,128)(2,1)S(1)}, u32[]{:S(2)}, u32[]{:S(2)}) collective-permute-start(bf16[1024,512]{1,0:T(8,128)(2,1)S(1)} %collective-permute-done.18.refs_4_), channel_id=1, source_target_pairs={{1,0},{2,3},{5,4},{6,7},{9,8},{10,11},{13,12},{14,15},{17,16},{18,... | collective-permute-start | bytes 3145736 | tf_op jit(solution)/shard_map/ppermute | solution.py:490
  378.1 35.2 %collective-permute-start.27 = (bf16[1024,1408]{1,0:T(8,128)(2,1)}, bf16[1024,1408]{1,0:T(8,128)(2,1)}, u32[]{:S(2)}, u32[]{:S(2)}) collective-permute-start(bf16[1024,1408]{1,0:T(8,128)(2,1)} %get-tuple-element.195), channel_id=1, source_target_pairs={{0,4},{4,0},{8,12},{12,8},{16,20},{20,16},{24,28},{28,24},{1,5},{5... | collective-permute-start | bytes 8650760 | tf_op jit(solution)/shard_map/ppermute | solution.py:683
  378.1 35.2 %collective-permute-start.28 = (bf16[1024,1408]{1,0:T(8,128)(2,1)}, bf16[1024,1408]{1,0:T(8,128)(2,1)}, u32[]{:S(2)}, u32[]{:S(2)}) collective-permute-start(bf16[1024,1408]{1,0:T(8,128)(2,1)} %get-tuple-element.196), channel_id=1, source_target_pairs={{0,4},{4,0},{8,12},{12,8},{16,20},{20,16},{24,28},{28,24},{1,5},{5... | collective-permute-start | bytes 8650760 | tf_op jit(solution)/shard_map/ppermute | solution.py:683
  378.6 34.7 %collective-permute-start.29 = (bf16[1024,1408]{1,0:T(8,128)(2,1)}, bf16[1024,1408]{1,0:T(8,128)(2,1)}, u32[]{:S(2)}, u32[]{:S(2)}) collective-permute-start(bf16[1024,1408]{1,0:T(8,128)(2,1)} %get-tuple-element.197), channel_id=1, source_target_pairs={{0,4},{4,0},{8,12},{12,8},{16,20},{20,16},{24,28},{28,24},{1,5},{5... | collective-permute-start | bytes 8650760 | tf_op jit(solution)/shard_map/ppermute | solution.py:683
  382.6 25.8 %collective-permute-start.23 = (bf16[1024,512]{1,0:T(8,128)(2,1)}, bf16[1024,512]{1,0:T(8,128)(2,1)S(1)}, u32[]{:S(2)}, u32[]{:S(2)}) collective-permute-start(bf16[1024,512]{1,0:T(8,128)(2,1)} %get-tuple-element.199), channel_id=1, source_target_pairs={{0,1},{1,0},{2,3},{3,2},{4,5},{5,4},{6,7},{7,6},{8,9},{9,8},{10,11... | collective-permute-start | bytes 3145736 | tf_op jit(solution)/shard_map/ppermute | solution.py:569
  423.9 44.9 %collective-permute-start.34 = (bf16[256,4224]{1,0:T(8,128)(2,1)}, bf16[256,4224]{1,0:T(8,128)(2,1)S(1)}, u32[]{:S(2)}, u32[]{:S(2)}) collective-permute-start(bf16[256,4224]{1,0:T(8,128)(2,1)} %get-tuple-element.221), channel_id=1, source_target_pairs={{0,8},{4,12},{8,0},{12,4},{16,24},{20,28},{24,16},{28,20},{1,9},{5... | collective-permute-start | bytes 6488072 | tf_op jit(solution)/shard_map/ppermute | solution.py:683
  425.5 45.7 %collective-permute-start.35 = (bf16[256,4224]{1,0:T(8,128)(2,1)}, bf16[256,4224]{1,0:T(8,128)(2,1)S(1)}, u32[]{:S(2)}, u32[]{:S(2)}) collective-permute-start(bf16[256,4224]{1,0:T(8,128)(2,1)} %get-tuple-element.224), channel_id=1, source_target_pairs={{0,16},{4,20},{8,24},{12,28},{16,0},{20,4},{24,8},{28,12},{1,17},{... | collective-permute-start | bytes 6488072 | tf_op jit(solution)/shard_map/ppermute | solution.py:683
  472.8 26.3 %collective-permute-start.37 = (bf16[128,4224]{1,0:T(8,128)(2,1)S(1)}, bf16[128,4224]{1,0:T(8,128)(2,1)S(1)}, u32[]{:S(2)}, u32[]{:S(2)}) collective-permute-start(bf16[128,4224]{1,0:T(8,128)(2,1)S(1)} %get-tuple-element.235), channel_id=1, source_target_pairs={{0,16},{4,20},{8,24},{12,28},{16,0},{20,4},{24,8},{28,12},{1,17},{... | collective-permute-start | bytes 3244040 | tf_op jit(solution)/shard_map/ppermute | solution.py:683
  493.9 38.7 %collective-permute-start.36 = (bf16[1024,512]{1,0:T(8,128)(2,1)}, bf16[1024,512]{1,0:T(8,128)(2,1)}, u32[]{:S(2)}, u32[]{:S(2)}) collective-permute-start(bf16[1024,512]{1,0:T(8,128)(2,1)} %add_convert_fusion.8), channel_id=1, source_target_pairs={{1,2},{2,1},{5,6},{6,5},{9,10},{10,9},{13,14},{14,13},{17,18},{18,... | collective-permute-start | bytes 3145736 | tf_op jit(solution)/shard_map/ppermute | solution.py:569
  496.0 36.6 %collective-permute-start.41 = (bf16[1024,512]{1,0:T(8,128)(2,1)}, bf16[1024,512]{1,0:T(8,128)(2,1)}, u32[]{:S(2)}, u32[]{:S(2)}) collective-permute-start(bf16[1024,512]{1,0:T(8,128)(2,1)} %constant_dynamic-slice_fusion.1), channel_id=1, source_target_pairs={{0,1},{3,2},{4,5},{7,6},{8,9},{11,10},{12,13},{15,14},{16,17},{19,... | collective-permute-start | bytes 3145736 | tf_op jit(solution)/shard_map/ppermute | solution.py:569
  539.6 58.3 %collective-permute-start.46 = (bf16[256,4224]{1,0:T(8,128)(2,1)}, bf16[256,4224]{1,0:T(8,128)(2,1)}, u32[]{:S(2)}, u32[]{:S(2)}) collective-permute-start(bf16[256,4224]{1,0:T(8,128)(2,1)} %get-tuple-element.258.refs_0_), channel_id=1, source_target_pairs={{0,8},{4,12},{8,0},{12,4},{16,24},{20,28},{24,16},{28,20},{1,9},{5... | collective-permute-start | bytes 6488072 | tf_op jit(solution)/shard_map/ppermute | solution.py:683
  551.0 45.3 %collective-permute-start.47 = (bf16[256,4224]{1,0:T(8,128)(2,1)}, bf16[256,4224]{1,0:T(8,128)(2,1)}, u32[]{:S(2)}, u32[]{:S(2)}) collective-permute-start(bf16[256,4224]{1,0:T(8,128)(2,1)} %get-tuple-element.259.refs_2_), channel_id=1, source_target_pairs={{0,16},{4,20},{8,24},{12,28},{16,0},{20,4},{24,8},{28,12},{1,17},{... | collective-permute-start | bytes 6488072 | tf_op jit(solution)/shard_map/ppermute | solution.py:683
  590.2 25.7 %collective-permute-start.49 = (bf16[256,2048]{1,0:T(8,128)(2,1)}, bf16[256,2048]{1,0:T(8,128)(2,1)S(1)}, u32[]{:S(2)}, u32[]{:S(2)}) collective-permute-start(bf16[256,2048]{1,0:T(8,128)(2,1)} %get-tuple-element.265), channel_id=1, source_target_pairs={{0,16},{4,20},{8,24},{12,28},{16,0},{20,4},{24,8},{28,12},{1,17},{... | collective-permute-start | bytes 3145736 | tf_op jit(solution)/shard_map/ppermute | solution.py:683
  593.8 32.1 %collective-permute-start.50 = (bf16[1040,512]{1,0:T(8,128)(2,1)}, bf16[1040,512]{1,0:T(8,128)(2,1)}, u32[]{:S(2)}, u32[]{:S(2)}) collective-permute-start(bf16[1040,512]{1,0:T(8,128)(2,1)} %get-tuple-element.268), channel_id=1, source_target_pairs={{0,1},{1,0},{2,3},{3,2},{4,5},{5,4},{6,7},{7,6},{8,9},{9,8},{10,11... | collective-permute-start | bytes 3194888 | tf_op jit(solution)/shard_map/ppermute | solution.py:569
  596.3 29.7 %collective-permute-start.51 = (bf16[1040,512]{1,0:T(8,128)(2,1)}, bf16[1040,512]{1,0:T(8,128)(2,1)}, u32[]{:S(2)}, u32[]{:S(2)}) collective-permute-start(bf16[1040,512]{1,0:T(8,128)(2,1)} %get-tuple-element.270), channel_id=1, source_target_pairs={{1,2},{2,1},{5,6},{6,5},{9,10},{10,9},{13,14},{14,13},{17,18},{18,... | collective-permute-start | bytes 3194888 | tf_op jit(solution)/shard_map/ppermute | solution.py:569
  606.3 37.8 %collective-permute-start.54 = (bf16[1024,1408]{1,0:T(8,128)(2,1)}, bf16[1024,1408]{1,0:T(8,128)(2,1)}, u32[]{:S(2)}, u32[]{:S(2)}) collective-permute-start(bf16[1024,1408]{1,0:T(8,128)(2,1)} %bitcast.67), channel_id=1, source_target_pairs={{0,4},{4,0},{8,12},{12,8},{16,20},{20,16},{24,28},{28,24},{1,5},{5... | collective-permute-start | bytes 8650760 | tf_op jit(solution)/shard_map/ppermute | solution.py:683
  625.9 42.3 %collective-permute-start.58 = (bf16[1024,1408]{1,0:T(8,128)(2,1)}, bf16[1024,1408]{1,0:T(8,128)(2,1)}, u32[]{:S(2)}, u32[]{:S(2)}) collective-permute-start(bf16[1024,1408]{1,0:T(8,128)(2,1)} %bitcast.69), channel_id=1, source_target_pairs={{0,4},{4,0},{8,12},{12,8},{16,20},{20,16},{24,28},{28,24},{1,5},{5... | collective-permute-start | bytes 8650760 | tf_op jit(solution)/shard_map/ppermute | solution.py:683
  626.0 42.8 %collective-permute-start.59 = (bf16[1024,1408]{1,0:T(8,128)(2,1)}, bf16[1024,1408]{1,0:T(8,128)(2,1)}, u32[]{:S(2)}, u32[]{:S(2)}) collective-permute-start(bf16[1024,1408]{1,0:T(8,128)(2,1)} %bitcast.71), channel_id=1, source_target_pairs={{0,4},{4,0},{8,12},{12,8},{16,20},{20,16},{24,28},{28,24},{1,5},{5... | collective-permute-start | bytes 8650760 | tf_op jit(solution)/shard_map/ppermute | solution.py:683
  659.0 34.5 %collective-permute-start.62 = (bf16[256,2048]{1,0:T(8,128)(2,1)}, bf16[256,2048]{1,0:T(8,128)(2,1)}, u32[]{:S(2)}, u32[]{:S(2)}) collective-permute-start(bf16[256,2048]{1,0:T(8,128)(2,1)} %get-tuple-element.292.refs_0_), channel_id=1, source_target_pairs={{0,8},{4,12},{8,0},{12,4},{16,24},{20,28},{24,16},{28,20},{1,9},{5... | collective-permute-start | bytes 3145736 | tf_op jit(solution)/shard_map/ppermute | solution.py:683
  663.0 30.5 %collective-permute-start.61 = (bf16[1024,512]{1,0:T(8,128)(2,1)}, bf16[1024,512]{1,0:T(8,128)(2,1)}, u32[]{:S(2)}, u32[]{:S(2)}) collective-permute-start(bf16[1024,512]{1,0:T(8,128)(2,1)} %get-tuple-element.291), channel_id=1, source_target_pairs={{1,2},{2,1},{5,6},{6,5},{9,10},{10,9},{13,14},{14,13},{17,18},{18,... | collective-permute-start | bytes 3145736 | tf_op jit(solution)/shard_map/ppermute | solution.py:569
  664.9 28.6 %collective-permute-start.57 = (bf16[1024,512]{1,0:T(8,128)(2,1)}, bf16[1024,512]{1,0:T(8,128)(2,1)}, u32[]{:S(2)}, u32[]{:S(2)}) collective-permute-start(bf16[1024,512]{1,0:T(8,128)(2,1)} %get-tuple-element.283), channel_id=1, source_target_pairs={{0,1},{1,0},{2,3},{3,2},{4,5},{5,4},{6,7},{7,6},{8,9},{9,8},{10,11... | collective-permute-start | bytes 3145736 | tf_op jit(solution)/shard_map/ppermute | solution.py:569
  (134 other events, 1880.5 us)

commit v6 on v5

--- a/solution.py
+++ b/solution.py
@@ -174,7 +174,7 @@
             pl.BlockSpec((1, t, width), lambda k: (k, c, 0)),
         ],
         previous,
-        mib=34,
+        mib=56,
         name="project",
     )
 
@@ -515,7 +515,7 @@
             got = self.step(order)
         return got
 
-    def whole(self):
+    def whole(self, mib=14):
         share = self.pieces[0]
         t, width = share.shape
         return prefetched(
@@ -526,7 +526,7 @@
             [still((t, width), lambda j, me: (0, 0))] * len(self.pieces),
             [sds((t, self.n * width), share.dtype)],
             [pl.BlockSpec((t, width), lambda j, me: (0, j))],
-            mib=14,
+            mib=mib,
             name="assemble",
         )[0]
 
@@ -859,7 +859,7 @@
         for k in range(2):
             outs[0][:, k, :] = arrays[k][...].astype(F32)
 
-    units, block = own[0].shape[1], 128
+    units, block = own[0].shape[1], 256
     outs, spec = [sds((D, 2, units), F32)], [pl.BlockSpec((block, 2, units), lambda i, c: (i, 0, 0))]
     return from_halves(store, core, own, other, outs, spec, block, 56, "gate_up_out")[0]
 
@@ -868,7 +868,7 @@
     def store(arrays, outs):
         outs[0][...] = arrays[0][...].astype(F32).T
 
-    units, block = own[0].shape[1], 128
+    units, block = own[0].shape[1], 256
     outs, spec = [sds((units, D), F32)], [pl.BlockSpec((units, block), lambda i, c: (0, i))]
     return from_halves(store, core, own, other, outs, spec, block, 56, "down_out")[0]
 
@@ -920,7 +920,7 @@
     tables = rope_tables()
     order.done(*got, up_w, tables)
     whole_x.last(order)
-    x = whole_x.whole()
+    x = whole_x.whole(56)
     gain_one, gain_two, shift_two = (x[t + i : t + i + 1].astype(F32) for i in (0, 2, 3))
     project_w = project_weight.transpose(1, 0, 2)
     bias = project_bias.astype(F32)[:, None, :]

time: 722 us -> 715 us (level)
  local copies, waits for them, and re-layouts: 72.4 us -> 63.1 us
    unnamed x181 -> x171, local copies, waits for them, and re-layouts: 47.4 us -> 37.6 us
where the time goes in v6:
time: 715 us; the launch traced here: 708 us
  Pallas kernels  265 us (37%)
  waiting for transfers between devices  216 us (30%)
  starting transfers between devices  113 us (16%)
  local copies, waits for them, and re-layouts  63.1 us (9%)
  other arithmetic  46.6 us (7%)
    pallas_call x25, Pallas kernels, prefetched(): pl.pallas_call(body, grid_spec=pltpu.PrefetchScalarGridSpec(num_scalar_pr...  183 us
    ppermute x20, waiting for transfers between devices, send(): self.pieces.append(lax.ppermute(order(self.pieces[piece]), 'tensor', pairs))  147 us
    pallas_call x4, Pallas kernels, kernel_call(): pl.pallas_call(run, grid=grid, in_specs=list(in_specs) + [ANY] * len(prev...  81.4 us
    ppermute x20, starting transfers between devices, send(): self.got[name] = lax.ppermute(order(value), 'tensor', pairs)  60.8 us
    ppermute x20, waiting for transfers between devices, send(): self.got[name] = lax.ppermute(order(value), 'tensor', pairs)  42.3 us
    unnamed x171, local copies, waits for them, and re-layouts  37.6 us
    ppermute x20, starting transfers between devices, send(): self.pieces.append(lax.ppermute(order(self.pieces[piece]), 'tensor', pairs))  30 us
    ppermute x25, waiting for transfers between devices, swap(): return lax.ppermute(value, axis, [(i, i ^ 1 << bit) for i in range(n)])  25.9 us
  transfers between devices with their start and end apart: 68, of which 23 were waited for; matrix products, arithmetic and copies ran while one was open for 10% of the time, Pallas kernels for 26%

profile of v6, /device:TPU:0, one launch (start us, length us, event | category | flops | bytes accessed | tf_op | source)
XLA Modules:
  0.0 708.3 jit_solution(2967781050086717612)
XLA Ops:
  22.3 12.2 %collective-permute-done.refs_1_ = bf16[1040,512]{1,0:T(8,128)(2,1)S(1)} collective-permute-done((bf16[1040,512]{1,0:T(8,128)(2,1)S(1)}, bf16[1040,512]{1,0:T(8,128)(2,1)S(1)}, u32[]{:S(2)}, u32[]{:S(2)}) %collective-permute-start) | collective-permute-done | bytes 1064992 | tf_op jit(solution)/shard_map/ppermute | solution.py:490
  47.0 13.7 %collective-permute-done.2.refs_3_ = bf16[1040,512]{1,0:T(8,128)(2,1)S(1)} collective-permute-done((bf16[1040,512]{1,0:T(8,128)(2,1)S(1)}, bf16[1040,512]{1,0:T(8,128)(2,1)S(1)}, u32[]{:S(2)}, u32[]{:S(2)}) %collective-permute-start.2) | collective-permute-done | bytes 1064992 | tf_op jit(solution)/shard_map/ppermute | solution.py:490
  63.0 24.2 %collective-permute-done.4.refs_5_ = bf16[1040,512]{1,0:T(8,128)(2,1)S(1)} collective-permute-done((bf16[1040,512]{1,0:T(8,128)(2,1)S(1)}, bf16[1040,512]{1,0:T(8,128)(2,1)S(1)}, u32[]{:S(2)}, u32[]{:S(2)}) %collective-permute-start.4) | collective-permute-done | bytes 1064992 | tf_op jit(solution)/shard_map/ppermute | solution.py:490
  96.7 20.2 %project.1 = (bf16[1024,2048]{1,0:T(8,128)(2,1)}, f32[1024,128]{1,0:T(8,128)}, bf16[3,1024,512]{2,1,0:T(8,128)(2,1)}) custom-call(bf16[1040,2048]{1,0:T(8,128)(2,1)} %assemble.4.refs_0_.refs_1_.x_ref, bf16[1040,2048]{1,0:T(8,128)(2,1)} %assemble.4.refs_0_.refs_1_.x_ref, bf16[3,2048,512]{2,1,0:T(8,128)(2,1)} %bitcast.50, f32[3,1,512]{2,1,0:T(1,128)} %copy.27.refs_3_, ...), custom_call_target="tpu_custom_call" | custom-call | tf_op jit(solution)/shard_map/project/pallas_call | solution.py:53
  121.5 16.9 %attend.1 = (bf16[1024,512]{1,0:T(8,128)(2,1)S(1)}, bf16[1024,1536]{1,0:T(8,128)(2,1)S(1)}, bf16[1024,512]{1,0:T(8,128)(2,1)S(1)}, f32[1024,512]{1,0:T(8,128)S(1)}) custom-call(s32[4]{0:T(128)S(1)} %pad_add_fusion.owners_ref, bf16[3,1024,512]{2,1,0:T(8,128)(2,1)S(1)} %copy-done.4, bf16[3,1024,512]{2,1,0:T(8,128)(2,1)S(1)} %copy-done.4, ...), custom_call_target="tpu_custom_call" | custom-call | tf_op jit(solution)/shard_map/attend/pallas_call | solution.py:76
  151.3 10.5 %collective-permute-done.8.refs_3_ = bf16[1024,512]{1,0:T(8,128)(2,1)S(1)} collective-permute-done((bf16[1024,512]{1,0:T(8,128)(2,1)}, bf16[1024,512]{1,0:T(8,128)(2,1)S(1)}, u32[]{:S(2)}, u32[]{:S(2)}) %collective-permute-start.8) | collective-permute-done | bytes 1048608 | tf_op jit(solution)/shard_map/ppermute | solution.py:490
  177.4 14.2 %collective-permute-done.11.refs_5_ = bf16[1024,512]{1,0:T(8,128)(2,1)} collective-permute-done((bf16[1024,512]{1,0:T(8,128)(2,1)}, bf16[1024,512]{1,0:T(8,128)(2,1)}, u32[]{:S(2)}, u32[]{:S(2)}) %collective-permute-start.11) | collective-permute-done | bytes 1048608 | tf_op jit(solution)/shard_map/ppermute | solution.py:490
  205.3 16.5 %collective-permute-done.13 = bf16[1024,512]{1,0:T(8,128)(2,1)} collective-permute-done((bf16[1024,512]{1,0:T(8,128)(2,1)}, bf16[1024,512]{1,0:T(8,128)(2,1)}, u32[]{:S(2)}, u32[]{:S(2)}) %collective-permute-start.13) | collective-permute-done | bytes 1048608 | tf_op jit(solution)/shard_map/ppermute | solution.py:569
  227.2 17.5 %collective-permute-done.15.refs_1_ = bf16[1024,512]{1,0:T(8,128)(2,1)S(1)} collective-permute-done((bf16[1024,512]{1,0:T(8,128)(2,1)S(1)}, bf16[1024,512]{1,0:T(8,128)(2,1)S(1)}, u32[]{:S(2)}, u32[]{:S(2)}) %collective-permute-start.15) | collective-permute-done | bytes 1048608 | tf_op jit(solution)/shard_map/ppermute | solution.py:490
  254.6 11.4 %collective-permute-done.17.refs_3_ = bf16[1024,512]{1,0:T(8,128)(2,1)S(1)} collective-permute-done((bf16[1024,512]{1,0:T(8,128)(2,1)S(1)}, bf16[1024,512]{1,0:T(8,128)(2,1)S(1)}, u32[]{:S(2)}, u32[]{:S(2)}) %collective-permute-start.17) | collective-permute-done | bytes 1048608 | tf_op jit(solution)/shard_map/ppermute | solution.py:490
  266.0 21.7 %collective-permute-done.19.refs_5_ = bf16[1024,512]{1,0:T(8,128)(2,1)S(1)} collective-permute-done((bf16[1024,512]{1,0:T(8,128)(2,1)S(1)}, bf16[1024,512]{1,0:T(8,128)(2,1)S(1)}, u32[]{:S(2)}, u32[]{:S(2)}) %collective-permute-start.19) | collective-permute-done | bytes 1048608 | tf_op jit(solution)/shard_map/ppermute | solution.py:490
  290.5 32.2 %mlp.1 = (bf16[1024,2048]{1,0:T(8,128)(2,1)}, f32[1024,128]{1,0:T(8,128)S(1)}, bf16[1024,1408]{1,0:T(8,128)(2,1)S(1)}, bf16[1024,1408]{1,0:T(8,128)(2,1)S(1)}, bf16[1024,1408]{1,0:T(8,128)(2,1)}) custom-call(bf16[1024,2048]{1,0:T(8,128)(2,1)} %copy-done.2, bf16[1024,2048]{1,0:T(8,128)(2,1)} %copy-done, f32[1,2048]{1,0:T(1,128)S(1)} %get-tuple-element.313.refs_2_, ...), custom_call_target="tpu_custom_call" | custom-call | tf_op jit(solution)/shard_map/mlp/pallas_call | solution.py:53
  336.1 15.7 %mlp_back.3 = bf16[1024,1536]{1,0:T(8,128)(2,1)} custom-call(s32[3]{0:T(128)} %pad_add_fusion.1.owners_ref, bf16[1024,1408]{1,0:T(8,128)(2,1)} %copy-done.6, bf16[1024,1408]{1,0:T(8,128)(2,1)} %get-tuple-element.187.dup_ref.refs_3_, bf16[2048,1408]{1,0:T(8,128)(2,1)} %bitcast.65, bf16[2048,1408]{1,0:T(8,128)(2,1)} %slice_bitcast_fusion.refs_5_.up_w_ref), custom_call_target="tpu_custom_call" | custom-call | tf_op jit(solution)/shard_map/mlp_back/pallas_call | solution.py:76
  362.8 15.6 %mlp_given.1 = (bf16[1024,1408]{1,0:T(8,128)(2,1)}, bf16[1024,1408]{1,0:T(8,128)(2,1)}, bf16[1024,1408]{1,0:T(8,128)(2,1)}) custom-call(s32[1]{0:T(128)} %bitcast.12.which_ref, bf16[1024,2048]{1,0:T(8,128)(2,1)} %get-tuple-element.193.refs_0_, bf16[1024,2048]{1,0:T(8,128)(2,1)} %copy-done, bf16[1024,1408]{1,0:T(8,128)(2,1)} %copy-done.6, ...), custom_call_target="tpu_custom_call" | custom-call | tf_op jit(solution)/shard_map/mlp_given/pallas_call | solution.py:76
  387.6 15.4 %mlp_kept.1 = (bf16[1024,1408]{1,0:T(8,128)(2,1)}, bf16[1024,1408]{1,0:T(8,128)(2,1)}, bf16[1024,1408]{1,0:T(8,128)(2,1)}) custom-call(s32[1]{0:T(128)} %bitcast.13.which_ref.core_ref, bf16[1024,2048]{1,0:T(8,128)(2,1)} %get-tuple-element.193.refs_0_, bf16[1024,2048]{1,0:T(8,128)(2,1)} %copy-done, bf16[1024,1408]{1,0:T(8,128)(2,1)} %copy-done.6, ...), custom_call_target="tpu_custom_call" | custom-call | flops 30000001024 | tf_op jit(solution)/shard_map/mlp_kept/pallas_call | solution.py:76
  413.9 10.7 %split.4 = (bf16[256,4224]{1,0:T(8,128)(2,1)}, bf16[256,4224]{1,0:T(8,128)(2,1)}, bf16[256,4224]{1,0:T(8,128)(2,1)}, bf16[256,4224]{1,0:T(8,128)(2,1)}) custom-call(s32[2]{0:T(128)} %pad_add_fusion.2.bits_ref, bf16[1024,1408]{1,0:T(8,128)(2,1)} %get-tuple-element.209.refs_0_.refs_6_, bf16[1024,1408]{1,0:T(8,128)(2,1)} %collective-permute-done.27.refs_1_.refs_7_, ...), custom_call_target="tpu_custom_call" | custom-call | tf_op jit(solution)/shard_map/split/pallas_call | solution.py:76
  437.3 8.9 %mlp_out.1 = (bf16[1024,512]{1,0:T(8,128)(2,1)S(1)}, bf16[1024,1536]{1,0:T(8,128)(2,1)S(1)}) custom-call(s32[4]{0:T(128)S(1)} %pad_add_fusion.owners_ref, bf16[1024,1408]{1,0:T(8,128)(2,1)S(1)} %copy-done.35, bf16[1408,2048]{1,0:T(8,128)(2,1)S(1)} %bitcast.60), custom_call_target="tpu_custom_call" | custom-call | flops 10000000000 | tf_op jit(solution)/shard_map/mlp_out/pallas_call | solution.py:76
  446.1 10.4 %collective-permute-done.30.refs_3_ = bf16[1024,512]{1,0:T(8,128)(2,1)S(1)} collective-permute-done((bf16[1024,512]{1,0:T(8,128)(2,1)}, bf16[1024,512]{1,0:T(8,128)(2,1)S(1)}, u32[]{:S(2)}, u32[]{:S(2)}) %collective-permute-start.30) | collective-permute-done | bytes 1048608 | tf_op jit(solution)/shard_map/ppermute | solution.py:490
  505.6 21.2 %attend_back.1 = (bf16[1024,512]{1,0:T(8,128)(2,1)S(1)}, bf16[1024,512]{1,0:T(8,128)(2,1)S(1)}, bf16[1024,512]{1,0:T(8,128)(2,1)S(1)}, f32[8,1024]{1,0:T(8,128)S(1)}) custom-call(bf16[3,1024,512]{2,1,0:T(8,128)(2,1)S(1)} %copy-done.5, bf16[3,1024,512]{2,1,0:T(8,128)(2,1)S(1)} %copy-done.5, bf16[3,1024,512]{2,1,0:T(8,128)(2,1)S(1)} %copy-done.5, ...), custom_call_target="tpu_custom_call" | custom-call | flops 20000000000 | tf_op jit(solution)/shard_map/attend_back/pallas_call | solution.py:53
  576.0 14.4 %collective-permute-done.45 = bf16[1040,512]{1,0:T(8,128)(2,1)S(1)} collective-permute-done((bf16[1040,512]{1,0:T(8,128)(2,1)S(1)}, bf16[1040,512]{1,0:T(8,128)(2,1)S(1)}, u32[]{:S(2)}, u32[]{:S(2)}) %collective-permute-start.45) | collective-permute-done | bytes 1064992 | tf_op jit(solution)/shard_map/ppermute | solution.py:569
  598.8 8.3 %merge.5 = (bf16[2,512,1408]{2,1,0:T(8,128)(2,1)}, bf16[2,512,1408]{2,1,0:T(8,128)(2,1)}, bf16[2,512,1408]{2,1,0:T(8,128)(2,1)}) custom-call(s32[2]{0:T(128)} %pad_add_fusion.2.bits_ref, bf16[256,4224]{1,0:T(8,128)(2,1)} %get-tuple-element.258.refs_0_, bf16[256,4224]{1,0:T(8,128)(2,1)} %collective-permute-done.46.refs_1_, ...), custom_call_target="tpu_custom_call" | custom-call | flops 15000000512 | tf_op jit(solution)/shard_map/merge/pallas_call | solution.py:76
  607.2 8.4 %collective-permute-done.48.refs_1_ = bf16[256,2048]{1,0:T(8,128)(2,1)S(1)} collective-permute-done((bf16[256,2048]{1,0:T(8,128)(2,1)}, bf16[256,2048]{1,0:T(8,128)(2,1)S(1)}, u32[]{:S(2)}, u32[]{:S(2)}) %collective-permute-start.48) | collective-permute-done | bytes 1048608 | tf_op jit(solution)/shard_map/ppermute | solution.py:683
  644.6 9.5 %down_out.1 = f32[1408,2048]{1,0:T(8,128)} custom-call(s32[1]{0:T(128)} %bitcast.13.which_ref.core_ref, bf16[1024,1408]{1,0:T(8,128)(2,1)} %bitcast.68, bf16[1024,1408]{1,0:T(8,128)(2,1)} %collective-permute-done.54.refs_1_), custom_call_target="tpu_custom_call" | custom-call | tf_op jit(solution)/shard_map/down_out/pallas_call | solution.py:76
  665.2 14.7 %gate_up_out.1 = f32[2048,2,1408]{2,1,0:T(2,128)} custom-call(s32[1]{0:T(128)} %bitcast.13.which_ref.core_ref, bf16[1024,1408]{1,0:T(8,128)(2,1)} %bitcast.70, bf16[1024,1408]{1,0:T(8,128)(2,1)} %bitcast.72, bf16[1024,1408]{1,0:T(8,128)(2,1)} %collective-permute-done.58.refs_2_, bf16[1024,1408]{1,0:T(8,128)(2,1)} %collective-permute-done.59.refs_3_), custom_call_target="tpu_custom_call" | custom-call | tf_op jit(solution)/shard_map/gate_up_out/pallas_call | solution.py:76
  (383 shorter events, 342.0 us)
Async XLA Ops:
  5.4 29.1 %collective-permute-start = (bf16[1040,512]{1,0:T(8,128)(2,1)S(1)}, bf16[1040,512]{1,0:T(8,128)(2,1)S(1)}, u32[]{:S(2)}, u32[]{:S(2)}) collective-permute-start(bf16[1040,512]{1,0:T(8,128)(2,1)S(1)} %pad_maximum_fusion.1.refs_0_), channel_id=1, source_target_pairs={{0,1},{1,0},{2,3},{3,2},{4,5},{5,4},{6,7},{7,6},{8,9},{9,8},{10,11... | collective-permute-start | bytes 3194888 | tf_op jit(solution)/shard_map/ppermute | solution.py:490
  34.5 26.3 %collective-permute-start.2 = (bf16[1040,512]{1,0:T(8,128)(2,1)S(1)}, bf16[1040,512]{1,0:T(8,128)(2,1)S(1)}, u32[]{:S(2)}, u32[]{:S(2)}) collective-permute-start(bf16[1040,512]{1,0:T(8,128)(2,1)S(1)} %collective-permute-done.1.refs_2_), channel_id=1, source_target_pairs={{1,0},{2,3},{5,4},{6,7},{9,8},{10,11},{13,12},{14,15},{17,16},{18,... | collective-permute-start | bytes 3194888 | tf_op jit(solution)/shard_map/ppermute | solution.py:490
  247.3 40.4 %collective-permute-start.19 = (bf16[1024,512]{1,0:T(8,128)(2,1)S(1)}, bf16[1024,512]{1,0:T(8,128)(2,1)S(1)}, u32[]{:S(2)}, u32[]{:S(2)}) collective-permute-start(bf16[1024,512]{1,0:T(8,128)(2,1)S(1)} %collective-permute-done.18.refs_4_), channel_id=1, source_target_pairs={{1,0},{2,3},{5,4},{6,7},{9,8},{10,11},{13,12},{14,15},{17,16},{18,... | collective-permute-start | bytes 3145736 | tf_op jit(solution)/shard_map/ppermute | solution.py:490
  378.4 35.6 %collective-permute-start.27 = (bf16[1024,1408]{1,0:T(8,128)(2,1)}, bf16[1024,1408]{1,0:T(8,128)(2,1)}, u32[]{:S(2)}, u32[]{:S(2)}) collective-permute-start(bf16[1024,1408]{1,0:T(8,128)(2,1)} %get-tuple-element.195), channel_id=1, source_target_pairs={{0,4},{4,0},{8,12},{12,8},{16,20},{20,16},{24,28},{28,24},{1,5},{5... | collective-permute-start | bytes 8650760 | tf_op jit(solution)/shard_map/ppermute | solution.py:683
  378.4 35.6 %collective-permute-start.28 = (bf16[1024,1408]{1,0:T(8,128)(2,1)}, bf16[1024,1408]{1,0:T(8,128)(2,1)}, u32[]{:S(2)}, u32[]{:S(2)}) collective-permute-start(bf16[1024,1408]{1,0:T(8,128)(2,1)} %get-tuple-element.196), channel_id=1, source_target_pairs={{0,4},{4,0},{8,12},{12,8},{16,20},{20,16},{24,28},{28,24},{1,5},{5... | collective-permute-start | bytes 8650760 | tf_op jit(solution)/shard_map/ppermute | solution.py:683
  378.9 35.1 %collective-permute-start.29 = (bf16[1024,1408]{1,0:T(8,128)(2,1)}, bf16[1024,1408]{1,0:T(8,128)(2,1)}, u32[]{:S(2)}, u32[]{:S(2)}) collective-permute-start(bf16[1024,1408]{1,0:T(8,128)(2,1)} %get-tuple-element.197), channel_id=1, source_target_pairs={{0,4},{4,0},{8,12},{12,8},{16,20},{20,16},{24,28},{28,24},{1,5},{5... | collective-permute-start | bytes 8650760 | tf_op jit(solution)/shard_map/ppermute | solution.py:683
  382.8 25.8 %collective-permute-start.23 = (bf16[1024,512]{1,0:T(8,128)(2,1)}, bf16[1024,512]{1,0:T(8,128)(2,1)S(1)}, u32[]{:S(2)}, u32[]{:S(2)}) collective-permute-start(bf16[1024,512]{1,0:T(8,128)(2,1)} %get-tuple-element.199), channel_id=1, source_target_pairs={{0,1},{1,0},{2,3},{3,2},{4,5},{5,4},{6,7},{7,6},{8,9},{9,8},{10,11... | collective-permute-start | bytes 3145736 | tf_op jit(solution)/shard_map/ppermute | solution.py:569
  424.7 45.6 %collective-permute-start.34 = (bf16[256,4224]{1,0:T(8,128)(2,1)}, bf16[256,4224]{1,0:T(8,128)(2,1)S(1)}, u32[]{:S(2)}, u32[]{:S(2)}) collective-permute-start(bf16[256,4224]{1,0:T(8,128)(2,1)} %get-tuple-element.221), channel_id=1, source_target_pairs={{0,8},{4,12},{8,0},{12,4},{16,24},{20,28},{24,16},{28,20},{1,9},{5... | collective-permute-start | bytes 6488072 | tf_op jit(solution)/shard_map/ppermute | solution.py:683
  426.2 45.7 %collective-permute-start.35 = (bf16[256,4224]{1,0:T(8,128)(2,1)}, bf16[256,4224]{1,0:T(8,128)(2,1)S(1)}, u32[]{:S(2)}, u32[]{:S(2)}) collective-permute-start(bf16[256,4224]{1,0:T(8,128)(2,1)} %get-tuple-element.224), channel_id=1, source_target_pairs={{0,16},{4,20},{8,24},{12,28},{16,0},{20,4},{24,8},{28,12},{1,17},{... | collective-permute-start | bytes 6488072 | tf_op jit(solution)/shard_map/ppermute | solution.py:683
  457.8 26.2 %collective-permute-start.32 = (bf16[1024,512]{1,0:T(8,128)(2,1)S(1)}, bf16[1024,512]{1,0:T(8,128)(2,1)S(1)}, u32[]{:S(2)}, u32[]{:S(2)}) collective-permute-start(bf16[1024,512]{1,0:T(8,128)(2,1)S(1)} %get-tuple-element.218), channel_id=1, source_target_pairs={{0,1},{3,2},{4,5},{7,6},{8,9},{11,10},{12,13},{15,14},{16,17},{19,... | collective-permute-start | bytes 3145736 | tf_op jit(solution)/shard_map/ppermute | solution.py:569
  473.5 27.2 %collective-permute-start.37 = (bf16[128,4224]{1,0:T(8,128)(2,1)S(1)}, bf16[128,4224]{1,0:T(8,128)(2,1)S(1)}, u32[]{:S(2)}, u32[]{:S(2)}) collective-permute-start(bf16[128,4224]{1,0:T(8,128)(2,1)S(1)} %get-tuple-element.235), channel_id=1, source_target_pairs={{0,16},{4,20},{8,24},{12,28},{16,0},{20,4},{24,8},{28,12},{1,17},{... | collective-permute-start | bytes 3244040 | tf_op jit(solution)/shard_map/ppermute | solution.py:683
  476.2 25.8 %collective-permute-start.38 = (bf16[128,4224]{1,0:T(8,128)(2,1)S(1)}, bf16[128,4224]{1,0:T(8,128)(2,1)S(1)}, u32[]{:S(2)}, u32[]{:S(2)}) collective-permute-start(bf16[128,4224]{1,0:T(8,128)(2,1)S(1)} %get-tuple-element.238), channel_id=1, source_target_pairs={{0,8},{4,12},{8,0},{12,4},{16,24},{20,28},{24,16},{28,20},{1,9},{5... | collective-permute-start | bytes 3244040 | tf_op jit(solution)/shard_map/ppermute | solution.py:683
  494.7 38.9 %collective-permute-start.36 = (bf16[1024,512]{1,0:T(8,128)(2,1)}, bf16[1024,512]{1,0:T(8,128)(2,1)}, u32[]{:S(2)}, u32[]{:S(2)}) collective-permute-start(bf16[1024,512]{1,0:T(8,128)(2,1)} %add_convert_fusion.8), channel_id=1, source_target_pairs={{1,2},{2,1},{5,6},{6,5},{9,10},{10,9},{13,14},{14,13},{17,18},{18,... | collective-permute-start | bytes 3145736 | tf_op jit(solution)/shard_map/ppermute | solution.py:569
  496.8 36.8 %collective-permute-start.41 = (bf16[1024,512]{1,0:T(8,128)(2,1)}, bf16[1024,512]{1,0:T(8,128)(2,1)}, u32[]{:S(2)}, u32[]{:S(2)}) collective-permute-start(bf16[1024,512]{1,0:T(8,128)(2,1)} %constant_dynamic-slice_fusion.1), channel_id=1, source_target_pairs={{0,1},{3,2},{4,5},{7,6},{8,9},{11,10},{12,13},{15,14},{16,17},{19,... | collective-permute-start | bytes 3145736 | tf_op jit(solution)/shard_map/ppermute | solution.py:569
  540.6 58.3 %collective-permute-start.46 = (bf16[256,4224]{1,0:T(8,128)(2,1)}, bf16[256,4224]{1,0:T(8,128)(2,1)}, u32[]{:S(2)}, u32[]{:S(2)}) collective-permute-start(bf16[256,4224]{1,0:T(8,128)(2,1)} %get-tuple-element.258.refs_0_), channel_id=1, source_target_pairs={{0,8},{4,12},{8,0},{12,4},{16,24},{20,28},{24,16},{28,20},{1,9},{5... | collective-permute-start | bytes 6488072 | tf_op jit(solution)/shard_map/ppermute | solution.py:683
  552.2 45.0 %collective-permute-start.47 = (bf16[256,4224]{1,0:T(8,128)(2,1)}, bf16[256,4224]{1,0:T(8,128)(2,1)}, u32[]{:S(2)}, u32[]{:S(2)}) collective-permute-start(bf16[256,4224]{1,0:T(8,128)(2,1)} %get-tuple-element.259.refs_2_), channel_id=1, source_target_pairs={{0,16},{4,20},{8,24},{12,28},{16,0},{20,4},{24,8},{28,12},{1,17},{... | collective-permute-start | bytes 6488072 | tf_op jit(solution)/shard_map/ppermute | solution.py:683
  591.1 25.7 %collective-permute-start.49 = (bf16[256,2048]{1,0:T(8,128)(2,1)}, bf16[256,2048]{1,0:T(8,128)(2,1)S(1)}, u32[]{:S(2)}, u32[]{:S(2)}) collective-permute-start(bf16[256,2048]{1,0:T(8,128)(2,1)} %get-tuple-element.265), channel_id=1, source_target_pairs={{0,16},{4,20},{8,24},{12,28},{16,0},{20,4},{24,8},{28,12},{1,17},{... | collective-permute-start | bytes 3145736 | tf_op jit(solution)/shard_map/ppermute | solution.py:683
  594.7 32.0 %collective-permute-start.50 = (bf16[1040,512]{1,0:T(8,128)(2,1)}, bf16[1040,512]{1,0:T(8,128)(2,1)}, u32[]{:S(2)}, u32[]{:S(2)}) collective-permute-start(bf16[1040,512]{1,0:T(8,128)(2,1)} %get-tuple-element.268), channel_id=1, source_target_pairs={{0,1},{1,0},{2,3},{3,2},{4,5},{5,4},{6,7},{7,6},{8,9},{9,8},{10,11... | collective-permute-start | bytes 3194888 | tf_op jit(solution)/shard_map/ppermute | solution.py:569
  597.2 29.6 %collective-permute-start.51 = (bf16[1040,512]{1,0:T(8,128)(2,1)}, bf16[1040,512]{1,0:T(8,128)(2,1)}, u32[]{:S(2)}, u32[]{:S(2)}) collective-permute-start(bf16[1040,512]{1,0:T(8,128)(2,1)} %get-tuple-element.270), channel_id=1, source_target_pairs={{1,2},{2,1},{5,6},{6,5},{9,10},{10,9},{13,14},{14,13},{17,18},{18,... | collective-permute-start | bytes 3194888 | tf_op jit(solution)/shard_map/ppermute | solution.py:569
  607.2 37.4 %collective-permute-start.54 = (bf16[1024,1408]{1,0:T(8,128)(2,1)}, bf16[1024,1408]{1,0:T(8,128)(2,1)}, u32[]{:S(2)}, u32[]{:S(2)}) collective-permute-start(bf16[1024,1408]{1,0:T(8,128)(2,1)} %bitcast.67), channel_id=1, source_target_pairs={{0,4},{4,0},{8,12},{12,8},{16,20},{20,16},{24,28},{28,24},{1,5},{5... | collective-permute-start | bytes 8650760 | tf_op jit(solution)/shard_map/ppermute | solution.py:683
  626.6 37.6 %collective-permute-start.58 = (bf16[1024,1408]{1,0:T(8,128)(2,1)}, bf16[1024,1408]{1,0:T(8,128)(2,1)}, u32[]{:S(2)}, u32[]{:S(2)}) collective-permute-start(bf16[1024,1408]{1,0:T(8,128)(2,1)} %bitcast.69), channel_id=1, source_target_pairs={{0,4},{4,0},{8,12},{12,8},{16,20},{20,16},{24,28},{28,24},{1,5},{5... | collective-permute-start | bytes 8650760 | tf_op jit(solution)/shard_map/ppermute | solution.py:683
  626.7 38.4 %collective-permute-start.59 = (bf16[1024,1408]{1,0:T(8,128)(2,1)}, bf16[1024,1408]{1,0:T(8,128)(2,1)}, u32[]{:S(2)}, u32[]{:S(2)}) collective-permute-start(bf16[1024,1408]{1,0:T(8,128)(2,1)} %bitcast.71), channel_id=1, source_target_pairs={{0,4},{4,0},{8,12},{12,8},{16,20},{20,16},{24,28},{28,24},{1,5},{5... | collective-permute-start | bytes 8650760 | tf_op jit(solution)/shard_map/ppermute | solution.py:683
  656.1 31.3 %collective-permute-start.62 = (bf16[256,2048]{1,0:T(8,128)(2,1)}, bf16[256,2048]{1,0:T(8,128)(2,1)}, u32[]{:S(2)}, u32[]{:S(2)}) collective-permute-start(bf16[256,2048]{1,0:T(8,128)(2,1)} %get-tuple-element.292.refs_0_), channel_id=1, source_target_pairs={{0,8},{4,12},{8,0},{12,4},{16,24},{20,28},{24,16},{28,20},{1,9},{5... | collective-permute-start | bytes 3145736 | tf_op jit(solution)/shard_map/ppermute | solution.py:683
  660.3 27.1 %collective-permute-start.61 = (bf16[1024,512]{1,0:T(8,128)(2,1)}, bf16[1024,512]{1,0:T(8,128)(2,1)}, u32[]{:S(2)}, u32[]{:S(2)}) collective-permute-start(bf16[1024,512]{1,0:T(8,128)(2,1)} %get-tuple-element.291), channel_id=1, source_target_pairs={{1,2},{2,1},{5,6},{6,5},{9,10},{10,9},{13,14},{14,13},{17,18},{18,... | collective-permute-start | bytes 3145736 | tf_op jit(solution)/shard_map/ppermute | solution.py:569
  (129 other events, 1889.0 us)

commit v7 on v6

--- a/solution.py
+++ b/solution.py
@@ -174,7 +174,7 @@
             pl.BlockSpec((1, t, width), lambda k: (k, c, 0)),
         ],
         previous,
-        mib=56,
+        mib=34,
         name="project",
     )
 
@@ -701,9 +701,9 @@
 def split(upper, lower, bits, joined):
     groups = len(upper)
     rows = upper[0][0].shape[0] // (4 if joined else 2)
-    block = min(128, rows)
+    columns = sum(keep.shape[1] for keep, _ in upper)
+    block = min(64 if columns > D else 128, rows)
     nb = rows // block
-    columns = sum(keep.shape[1] for keep, _ in upper)
     ins, in_specs = [], []
     for part, pairs in enumerate((upper, lower)):
         first = 2 * nb * part if joined else 0
@@ -749,7 +749,7 @@
 
 def merge(upper, lower, bits, widths=()):
     rows, columns = upper[0].shape
-    block = min(128, rows)
+    block = min(64 if columns > D else 128, rows)
     nb = rows // block
 
     def spec(part, which):
@@ -920,7 +920,7 @@
     tables = rope_tables()
     order.done(*got, up_w, tables)
     whole_x.last(order)
-    x = whole_x.whole(56)
+    x = whole_x.whole()
     gain_one, gain_two, shift_two = (x[t + i : t + i + 1].astype(F32) for i in (0, 2, 3))
     project_w = project_weight.transpose(1, 0, 2)
     bias = project_bias.astype(F32)[:, None, :]

time: 715 us -> 716 us (level)
  local copies, waits for them, and re-layouts: 63.1 us -> 71 us
    unnamed x171 -> x181, local copies, waits for them, and re-layouts: 37.6 us -> 46 us
where the time goes in v7:
time: 716 us; the launch traced here: 709 us
  Pallas kernels  261 us (36%)
  waiting for transfers between devices  210 us (29%)
  starting transfers between devices  114 us (16%)
  local copies, waits for them, and re-layouts  71 us (10%)
  other arithmetic  46.6 us (7%)
    pallas_call x25, Pallas kernels, prefetched(): pl.pallas_call(body, grid_spec=pltpu.PrefetchScalarGridSpec(num_scalar_pr...  186 us
    ppermute x20, waiting for transfers between devices, send(): self.pieces.append(lax.ppermute(order(self.pieces[piece]), 'tensor', pairs))  144 us
    pallas_call x4, Pallas kernels, kernel_call(): pl.pallas_call(run, grid=grid, in_specs=list(in_specs) + [ANY] * len(prev...  75.4 us
    ppermute x20, starting transfers between devices, send(): self.got[name] = lax.ppermute(order(value), 'tensor', pairs)  61.2 us
    unnamed x181, local copies, waits for them, and re-layouts  46 us
    ppermute x20, waiting for transfers between devices, send(): self.got[name] = lax.ppermute(order(value), 'tensor', pairs)  41.5 us
    ppermute x20, starting transfers between devices, send(): self.pieces.append(lax.ppermute(order(self.pieces[piece]), 'tensor', pairs))  29.3 us
    ppermute x25, waiting for transfers between devices, swap(): return lax.ppermute(value, axis, [(i, i ^ 1 << bit) for i in range(n)])  24.3 us
  transfers between devices with their start and end apart: 68, of which 23 were waited for; matrix products, arithmetic and copies ran while one was open for 10% of the time, Pallas kernels for 26%

profile of v7, /device:TPU:0, one launch (start us, length us, event | category | flops | bytes accessed | tf_op | source)
XLA Modules:
  0.0 708.6 jit_solution(17604367930845715990)
XLA Ops:
  22.4 12.1 %collective-permute-done.refs_1_ = bf16[1040,512]{1,0:T(8,128)(2,1)S(1)} collective-permute-done((bf16[1040,512]{1,0:T(8,128)(2,1)S(1)}, bf16[1040,512]{1,0:T(8,128)(2,1)S(1)}, u32[]{:S(2)}, u32[]{:S(2)}) %collective-permute-start) | collective-permute-done | bytes 1064992 | tf_op jit(solution)/shard_map/ppermute | solution.py:490
  47.0 13.7 %collective-permute-done.2.refs_3_ = bf16[1040,512]{1,0:T(8,128)(2,1)S(1)} collective-permute-done((bf16[1040,512]{1,0:T(8,128)(2,1)S(1)}, bf16[1040,512]{1,0:T(8,128)(2,1)S(1)}, u32[]{:S(2)}, u32[]{:S(2)}) %collective-permute-start.2) | collective-permute-done | bytes 1064992 | tf_op jit(solution)/shard_map/ppermute | solution.py:490
  64.0 23.3 %collective-permute-done.4.refs_5_ = bf16[1040,512]{1,0:T(8,128)(2,1)} collective-permute-done((bf16[1040,512]{1,0:T(8,128)(2,1)S(1)}, bf16[1040,512]{1,0:T(8,128)(2,1)}, u32[]{:S(2)}, u32[]{:S(2)}) %collective-permute-start.4) | collective-permute-done | bytes 1064992 | tf_op jit(solution)/shard_map/ppermute | solution.py:490
  105.1 14.2 %project.1 = (bf16[1024,2048]{1,0:T(8,128)(2,1)S(1)}, f32[1024,128]{1,0:T(8,128)S(1)}, bf16[3,1024,512]{2,1,0:T(8,128)(2,1)S(1)}) custom-call(bf16[1040,2048]{1,0:T(8,128)(2,1)S(1)} %copy-done.2, bf16[1040,2048]{1,0:T(8,128)(2,1)S(1)} %copy-done.2, bf16[3,2048,512]{2,1,0:T(8,128)(2,1)S(1)} %bitcast.50, f32[3,1,512]{2,1,0:T(1,128)S(1)} %copy.27.refs_3_, ...), custom_call_target="tpu_custom_call" | custom-call | tf_op jit(solution)/shard_map/project/pallas_call | solution.py:53
  121.0 16.9 %attend.1 = (bf16[1024,512]{1,0:T(8,128)(2,1)S(1)}, bf16[1024,1536]{1,0:T(8,128)(2,1)S(1)}, bf16[1024,512]{1,0:T(8,128)(2,1)S(1)}, f32[1024,512]{1,0:T(8,128)S(1)}) custom-call(s32[4]{0:T(128)S(1)} %pad_add_fusion.owners_ref, bf16[3,1024,512]{2,1,0:T(8,128)(2,1)S(1)} %get-tuple-element.164.q_ref.k_ref.v_ref.refs_0_.refs_1_.refs_2_, ...), custom_call_target="tpu_custom_call" | custom-call | tf_op jit(solution)/shard_map/attend/pallas_call | solution.py:76
  150.8 10.6 %collective-permute-done.8.refs_3_ = bf16[1024,512]{1,0:T(8,128)(2,1)S(1)} collective-permute-done((bf16[1024,512]{1,0:T(8,128)(2,1)}, bf16[1024,512]{1,0:T(8,128)(2,1)S(1)}, u32[]{:S(2)}, u32[]{:S(2)}) %collective-permute-start.8) | collective-permute-done | bytes 1048608 | tf_op jit(solution)/shard_map/ppermute | solution.py:490
  168.6 8.2 %collective-permute-start.12 = (bf16[1024,512]{1,0:T(8,128)(2,1)}, bf16[1024,512]{1,0:T(8,128)(2,1)}, u32[]{:S(2)}, u32[]{:S(2)}) collective-permute-start(bf16[1024,512]{1,0:T(8,128)(2,1)} %constant_dynamic-slice_fusion.3), channel_id=1, source_target_pairs={{0,1},{3,2},{4,5},{7,6},{8,9},{11,10},{12,13},{15,14},{16,17},{19,... | collective-permute-start | bytes 3145736 | tf_op jit(solution)/shard_map/ppermute | solution.py:569
  176.8 14.3 %collective-permute-done.11.refs_5_ = bf16[1024,512]{1,0:T(8,128)(2,1)} collective-permute-done((bf16[1024,512]{1,0:T(8,128)(2,1)}, bf16[1024,512]{1,0:T(8,128)(2,1)}, u32[]{:S(2)}, u32[]{:S(2)}) %collective-permute-start.11) | collective-permute-done | bytes 1048608 | tf_op jit(solution)/shard_map/ppermute | solution.py:490
  203.9 16.6 %collective-permute-done.13 = bf16[1024,512]{1,0:T(8,128)(2,1)} collective-permute-done((bf16[1024,512]{1,0:T(8,128)(2,1)}, bf16[1024,512]{1,0:T(8,128)(2,1)}, u32[]{:S(2)}, u32[]{:S(2)}) %collective-permute-start.13) | collective-permute-done | bytes 1048608 | tf_op jit(solution)/shard_map/ppermute | solution.py:569
  225.8 16.4 %collective-permute-done.15.refs_1_ = bf16[1024,512]{1,0:T(8,128)(2,1)S(1)} collective-permute-done((bf16[1024,512]{1,0:T(8,128)(2,1)S(1)}, bf16[1024,512]{1,0:T(8,128)(2,1)S(1)}, u32[]{:S(2)}, u32[]{:S(2)}) %collective-permute-start.15) | collective-permute-done | bytes 1048608 | tf_op jit(solution)/shard_map/ppermute | solution.py:490
  252.4 12.7 %collective-permute-done.17.refs_3_ = bf16[1024,512]{1,0:T(8,128)(2,1)S(1)} collective-permute-done((bf16[1024,512]{1,0:T(8,128)(2,1)S(1)}, bf16[1024,512]{1,0:T(8,128)(2,1)S(1)}, u32[]{:S(2)}, u32[]{:S(2)}) %collective-permute-start.17) | collective-permute-done | bytes 1048608 | tf_op jit(solution)/shard_map/ppermute | solution.py:490
  265.1 20.8 %collective-permute-done.19.refs_5_ = bf16[1024,512]{1,0:T(8,128)(2,1)S(1)} collective-permute-done((bf16[1024,512]{1,0:T(8,128)(2,1)S(1)}, bf16[1024,512]{1,0:T(8,128)(2,1)S(1)}, u32[]{:S(2)}, u32[]{:S(2)}) %collective-permute-start.19) | collective-permute-done | bytes 1048608 | tf_op jit(solution)/shard_map/ppermute | solution.py:490
  288.7 32.2 %mlp.1 = (bf16[1024,2048]{1,0:T(8,128)(2,1)}, f32[1024,128]{1,0:T(8,128)S(1)}, bf16[1024,1408]{1,0:T(8,128)(2,1)S(1)}, bf16[1024,1408]{1,0:T(8,128)(2,1)S(1)}, bf16[1024,1408]{1,0:T(8,128)(2,1)}) custom-call(bf16[1024,2048]{1,0:T(8,128)(2,1)} %copy-done.5, bf16[1024,2048]{1,0:T(8,128)(2,1)} %copy-done.3, f32[1,2048]{1,0:T(1,128)S(1)} %get-tuple-element.313.refs_2_, ...), custom_call_target="tpu_custom_call" | custom-call | tf_op jit(solution)/shard_map/mlp/pallas_call | solution.py:53
  334.3 15.7 %mlp_back.3 = bf16[1024,1536]{1,0:T(8,128)(2,1)} custom-call(s32[3]{0:T(128)} %pad_add_fusion.1.owners_ref, bf16[1024,1408]{1,0:T(8,128)(2,1)} %copy-done.9, bf16[1024,1408]{1,0:T(8,128)(2,1)} %get-tuple-element.187.dup_ref.refs_3_, bf16[2048,1408]{1,0:T(8,128)(2,1)} %bitcast.65, bf16[2048,1408]{1,0:T(8,128)(2,1)} %slice_bitcast_fusion.refs_5_.up_w_ref), custom_call_target="tpu_custom_call" | custom-call | tf_op jit(solution)/shard_map/mlp_back/pallas_call | solution.py:76
  362.5 15.6 %mlp_given.1 = (bf16[1024,1408]{1,0:T(8,128)(2,1)}, bf16[1024,1408]{1,0:T(8,128)(2,1)}, bf16[1024,1408]{1,0:T(8,128)(2,1)}) custom-call(s32[1]{0:T(128)} %bitcast.12.which_ref, bf16[1024,2048]{1,0:T(8,128)(2,1)} %get-tuple-element.193.refs_0_, bf16[1024,2048]{1,0:T(8,128)(2,1)} %copy-done.3, bf16[1024,1408]{1,0:T(8,128)(2,1)} %copy-done.9, ...), custom_call_target="tpu_custom_call" | custom-call | tf_op jit(solution)/shard_map/mlp_given/pallas_call | solution.py:76
  386.8 15.4 %mlp_kept.1 = (bf16[1024,1408]{1,0:T(8,128)(2,1)}, bf16[1024,1408]{1,0:T(8,128)(2,1)}, bf16[1024,1408]{1,0:T(8,128)(2,1)}) custom-call(s32[1]{0:T(128)} %bitcast.13.which_ref.core_ref, bf16[1024,2048]{1,0:T(8,128)(2,1)} %get-tuple-element.193.refs_0_, bf16[1024,2048]{1,0:T(8,128)(2,1)} %copy-done.3, bf16[1024,1408]{1,0:T(8,128)(2,1)} %copy-done.9, ...), custom_call_target="tpu_custom_call" | custom-call | flops 30000001024 | tf_op jit(solution)/shard_map/mlp_kept/pallas_call | solution.py:76
  413.3 12.5 %split.4 = (bf16[256,4224]{1,0:T(8,128)(2,1)}, bf16[256,4224]{1,0:T(8,128)(2,1)}, bf16[256,4224]{1,0:T(8,128)(2,1)}, bf16[256,4224]{1,0:T(8,128)(2,1)}) custom-call(s32[2]{0:T(128)} %pad_add_fusion.2.bits_ref, bf16[1024,1408]{1,0:T(8,128)(2,1)} %get-tuple-element.209.refs_0_.refs_6_, bf16[1024,1408]{1,0:T(8,128)(2,1)} %collective-permute-done.27.refs_1_.refs_7_, ...), custom_call_target="tpu_custom_call" | custom-call | tf_op jit(solution)/shard_map/split/pallas_call | solution.py:76
  437.4 8.8 %mlp_out.1 = (bf16[1024,512]{1,0:T(8,128)(2,1)S(1)}, bf16[1024,1536]{1,0:T(8,128)(2,1)S(1)}) custom-call(s32[4]{0:T(128)S(1)} %pad_add_fusion.owners_ref, bf16[1024,1408]{1,0:T(8,128)(2,1)S(1)} %copy-done.38, bf16[1408,2048]{1,0:T(8,128)(2,1)S(1)} %bitcast.60), custom_call_target="tpu_custom_call" | custom-call | flops 10000000000 | tf_op jit(solution)/shard_map/mlp_out/pallas_call | solution.py:76
  446.3 10.9 %collective-permute-done.30.refs_3_ = bf16[1024,512]{1,0:T(8,128)(2,1)S(1)} collective-permute-done((bf16[1024,512]{1,0:T(8,128)(2,1)}, bf16[1024,512]{1,0:T(8,128)(2,1)S(1)}, u32[]{:S(2)}, u32[]{:S(2)}) %collective-permute-start.30) | collective-permute-done | bytes 1048608 | tf_op jit(solution)/shard_map/ppermute | solution.py:490
  504.9 21.2 %attend_back.1 = (bf16[1024,512]{1,0:T(8,128)(2,1)S(1)}, bf16[1024,512]{1,0:T(8,128)(2,1)S(1)}, bf16[1024,512]{1,0:T(8,128)(2,1)S(1)}, f32[8,1024]{1,0:T(8,128)S(1)}) custom-call(bf16[3,1024,512]{2,1,0:T(8,128)(2,1)S(1)} %copy-done.8, bf16[3,1024,512]{2,1,0:T(8,128)(2,1)S(1)} %copy-done.8, bf16[3,1024,512]{2,1,0:T(8,128)(2,1)S(1)} %copy-done.8, ...), custom_call_target="tpu_custom_call" | custom-call | flops 20000000000 | tf_op jit(solution)/shard_map/attend_back/pallas_call | solution.py:53
  575.7 13.5 %collective-permute-done.45 = bf16[1040,512]{1,0:T(8,128)(2,1)S(1)} collective-permute-done((bf16[1040,512]{1,0:T(8,128)(2,1)S(1)}, bf16[1040,512]{1,0:T(8,128)(2,1)S(1)}, u32[]{:S(2)}, u32[]{:S(2)}) %collective-permute-start.45) | collective-permute-done | bytes 1064992 | tf_op jit(solution)/shard_map/ppermute | solution.py:569
  598.1 10.3 %merge.5 = (bf16[2,512,1408]{2,1,0:T(8,128)(2,1)}, bf16[2,512,1408]{2,1,0:T(8,128)(2,1)}, bf16[2,512,1408]{2,1,0:T(8,128)(2,1)}) custom-call(s32[2]{0:T(128)} %pad_add_fusion.2.bits_ref, bf16[256,4224]{1,0:T(8,128)(2,1)} %get-tuple-element.258.refs_0_, bf16[256,4224]{1,0:T(8,128)(2,1)} %collective-permute-done.46.refs_1_, ...), custom_call_target="tpu_custom_call" | custom-call | flops 15000000512 | tf_op jit(solution)/shard_map/merge/pallas_call | solution.py:76
  644.2 9.5 %down_out.1 = f32[1408,2048]{1,0:T(8,128)} custom-call(s32[1]{0:T(128)} %bitcast.13.which_ref.core_ref, bf16[1024,1408]{1,0:T(8,128)(2,1)} %bitcast.68, bf16[1024,1408]{1,0:T(8,128)(2,1)} %collective-permute-done.54.refs_1_), custom_call_target="tpu_custom_call" | custom-call | tf_op jit(solution)/shard_map/down_out/pallas_call | solution.py:76
  665.5 14.7 %gate_up_out.1 = f32[2048,2,1408]{2,1,0:T(2,128)} custom-call(s32[1]{0:T(128)} %bitcast.13.which_ref.core_ref, bf16[1024,1408]{1,0:T(8,128)(2,1)} %bitcast.70, bf16[1024,1408]{1,0:T(8,128)(2,1)} %bitcast.72, bf16[1024,1408]{1,0:T(8,128)(2,1)} %collective-permute-done.58.refs_2_, bf16[1024,1408]{1,0:T(8,128)(2,1)} %collective-permute-done.59.refs_3_), custom_call_target="tpu_custom_call" | custom-call | tf_op jit(solution)/shard_map/gate_up_out/pallas_call | solution.py:76
  (393 shorter events, 346.4 us)
Async XLA Ops:
  5.4 29.1 %collective-permute-start = (bf16[1040,512]{1,0:T(8,128)(2,1)S(1)}, bf16[1040,512]{1,0:T(8,128)(2,1)S(1)}, u32[]{:S(2)}, u32[]{:S(2)}) collective-permute-start(bf16[1040,512]{1,0:T(8,128)(2,1)S(1)} %pad_maximum_fusion.1.refs_0_), channel_id=1, source_target_pairs={{0,1},{1,0},{2,3},{3,2},{4,5},{5,4},{6,7},{7,6},{8,9},{9,8},{10,11... | collective-permute-start | bytes 3194888 | tf_op jit(solution)/shard_map/ppermute | solution.py:490
  34.5 26.3 %collective-permute-start.2 = (bf16[1040,512]{1,0:T(8,128)(2,1)S(1)}, bf16[1040,512]{1,0:T(8,128)(2,1)S(1)}, u32[]{:S(2)}, u32[]{:S(2)}) collective-permute-start(bf16[1040,512]{1,0:T(8,128)(2,1)S(1)} %collective-permute-done.1.refs_2_), channel_id=1, source_target_pairs={{1,0},{2,3},{5,4},{6,7},{9,8},{10,11},{13,12},{14,15},{17,16},{18,... | collective-permute-start | bytes 3194888 | tf_op jit(solution)/shard_map/ppermute | solution.py:490
  35.8 26.0 %collective-permute-start.3 = (bf16[1040,512]{1,0:T(8,128)(2,1)S(1)}, bf16[1040,512]{1,0:T(8,128)(2,1)S(1)}, u32[]{:S(2)}, u32[]{:S(2)}) collective-permute-start(bf16[1040,512]{1,0:T(8,128)(2,1)S(1)} %collective-permute-done.refs_1_), channel_id=1, source_target_pairs={{1,2},{2,1},{5,6},{6,5},{9,10},{10,9},{13,14},{14,13},{17,18},{18,... | collective-permute-start | bytes 3194888 | tf_op jit(solution)/shard_map/ppermute | solution.py:490
  61.7 25.6 %collective-permute-start.4 = (bf16[1040,512]{1,0:T(8,128)(2,1)S(1)}, bf16[1040,512]{1,0:T(8,128)(2,1)}, u32[]{:S(2)}, u32[]{:S(2)}) collective-permute-start(bf16[1040,512]{1,0:T(8,128)(2,1)S(1)} %collective-permute-done.3.refs_4_), channel_id=1, source_target_pairs={{1,0},{2,3},{5,4},{6,7},{9,8},{10,11},{13,12},{14,15},{17,16},{18,... | collective-permute-start | bytes 3194888 | tf_op jit(solution)/shard_map/ppermute | solution.py:490
  244.8 41.1 %collective-permute-start.19 = (bf16[1024,512]{1,0:T(8,128)(2,1)S(1)}, bf16[1024,512]{1,0:T(8,128)(2,1)S(1)}, u32[]{:S(2)}, u32[]{:S(2)}) collective-permute-start(bf16[1024,512]{1,0:T(8,128)(2,1)S(1)} %collective-permute-done.18.refs_4_), channel_id=1, source_target_pairs={{1,0},{2,3},{5,4},{6,7},{9,8},{10,11},{13,12},{14,15},{17,16},{18,... | collective-permute-start | bytes 3145736 | tf_op jit(solution)/shard_map/ppermute | solution.py:490
  378.1 35.2 %collective-permute-start.27 = (bf16[1024,1408]{1,0:T(8,128)(2,1)}, bf16[1024,1408]{1,0:T(8,128)(2,1)}, u32[]{:S(2)}, u32[]{:S(2)}) collective-permute-start(bf16[1024,1408]{1,0:T(8,128)(2,1)} %get-tuple-element.195), channel_id=1, source_target_pairs={{0,4},{4,0},{8,12},{12,8},{16,20},{20,16},{24,28},{28,24},{1,5},{5... | collective-permute-start | bytes 8650760 | tf_op jit(solution)/shard_map/ppermute | solution.py:683
  378.1 35.2 %collective-permute-start.28 = (bf16[1024,1408]{1,0:T(8,128)(2,1)}, bf16[1024,1408]{1,0:T(8,128)(2,1)}, u32[]{:S(2)}, u32[]{:S(2)}) collective-permute-start(bf16[1024,1408]{1,0:T(8,128)(2,1)} %get-tuple-element.196), channel_id=1, source_target_pairs={{0,4},{4,0},{8,12},{12,8},{16,20},{20,16},{24,28},{28,24},{1,5},{5... | collective-permute-start | bytes 8650760 | tf_op jit(solution)/shard_map/ppermute | solution.py:683
  378.6 34.7 %collective-permute-start.29 = (bf16[1024,1408]{1,0:T(8,128)(2,1)}, bf16[1024,1408]{1,0:T(8,128)(2,1)}, u32[]{:S(2)}, u32[]{:S(2)}) collective-permute-start(bf16[1024,1408]{1,0:T(8,128)(2,1)} %get-tuple-element.197), channel_id=1, source_target_pairs={{0,4},{4,0},{8,12},{12,8},{16,20},{20,16},{24,28},{28,24},{1,5},{5... | collective-permute-start | bytes 8650760 | tf_op jit(solution)/shard_map/ppermute | solution.py:683
  382.6 25.8 %collective-permute-start.23 = (bf16[1024,512]{1,0:T(8,128)(2,1)}, bf16[1024,512]{1,0:T(8,128)(2,1)S(1)}, u32[]{:S(2)}, u32[]{:S(2)}) collective-permute-start(bf16[1024,512]{1,0:T(8,128)(2,1)} %get-tuple-element.199), channel_id=1, source_target_pairs={{0,1},{1,0},{2,3},{3,2},{4,5},{5,4},{6,7},{7,6},{8,9},{9,8},{10,11... | collective-permute-start | bytes 3145736 | tf_op jit(solution)/shard_map/ppermute | solution.py:569
  425.8 44.9 %collective-permute-start.34 = (bf16[256,4224]{1,0:T(8,128)(2,1)}, bf16[256,4224]{1,0:T(8,128)(2,1)S(1)}, u32[]{:S(2)}, u32[]{:S(2)}) collective-permute-start(bf16[256,4224]{1,0:T(8,128)(2,1)} %get-tuple-element.221), channel_id=1, source_target_pairs={{0,8},{4,12},{8,0},{12,4},{16,24},{20,28},{24,16},{28,20},{1,9},{5... | collective-permute-start | bytes 6488072 | tf_op jit(solution)/shard_map/ppermute | solution.py:683
  427.3 45.6 %collective-permute-start.35 = (bf16[256,4224]{1,0:T(8,128)(2,1)}, bf16[256,4224]{1,0:T(8,128)(2,1)S(1)}, u32[]{:S(2)}, u32[]{:S(2)}) collective-permute-start(bf16[256,4224]{1,0:T(8,128)(2,1)} %get-tuple-element.224), channel_id=1, source_target_pairs={{0,16},{4,20},{8,24},{12,28},{16,0},{20,4},{24,8},{28,12},{1,17},{... | collective-permute-start | bytes 6488072 | tf_op jit(solution)/shard_map/ppermute | solution.py:683
  493.9 40.6 %collective-permute-start.36 = (bf16[1024,512]{1,0:T(8,128)(2,1)}, bf16[1024,512]{1,0:T(8,128)(2,1)}, u32[]{:S(2)}, u32[]{:S(2)}) collective-permute-start(bf16[1024,512]{1,0:T(8,128)(2,1)} %add_convert_fusion.8), channel_id=1, source_target_pairs={{1,2},{2,1},{5,6},{6,5},{9,10},{10,9},{13,14},{14,13},{17,18},{18,... | collective-permute-start | bytes 3145736 | tf_op jit(solution)/shard_map/ppermute | solution.py:569
  496.0 38.5 %collective-permute-start.41 = (bf16[1024,512]{1,0:T(8,128)(2,1)}, bf16[1024,512]{1,0:T(8,128)(2,1)}, u32[]{:S(2)}, u32[]{:S(2)}) collective-permute-start(bf16[1024,512]{1,0:T(8,128)(2,1)} %constant_dynamic-slice_fusion.1), channel_id=1, source_target_pairs={{0,1},{3,2},{4,5},{7,6},{8,9},{11,10},{12,13},{15,14},{16,17},{19,... | collective-permute-start | bytes 3145736 | tf_op jit(solution)/shard_map/ppermute | solution.py:569
  539.8 58.3 %collective-permute-start.46 = (bf16[256,4224]{1,0:T(8,128)(2,1)}, bf16[256,4224]{1,0:T(8,128)(2,1)}, u32[]{:S(2)}, u32[]{:S(2)}) collective-permute-start(bf16[256,4224]{1,0:T(8,128)(2,1)} %get-tuple-element.258.refs_0_), channel_id=1, source_target_pairs={{0,8},{4,12},{8,0},{12,4},{16,24},{20,28},{24,16},{28,20},{1,9},{5... | collective-permute-start | bytes 6488072 | tf_op jit(solution)/shard_map/ppermute | solution.py:683
  551.1 45.3 %collective-permute-start.47 = (bf16[256,4224]{1,0:T(8,128)(2,1)}, bf16[256,4224]{1,0:T(8,128)(2,1)}, u32[]{:S(2)}, u32[]{:S(2)}) collective-permute-start(bf16[256,4224]{1,0:T(8,128)(2,1)} %get-tuple-element.259.refs_2_), channel_id=1, source_target_pairs={{0,16},{4,20},{8,24},{12,28},{16,0},{20,4},{24,8},{28,12},{1,17},{... | collective-permute-start | bytes 6488072 | tf_op jit(solution)/shard_map/ppermute | solution.py:683
  590.4 25.7 %collective-permute-start.49 = (bf16[256,2048]{1,0:T(8,128)(2,1)}, bf16[256,2048]{1,0:T(8,128)(2,1)S(1)}, u32[]{:S(2)}, u32[]{:S(2)}) collective-permute-start(bf16[256,2048]{1,0:T(8,128)(2,1)} %get-tuple-element.265), channel_id=1, source_target_pairs={{0,16},{4,20},{8,24},{12,28},{16,0},{20,4},{24,8},{28,12},{1,17},{... | collective-permute-start | bytes 3145736 | tf_op jit(solution)/shard_map/ppermute | solution.py:683
  593.9 32.1 %collective-permute-start.50 = (bf16[1040,512]{1,0:T(8,128)(2,1)}, bf16[1040,512]{1,0:T(8,128)(2,1)}, u32[]{:S(2)}, u32[]{:S(2)}) collective-permute-start(bf16[1040,512]{1,0:T(8,128)(2,1)} %get-tuple-element.268), channel_id=1, source_target_pairs={{0,1},{1,0},{2,3},{3,2},{4,5},{5,4},{6,7},{7,6},{8,9},{9,8},{10,11... | collective-permute-start | bytes 3194888 | tf_op jit(solution)/shard_map/ppermute | solution.py:569
  596.4 29.7 %collective-permute-start.51 = (bf16[1040,512]{1,0:T(8,128)(2,1)}, bf16[1040,512]{1,0:T(8,128)(2,1)}, u32[]{:S(2)}, u32[]{:S(2)}) collective-permute-start(bf16[1040,512]{1,0:T(8,128)(2,1)} %get-tuple-element.270), channel_id=1, source_target_pairs={{1,2},{2,1},{5,6},{6,5},{9,10},{10,9},{13,14},{14,13},{17,18},{18,... | collective-permute-start | bytes 3194888 | tf_op jit(solution)/shard_map/ppermute | solution.py:569
  608.4 35.8 %collective-permute-start.54 = (bf16[1024,1408]{1,0:T(8,128)(2,1)}, bf16[1024,1408]{1,0:T(8,128)(2,1)}, u32[]{:S(2)}, u32[]{:S(2)}) collective-permute-start(bf16[1024,1408]{1,0:T(8,128)(2,1)} %bitcast.67), channel_id=1, source_target_pairs={{0,4},{4,0},{8,12},{12,8},{16,20},{20,16},{24,28},{28,24},{1,5},{5... | collective-permute-start | bytes 8650760 | tf_op jit(solution)/shard_map/ppermute | solution.py:683
  626.0 38.8 %collective-permute-start.58 = (bf16[1024,1408]{1,0:T(8,128)(2,1)}, bf16[1024,1408]{1,0:T(8,128)(2,1)}, u32[]{:S(2)}, u32[]{:S(2)}) collective-permute-start(bf16[1024,1408]{1,0:T(8,128)(2,1)} %bitcast.69), channel_id=1, source_target_pairs={{0,4},{4,0},{8,12},{12,8},{16,20},{20,16},{24,28},{28,24},{1,5},{5... | collective-permute-start | bytes 8650760 | tf_op jit(solution)/shard_map/ppermute | solution.py:683
  626.1 39.4 %collective-permute-start.59 = (bf16[1024,1408]{1,0:T(8,128)(2,1)}, bf16[1024,1408]{1,0:T(8,128)(2,1)}, u32[]{:S(2)}, u32[]{:S(2)}) collective-permute-start(bf16[1024,1408]{1,0:T(8,128)(2,1)} %bitcast.71), channel_id=1, source_target_pairs={{0,4},{4,0},{8,12},{12,8},{16,20},{20,16},{24,28},{28,24},{1,5},{5... | collective-permute-start | bytes 8650760 | tf_op jit(solution)/shard_map/ppermute | solution.py:683
  655.7 32.0 %collective-permute-start.62 = (bf16[256,2048]{1,0:T(8,128)(2,1)}, bf16[256,2048]{1,0:T(8,128)(2,1)}, u32[]{:S(2)}, u32[]{:S(2)}) collective-permute-start(bf16[256,2048]{1,0:T(8,128)(2,1)} %get-tuple-element.292.refs_0_), channel_id=1, source_target_pairs={{0,8},{4,12},{8,0},{12,4},{16,24},{20,28},{24,16},{28,20},{1,9},{5... | collective-permute-start | bytes 3145736 | tf_op jit(solution)/shard_map/ppermute | solution.py:683
  659.7 28.0 %collective-permute-start.61 = (bf16[1024,512]{1,0:T(8,128)(2,1)}, bf16[1024,512]{1,0:T(8,128)(2,1)}, u32[]{:S(2)}, u32[]{:S(2)}) collective-permute-start(bf16[1024,512]{1,0:T(8,128)(2,1)} %get-tuple-element.291), channel_id=1, source_target_pairs={{1,2},{2,1},{5,6},{6,5},{9,10},{10,9},{13,14},{14,13},{17,18},{18,... | collective-permute-start | bytes 3145736 | tf_op jit(solution)/shard_map/ppermute | solution.py:569
  661.6 26.1 %collective-permute-start.57 = (bf16[1024,512]{1,0:T(8,128)(2,1)}, bf16[1024,512]{1,0:T(8,128)(2,1)}, u32[]{:S(2)}, u32[]{:S(2)}) collective-permute-start(bf16[1024,512]{1,0:T(8,128)(2,1)} %get-tuple-element.283), channel_id=1, source_target_pairs={{0,1},{1,0},{2,3},{3,2},{4,5},{5,4},{6,7},{7,6},{8,9},{9,8},{10,11... | collective-permute-start | bytes 3145736 | tf_op jit(solution)/shard_map/ppermute | solution.py:569
  (134 other events, 1886.0 us)
